TPU v7x, 32 devices: a whole 2x2x4 slice. The times are simulated.
32 devices in a mesh: dp: 2 (over y), ctx: 4 (over x, core), tensor: 4 (over z).
Axes of the slice: x: 2, y: 2, z: 4, core: 2. Of those that a mesh axis runs over, the one named last changes fastest.
Arguments:
- hidden_in: bfloat16 [8, 1024, 2048], P('dp', 'ctx'), may hold values from -6 to 6
- output_cotangent: bfloat16 [8, 1024, 2048], P('dp', 'ctx'), may hold values from -6 to 6
- adapter_index: int32 [8, 1], P('dp'), may hold values from 0 to 7
- mixing_weight: bfloat16 [2048, 3, 2048], P(('dp', 'ctx'), None, 'tensor'), may hold values from -0.125 to 0.125
- output_weight: bfloat16 [2048, 2048], P('tensor', ('dp', 'ctx')), may hold values from -2.5 to 2.5
- expand_weight: bfloat16 [2048, 8192], P(('dp', 'ctx'), 'tensor'), may hold values from -0.125 to 0.125
- contract_weight: bfloat16 [8192, 2048], P('tensor', ('dp', 'ctx')), may hold values from -0.0625 to 0.0625
- first_gain: float32 [2048], replicated, may hold values from 0.1 to 1.9
- first_shift: float32 [2048], replicated, may hold values from -3 to 3
- second_gain: float32 [2048], replicated, may hold values from 0.1 to 1.9
- second_shift: float32 [2048], replicated, may hold values from -3 to 3
- mixing_down: bfloat16 [8, 16, 2048], replicated, may hold values from -0.125 to 0.125
- mixing_up: bfloat16 [8, 16, 3, 2048], P(None, None, None, 'tensor'), may hold values from -0.75 to 0.75
- output_down: bfloat16 [8, 16, 2048], P(None, None, 'tensor'), may hold values from -2.5 to 2.5
- output_up: bfloat16 [8, 16, 2048], replicated, may hold values from -0.75 to 0.75
- expand_down: bfloat16 [8, 16, 2048], replicated, may hold values from -0.125 to 0.125
- expand_up: bfloat16 [8, 16, 8192], P(None, None, 'tensor'), may hold values from -0.75 to 0.75
- contract_down: bfloat16 [8, 16, 8192], P(None, None, 'tensor'), may hold values from -0.0625 to 0.0625
- contract_up: bfloat16 [8, 16, 2048], replicated, may hold values from -0.75 to 0.75
Outputs:
- hidden_out: bfloat16 [8, 1024, 2048], P('dp', 'ctx')
- input_grad: bfloat16 [8, 1024, 2048], P('dp', 'ctx')
- mixing_down_grad: float32 [8, 16, 2048], replicated
- mixing_up_grad: float32 [8, 16, 3, 2048], P(None, None, None, 'tensor')
- output_down_grad: float32 [8, 16, 2048], P(None, None, 'tensor')
- output_up_grad: float32 [8, 16, 2048], replicated
- expand_down_grad: float32 [8, 16, 2048], replicated
- expand_up_grad: float32 [8, 16, 8192], P(None, None, 'tensor')
- contract_down_grad: float32 [8, 16, 8192], P(None, None, 'tensor')
- contract_up_grad: float32 [8, 16, 2048], replicated
Inputs may be any that keep to these rules, and one draw needn't show every extreme that they name: `adapter_index`: each of the 8 adapters serves at least one sequence.
All inputs are finite; a program needn't handle non-finite values.
Results may differ from a plain program's by a relative error of at most 0.025.
Values may be sent and summed in bfloat16 or wider, within the bound.
A program may use at most 256 MiB of HBM per device.

v0:
```python
import math

import jax
import jax.numpy as jnp
from jax import lax
from jax.sharding import PartitionSpec as P

HEAD_DIM = 128
NADAPT = 8


def smooth_gate(value):
    return (
        0.5
        * value
        * (1.0 + jnp.tanh(0.7978845608028654 * (value + 0.044715 * value * value * value)))
    )


def norm_rows(hidden, gain, shift):
    centred = hidden - jnp.mean(hidden, axis=-1, keepdims=True)
    spread = lax.rsqrt(jnp.mean(centred * centred, axis=-1, keepdims=True) + 1e-06)
    normed = centred * spread
    return (normed * gain + shift, normed, spread)


def norm_back(grad_rows, normed, spread, gain):
    scaled = grad_rows * gain
    return spread * (
        scaled
        - jnp.mean(scaled, axis=-1, keepdims=True)
        - normed * jnp.mean(scaled * normed, axis=-1, keepdims=True)
    )


def pick_rows(onehot_low, table):
    return jnp.einsum(
        "sn,n...->s...", onehot_low, table, preferred_element_type=jnp.float32
    ).astype(jnp.bfloat16)


def spread_back(onehot, per_seq):
    return jnp.einsum("sn,s...->n...", onehot, per_seq, precision=lax.Precision.HIGHEST)


def split_blocks(values, block_rows):
    return values.reshape((values.shape[0] // block_rows, block_rows) + values.shape[1:])


def sum_heads(parts):
    return (
        lax.psum(parts[0].astype(jnp.bfloat16), "tensor").astype(jnp.float32),
        lax.psum(parts[1].astype(jnp.bfloat16), "tensor").astype(jnp.float32),
    )


def attend_fold(queries, score_scale, state_now, shard_rows):
    key_rows, value_rows = shard_rows
    block_rows = math.gcd(key_rows.shape[0], 512)

    def attend_advance(state, pair):
        running_max, running_sum, weighted = state
        key_block, value_block = pair
        scores = (
            jnp.einsum("tshd,kshd->tshk", queries, key_block, preferred_element_type=jnp.float32)
            * score_scale
        )
        new_max = jnp.maximum(running_max, jnp.max(scores, axis=-1))
        factor = jnp.exp(running_max - new_max)
        raised = jnp.exp(scores - new_max[..., None])
        running_sum = running_sum * factor + jnp.sum(raised, axis=-1)
        weighted = weighted * factor[..., None] + jnp.einsum(
            "tshk,kshd->tshd",
            raised.astype(jnp.bfloat16),
            value_block,
            preferred_element_type=jnp.float32,
        )
        return ((new_max, running_sum, weighted), None)

    state_now, _ = lax.scan(
        attend_advance,
        state_now,
        (split_blocks(key_rows, block_rows), split_blocks(value_rows, block_rows)),
    )
    return state_now


def score_grads(
    query_block, grad_block, log_block, delta_block, key_block, value_block, score_scale
):
    scores = (
        jnp.einsum("tshd,kshd->tshk", query_block, key_block, preferred_element_type=jnp.float32)
        * score_scale
    )
    probs = jnp.exp(scores - log_block[..., None])
    dprobs = jnp.einsum(
        "tshd,kshd->tshk", grad_block, value_block, preferred_element_type=jnp.float32
    )
    dscores = (probs * (dprobs - delta_block[..., None])).astype(jnp.bfloat16)
    return (probs.astype(jnp.bfloat16), dscores)


def key_sweep(queries, grad_out, log_total, delta_rows, key_all, value_all, score_scale):
    block_rows = math.gcd(key_all.shape[0], 512)

    def key_advance(query_grad, pair):
        key_block, value_block = pair
        probs, dscores = score_grads(
            queries, grad_out, log_total, delta_rows, key_block, value_block, score_scale
        )
        query_grad = query_grad + score_scale * jnp.einsum(
            "tshk,kshd->tshd", dscores, key_block, preferred_element_type=jnp.float32
        )
        key_part = score_scale * jnp.einsum(
            "tshk,tshd->kshd", dscores, queries, preferred_element_type=jnp.float32
        )
        value_part = jnp.einsum(
            "tshk,tshd->kshd", probs, grad_out, preferred_element_type=jnp.float32
        )
        return (query_grad, (key_part, value_part))

    start_grad = jnp.zeros(queries.shape, jnp.float32)
    query_grad, (key_parts, value_parts) = lax.scan(
        key_advance,
        start_grad,
        (split_blocks(key_all, block_rows), split_blocks(value_all, block_rows)),
    )
    return (query_grad, key_parts.reshape(key_all.shape), value_parts.reshape(value_all.shape))


def per_device(
    hidden_in,
    output_cotangent,
    adapter_index,
    mixing_weight,
    output_weight,
    expand_weight,
    contract_weight,
    first_gain,
    first_shift,
    second_gain,
    second_shift,
    mixing_down,
    mixing_up,
    output_down,
    output_up,
    expand_down,
    expand_up,
    contract_down,
    contract_up,
):
    seq_count, tok_count, model_width = hidden_in.shape
    local_heads = mixing_weight.shape[2] // HEAD_DIM
    score_scale = HEAD_DIM ** (-0.5)
    head_shape = (tok_count, seq_count, local_heads, HEAD_DIM)
    adapter_ids = jnp.arange(NADAPT, dtype=jnp.int32)
    onehot = (adapter_index == adapter_ids[None, :]).astype(jnp.float32)
    onehot_low = onehot.astype(jnp.bfloat16)
    mixing_down_sel = pick_rows(onehot_low, mixing_down)
    mixing_up_sel = pick_rows(onehot_low, mixing_up)
    output_down_sel = pick_rows(onehot_low, output_down)
    output_up_sel = pick_rows(onehot_low, output_up)
    expand_down_sel = pick_rows(onehot_low, expand_down)
    expand_up_sel = pick_rows(onehot_low, expand_up)
    contract_down_sel = pick_rows(onehot_low, contract_down)
    contract_up_sel = pick_rows(onehot_low, contract_up)
    mixing_full, output_full = (
        lax.all_gather(mixing_weight, ("dp", "ctx"), axis=0, tiled=True),
        lax.all_gather(output_weight, ("dp", "ctx"), axis=1, tiled=True),
    )
    hidden_wide = hidden_in.astype(jnp.float32)
    mixing_rank = jnp.einsum(
        "std,srd->str", hidden_in, mixing_down_sel, preferred_element_type=jnp.float32
    ).astype(jnp.bfloat16)
    projected = jnp.einsum(
        "std,dcf->tscf", hidden_in, mixing_full, preferred_element_type=jnp.float32
    )
    projected = projected + jnp.einsum(
        "str,srcf->tscf", mixing_rank, mixing_up_sel, preferred_element_type=jnp.float32
    )
    projected = projected.astype(jnp.bfloat16)
    queries = projected[:, :, 0].reshape(head_shape)
    key_rows = projected[:, :, 1].reshape(head_shape)
    value_rows = projected[:, :, 2].reshape(head_shape)
    start_state = (
        jnp.full(head_shape[:3], -1e30, jnp.float32),
        jnp.zeros(head_shape[:3], jnp.float32),
        jnp.zeros(head_shape, jnp.float32),
    )
    running_max, running_sum, weighted = attend_fold(
        queries,
        score_scale,
        start_state,
        (
            lax.all_gather(key_rows, "ctx", axis=0, tiled=True),
            lax.all_gather(value_rows, "ctx", axis=0, tiled=True),
        ),
    )
    attended = weighted / running_sum[..., None]
    log_total = running_max + jnp.log(running_sum)
    context = attended.reshape(tok_count, seq_count, -1).astype(jnp.bfloat16)
    attn_part = jnp.einsum("tsc,ce->ste", context, output_full, preferred_element_type=jnp.float32)
    output_rank_part = jnp.einsum(
        "tsc,src->str", context, output_down_sel, preferred_element_type=jnp.float32
    )
    attn_main, output_rank = sum_heads((attn_part, output_rank_part))
    output_rank_low = output_rank.astype(jnp.bfloat16)
    attn_total = attn_main + jnp.einsum(
        "str,sre->ste", output_rank_low, output_up_sel, preferred_element_type=jnp.float32
    )
    first_out, first_normed, first_spread = norm_rows(
        hidden_wide + attn_total, first_gain, first_shift
    )
    first_low, output_rank_low = (first_out.astype(jnp.bfloat16), output_rank_low)
    expand_full, contract_full = (
        lax.all_gather(expand_weight, ("dp", "ctx"), axis=0, tiled=True),
        lax.all_gather(contract_weight, ("dp", "ctx"), axis=1, tiled=True),
    )
    expand_rank = jnp.einsum(
        "std,srd->str", first_low, expand_down_sel, preferred_element_type=jnp.float32
    ).astype(jnp.bfloat16)
    before = jnp.einsum("std,df->stf", first_low, expand_full, preferred_element_type=jnp.float32)
    before = before + jnp.einsum(
        "str,srf->stf", expand_rank, expand_up_sel, preferred_element_type=jnp.float32
    )
    activated, gelu_back = jax.vjp(smooth_gate, before)
    active_low = activated.astype(jnp.bfloat16)
    ffn_part = jnp.einsum(
        "stf,fe->ste", active_low, contract_full, preferred_element_type=jnp.float32
    )
    contract_rank_part = jnp.einsum(
        "stf,srf->str", active_low, contract_down_sel, preferred_element_type=jnp.float32
    )
    ffn_main, contract_rank = sum_heads((ffn_part, contract_rank_part))
    contract_rank_low = contract_rank.astype(jnp.bfloat16)
    ffn_total = ffn_main + jnp.einsum(
        "str,sre->ste", contract_rank_low, contract_up_sel, preferred_element_type=jnp.float32
    )
    second_out, second_normed, second_spread = norm_rows(
        first_out + ffn_total, second_gain, second_shift
    )
    second_grad = norm_back(
        output_cotangent.astype(jnp.float32), second_normed, second_spread, second_gain
    )
    out_low, second_low, contract_rank_low = (
        second_out.astype(jnp.bfloat16),
        second_grad.astype(jnp.bfloat16),
        contract_rank_low,
    )
    expand_back, contract_back = (
        lax.all_gather(expand_weight, ("dp", "ctx"), axis=0, tiled=True),
        lax.all_gather(contract_weight, ("dp", "ctx"), axis=1, tiled=True),
    )
    contract_rank_grad = jnp.einsum(
        "ste,sre->str", second_low, contract_up_sel, preferred_element_type=jnp.float32
    ).astype(jnp.bfloat16)
    active_grad = jnp.einsum(
        "ste,fe->stf", second_low, contract_back, preferred_element_type=jnp.float32
    )
    active_grad = active_grad + jnp.einsum(
        "str,srf->stf", contract_rank_grad, contract_down_sel, preferred_element_type=jnp.float32
    )
    before_low = gelu_back(active_grad)[0].astype(jnp.bfloat16)
    first_part = jnp.einsum(
        "stf,df->std", before_low, expand_back, preferred_element_type=jnp.float32
    )
    expand_rank_part = jnp.einsum(
        "stf,srf->str", before_low, expand_up_sel, preferred_element_type=jnp.float32
    )
    first_back, expand_rank_grad = sum_heads((first_part, expand_rank_part))
    expand_rank_low = expand_rank_grad.astype(jnp.bfloat16)
    first_total = (
        second_grad
        + first_back
        + jnp.einsum(
            "str,srd->std", expand_rank_low, expand_down_sel, preferred_element_type=jnp.float32
        )
    )
    attn_grad = norm_back(first_total, first_normed, first_spread, first_gain)
    attn_low, expand_rank_low = (attn_grad.astype(jnp.bfloat16), expand_rank_low)
    mixing_back, output_back = (
        lax.all_gather(mixing_weight, ("dp", "ctx"), axis=0, tiled=True),
        lax.all_gather(output_weight, ("dp", "ctx"), axis=1, tiled=True),
    )
    output_rank_grad = jnp.einsum(
        "ste,sre->str", attn_low, output_up_sel, preferred_element_type=jnp.float32
    ).astype(jnp.bfloat16)
    context_grad = jnp.einsum(
        "ste,ce->tsc", attn_low, output_back, preferred_element_type=jnp.float32
    )
    context_grad = context_grad + jnp.einsum(
        "str,src->tsc", output_rank_grad, output_down_sel, preferred_element_type=jnp.float32
    )
    grad_out = context_grad.astype(jnp.bfloat16).reshape(head_shape)
    delta_rows = jnp.sum(grad_out.astype(jnp.float32) * attended, axis=-1)
    key_all, value_all = (
        lax.all_gather(key_rows, "ctx", axis=0, tiled=True),
        lax.all_gather(value_rows, "ctx", axis=0, tiled=True),
    )
    query_grad, key_parts, value_parts = key_sweep(
        queries, grad_out, log_total, delta_rows, key_all, value_all, score_scale
    )
    key_grad, value_grad = (
        lax.psum_scatter(
            key_parts.astype(jnp.bfloat16), "ctx", scatter_dimension=0, tiled=True
        ).astype(jnp.float32),
        lax.psum_scatter(
            value_parts.astype(jnp.bfloat16), "ctx", scatter_dimension=0, tiled=True
        ).astype(jnp.float32),
    )
    grad_stack = jnp.stack([query_grad, key_grad, value_grad], axis=2).astype(jnp.bfloat16)
    grad_stack = grad_stack.reshape(tok_count, seq_count, 3, -1)
    input_part = jnp.einsum(
        "tscf,dcf->std", grad_stack, mixing_back, preferred_element_type=jnp.float32
    )
    mixing_rank_part = jnp.einsum(
        "tscf,srcf->str", grad_stack, mixing_up_sel, preferred_element_type=jnp.float32
    )
    input_back, mixing_rank_grad = sum_heads((input_part, mixing_rank_part))
    mixing_rank_low = mixing_rank_grad.astype(jnp.bfloat16)
    input_grad = (
        attn_grad
        + input_back
        + jnp.einsum(
            "str,srd->std", mixing_rank_low, mixing_down_sel, preferred_element_type=jnp.float32
        )
    )
    input_low, mixing_rank_low = (input_grad.astype(jnp.bfloat16), mixing_rank_low)
    mixing_down_part = spread_back(
        onehot,
        jnp.einsum("str,std->srd", mixing_rank_low, hidden_in, preferred_element_type=jnp.float32),
    )
    mixing_up_part = spread_back(
        onehot,
        jnp.einsum("str,tscf->srcf", mixing_rank, grad_stack, preferred_element_type=jnp.float32),
    )
    output_down_part = spread_back(
        onehot,
        jnp.einsum("str,tsc->src", output_rank_grad, context, preferred_element_type=jnp.float32),
    )
    output_up_part = spread_back(
        onehot,
        jnp.einsum("str,ste->sre", output_rank_low, attn_low, preferred_element_type=jnp.float32),
    )
    expand_down_part = spread_back(
        onehot,
        jnp.einsum("str,std->srd", expand_rank_low, first_low, preferred_element_type=jnp.float32),
    )
    expand_up_part = spread_back(
        onehot,
        jnp.einsum("str,stf->srf", expand_rank, before_low, preferred_element_type=jnp.float32),
    )
    contract_down_part = spread_back(
        onehot,
        jnp.einsum(
            "str,stf->srf", contract_rank_grad, active_low, preferred_element_type=jnp.float32
        ),
    )
    contract_up_part = spread_back(
        onehot,
        jnp.einsum(
            "str,ste->sre", contract_rank_low, second_low, preferred_element_type=jnp.float32
        ),
    )
    summed = (
        lax.psum(mixing_down_part.astype(jnp.bfloat16), ("dp", "ctx")).astype(jnp.float32),
        lax.psum(mixing_up_part.astype(jnp.bfloat16), ("dp", "ctx")).astype(jnp.float32),
        lax.psum(output_down_part.astype(jnp.bfloat16), ("dp", "ctx")).astype(jnp.float32),
        lax.psum(output_up_part.astype(jnp.bfloat16), ("dp", "ctx")).astype(jnp.float32),
        lax.psum(expand_down_part.astype(jnp.bfloat16), ("dp", "ctx")).astype(jnp.float32),
        lax.psum(expand_up_part.astype(jnp.bfloat16), ("dp", "ctx")).astype(jnp.float32),
        lax.psum(contract_down_part.astype(jnp.bfloat16), ("dp", "ctx")).astype(jnp.float32),
        lax.psum(contract_up_part.astype(jnp.bfloat16), ("dp", "ctx")).astype(jnp.float32),
    )
    return (
        out_low,
        input_low,
        summed[0],
        summed[1],
        summed[2],
        summed[3],
        summed[4],
        summed[5],
        summed[6],
        summed[7],
    )


def solution(mesh):
    return jax.shard_map(
        per_device,
        mesh=mesh,
        in_specs=(
            P("dp", "ctx", None),
            P("dp", "ctx", None),
            P("dp", None),
            P(("dp", "ctx"), None, "tensor"),
            P("tensor", ("dp", "ctx")),
            P(("dp", "ctx"), "tensor"),
            P("tensor", ("dp", "ctx")),
            P(),
            P(),
            P(),
            P(),
            P(),
            P(None, None, None, "tensor"),
            P(None, None, "tensor"),
            P(),
            P(),
            P(None, None, "tensor"),
            P(None, None, "tensor"),
            P(),
        ),
        out_specs=(
            P("dp", "ctx", None),
            P("dp", "ctx", None),
            P(),
            P(None, None, None, "tensor"),
            P(None, None, "tensor"),
            P(),
            P(),
            P(None, None, "tensor"),
            P(None, None, "tensor"),
            P(),
        ),
        check_vma=False,
    )
```

profile of v0, /device:TPU:0, one launch (start us, length us, event | category | flops | bytes accessed | tf_op | source)
XLA Modules:
  0.0 1288.5 jit_solution(9654820624804582114)
XLA Ops:
  7.2 2.3 copy.79
  12.9 3.4 convolution_convert_fusion.22
  16.3 43.6 %all-gather.7.cloned.1.call-done = bf16[2048,3,512]{0,2,1:T(8,128)(2,1)} async-done(((bf16[256,3,512]{0,2,1:T(8,128)(2,1)}), bf16[2048,3,512]{0,2,1:T(8,128)(2,1)}) %all-gather.7.cloned.1.call-update) | async-done | bytes 6291472 | tf_op jit(solution)/shard_map/all_gather | solution.py:168
  59.9 10.1 fusion.60
  77.6 31.6 %all-gather.9.cloned.1.call-done = bf16[1024,4,4,128]{3,0,2,1:T(8,128)(2,1)} async-done(((bf16[256,4,4,128]{3,0,2,1:T(8,128)(2,1)}), bf16[1024,4,4,128]{3,0,2,1:T(8,128)(2,1)}) %all-gather.9.cloned.1.call-update) | async-done | bytes 4194320 | tf_op jit(solution)/shard_map/all_gather | solution.py:195
  109.1 4.7 copy.87
  113.8 32.0 %all-gather.11.cloned.1.call-done = bf16[1024,4,4,128]{3,0,2,1:T(8,128)(2,1)} async-done(((bf16[256,4,4,128]{3,0,2,1:T(8,128)(2,1)}), bf16[1024,4,4,128]{3,0,2,1:T(8,128)(2,1)}) %all-gather.11.cloned.1.call-update) | async-done | bytes 4194320 | tf_op jit(solution)/shard_map/all_gather | solution.py:196
  145.8 34.5 %while.30 = (s32[]{:T(128)}, f32[256,4,4]{0,2,1:T(4,128)S(1)}, f32[256,4,4]{0,2,1:T(4,128)S(1)}, f32[256,4,4,128]{0,3,2,1:T(8,128)}, bf16[2,512,4,4,128]{4,1,3,2...) while((s32[]{:T(128)}, f32[256,4,4]{0,2,1:T(4,128)S(1)}, ...), condition=%wide.region_3.4_spmd.clone, body=%wide.region_0.3_spmd.clone.sunk | while | flops 1092112384 | bytes 68420744 | solution.py:80
  145.8 6.1 bitcast_reduce_fusion.2
  151.9 5.1 fusion.227
  157.9 4.9 bitcast_add_fusion.6
  162.8 6.1 bitcast_reduce_fusion.2
  169.0 4.9 fusion.227
  174.8 5.5 bitcast_add_fusion.6
  182.2 6.4 convert_bitcast_fusion
  195.1 30.7 %psum.113 = bf16[4,256,16]{1,2,0:T(8,128)(2,1)S(1)} all-reduce(bf16[4,256,16]{1,2,0:T(8,128)(2,1)S(1)} %convolution_convert_fusion.16), channel_id=1, replica_groups=mesh['dp'=2,'ctx'=4,'tensor'=4] {'tensor'}, use_global_device_ids=true, to_apply=%region_5.6 | all-reduce | flops 16384 | bytes 65536 | tf_op jit(solution)/shard_map/psum | solution.py:53
  225.8 119.0 %all-reduce.7.cloned.1.call-done = bf16[4,256,2048]{2,1,0:T(8,128)(2,1)} async-done(((bf16[4,256,2048]{2,1,0:T(8,128)(2,1)}), bf16[4,256,2048]{2,1,0:T(8,128)(2,1)}) %all-reduce.7.cloned.1.call-update) | async-done | bytes 4194320 | tf_op jit(solution)/shard_map/psum | solution.py:52
  344.8 5.4 fusion.156
  355.9 4.5 fusion.108
  360.4 39.8 %all-gather.15.cloned.1.call-done = bf16[2048,2048]{1,0:T(8,128)(2,1)} async-done(((bf16[256,2048]{1,0:T(8,128)(2,1)}), bf16[2048,2048]{1,0:T(8,128)(2,1)}) %all-gather.15.cloned.1.call-update) | async-done | bytes 8388624 | tf_op jit(solution)/shard_map/all_gather | solution.py:216
  400.2 18.0 %multiply_convert_fusion = (bf16[4,256,2048]{2,1,0:T(8,128)(2,1)}, f32[4,256,2048]{2,1,0:T(8,128)}) fusion(f32[4,256,2048]{2,1,0:T(8,128)} %fusion.108, bf16[4,256,2048]{2,1,0:T(8,128)(2,1)} %copy-done.12, bf16[2048,2048]{1,0:T(8,128)(2,1)} %all-gather.15.cloned.1.call-done), kind=kOutput, calls=%fused_computation.76 | convolution fusion | flops 8610906112 | bytes 33554432 | tf_op jit(solution)/shard_map/std,df->stf/dot_general | solution.py:222
  418.2 40.0 %all-gather.17.cloned.1.call-done = bf16[2048,2048]{1,0:T(8,128)(2,1)} async-done(((bf16[2048,256]{1,0:T(8,128)(2,1)}), bf16[2048,2048]{1,0:T(8,128)(2,1)}) %all-gather.17.cloned.1.call-update) | async-done | bytes 8388624 | tf_op jit(solution)/shard_map/all_gather | solution.py:217
  458.2 13.8 %fusion.77 = bf16[4,256,2048]{2,1,0:T(8,128)(2,1)} fusion(bf16[4,256,2048]{2,1,0:T(8,128)(2,1)} %get-tuple-element.277, bf16[2048,2048]{1,0:T(8,128)(2,1)} %all-gather.17.cloned.1.call-done), kind=kOutput, calls=%fused_computation.94 | convolution fusion | flops 8592031744 | bytes 16777216 | tf_op jit(solution)/shard_map/stf,fe->ste/dot_general | solution.py:228
  474.1 3.4 convolution_convert_fusion.20
  477.4 20.5 %psum.115 = bf16[4,256,16]{1,2,0:T(8,128)(2,1)S(1)} all-reduce(bf16[4,256,16]{1,2,0:T(8,128)(2,1)S(1)} %convolution_convert_fusion.20), channel_id=1, replica_groups=mesh['dp'=2,'ctx'=4,'tensor'=4] {'tensor'}, use_global_device_ids=true, to_apply=%region_9.10 | all-reduce | flops 16384 | bytes 65536 | tf_op jit(solution)/shard_map/psum | solution.py:53
  498.0 130.2 %all-reduce.9.cloned.1.call-done = bf16[4,256,2048]{2,1,0:T(8,128)(2,1)} async-done(((bf16[4,256,2048]{2,1,0:T(8,128)(2,1)}), bf16[4,256,2048]{2,1,0:T(8,128)(2,1)}) %all-reduce.9.cloned.1.call-update) | async-done | bytes 4194320 | tf_op jit(solution)/shard_map/psum | solution.py:52
  628.2 6.2 fusion.157
  635.4 4.2 copy-done.16
  639.6 2.5 fusion.58
  642.2 4.8 fusion.80
  648.1 4.5 fusion.104
  652.7 20.0 %fusion.47 = bf16[4,256,2048]{2,1,0:T(8,128)(2,1)} fusion(f32[4,256,2048]{2,1,0:T(8,128)} %get-tuple-element.278, f32[4,256,2048]{2,1,0:T(8,128)} %fusion.104, bf16[4,256,2048]{2,1,0:T(8,128)(2,1)S(1)} %get-tuple-element.270, bf16[2048,2048]{1,0:T(8,128)(2,1)} %all-gather.17.cloned.1.call-done), kind=kOutput, calls=%fused_computation.53 | convolution fusion | flops 8642363392 | bytes 33554432 | tf_op jit(solution)/shard_map/ste,fe->stf/dot_general | solution.py:257
  672.7 14.1 %fusion.74 = bf16[4,256,2048]{2,1,0:T(8,128)(2,1)} fusion(bf16[4,256,2048]{2,1,0:T(8,128)(2,1)} %fusion.47, bf16[2048,2048]{1,0:T(8,128)(2,1)} %all-gather.15.cloned.1.call-done), kind=kOutput, calls=%fused_computation.93 | convolution fusion | flops 8592031744 | bytes 16777216 | tf_op jit(solution)/shard_map/stf,df->std/dot_general | solution.py:264
  686.9 3.4 convolution_convert_fusion.18
  690.3 17.8 %psum.117 = bf16[4,256,16]{1,2,0:T(8,128)(2,1)S(1)} all-reduce(bf16[4,256,16]{1,2,0:T(8,128)(2,1)S(1)} %convolution_convert_fusion.18), channel_id=1, replica_groups=mesh['dp'=2,'ctx'=4,'tensor'=4] {'tensor'}, use_global_device_ids=true, to_apply=%region_15.16 | all-reduce | flops 16384 | bytes 65536 | tf_op jit(solution)/shard_map/psum | solution.py:53
  708.0 133.9 %all-reduce.11.cloned.1.call-done = bf16[4,256,2048]{2,1,0:T(8,128)(2,1)} async-done(((bf16[4,256,2048]{2,1,0:T(8,128)(2,1)}), bf16[4,256,2048]{2,1,0:T(8,128)(2,1)}) %all-reduce.11.cloned.1.call-update) | async-done | bytes 4194320 | tf_op jit(solution)/shard_map/psum | solution.py:52
  841.9 11.1 fusion.154
  853.0 7.7 fusion.85
  861.9 2.4 fusion.82
  870.7 44.3 %while.31 = (s32[]{:T(128)}, f32[256,4,4,128]{0,3,2,1:T(8,128)}, bf16[2,512,4,4,128]{4,1,0,3,2:T(8,128)(2,1)}, bf16[2,512,4,4,128]{4,1,0,3,2:T(8,128)(2,1)}, bf1...) while((s32[]{:T(128)}, f32[256,4,4,128]{0,3,2,1:T(8,128)}, ...), condition=%wide.region_20.21_spmd.clone, body=%wide.region_19.20_spmd.clone.sunk | while | flops 2703753216 | bytes 161532144 | solution.py:123
  870.9 3.0 fusion.239
  874.0 3.3 copy-done.3
  881.2 2.7 bitcast_dynamic-update-slice_fusion.4
  883.9 5.2 bitcast_add_fusion.7
  889.9 2.8 bitcast_dynamic-update-slice_fusion.5
  892.7 3.0 fusion.239
  895.7 3.3 copy-done.3
  903.0 2.6 bitcast_dynamic-update-slice_fusion.4
  905.6 5.8 bitcast_add_fusion.7
  912.2 2.8 bitcast_dynamic-update-slice_fusion.5
  916.1 3.0 fusion.162
  920.9 4.0 fusion.161
  935.2 2.8 fusion.160
  939.9 18.8 %reduce-scatter.3.cloned.1.call-done = bf16[256,4,4,128]{3,0,2,1:T(8,128)(2,1)} async-done(((bf16[1024,4,4,128]{3,0,2,1:T(8,128)(2,1)}), bf16[256,4,4,128]{3,0,2,1:T(8,128)(2,1)}) %reduce-scatter.3.cloned.1.call-update) | async-done | bytes 1048592 | tf_op jit(solution)/shard_map/reduce_scatter | solution.py:304
  961.9 43.8 %reduce-scatter.5.cloned.1.call-done = bf16[256,4,4,128]{3,0,2,1:T(8,128)(2,1)} async-done(((bf16[1024,4,4,128]{3,0,2,1:T(8,128)(2,1)}), bf16[256,4,4,128]{3,0,2,1:T(8,128)(2,1)}) %reduce-scatter.5.cloned.1.call-update) | async-done | bytes 1048592 | tf_op jit(solution)/shard_map/reduce_scatter | solution.py:307
  1011.0 2.5 fusion.86
  1015.2 19.0 %psum.119 = bf16[4,256,16]{1,2,0:T(8,128)(2,1)S(1)} all-reduce(bf16[4,256,16]{1,2,0:T(8,128)(2,1)S(1)} %fusion.86), channel_id=1, replica_groups=mesh['dp'=2,'ctx'=4,'tensor'=4] {'tensor'}, use_global_device_ids=true, to_apply=%region_24.25 | all-reduce | flops 16384 | bytes 65536 | tf_op jit(solution)/shard_map/psum | solution.py:53
  1034.1 2.8 fusion.158
  1038.9 11.4 fusion.70
  1050.4 62.6 %all-reduce.15.cloned.1.call-done = (bf16[8,16,2048]{2,0,1:T(8,128)(2,1)}, bf16[8,16,3,512]{3,0,2,1:T(8,128)(2,1)}, bf16[8,16,512]{2,0,1:T(8,128)(2,1)}, bf16[8,...) async-done(((bf16[8,16,2048]{2,0,1:T(8,128)(2,1)}, ...) | async-done | bytes 3670032 | tf_op jit(solution)/shard_map/psum | solution.py:366
  1113.0 2.4 copy.124
  1122.3 2.3 copy.130
  1128.8 142.3 %all-reduce.13.cloned.1.call-done = bf16[4,256,2048]{2,1,0:T(8,128)(2,1)} async-done(((bf16[4,256,2048]{2,1,0:T(8,128)(2,1)}), bf16[4,256,2048]{2,1,0:T(8,128)(2,1)}) %all-reduce.13.cloned.1.call-update) | async-done | bytes 4194320 | tf_op jit(solution)/shard_map/psum | solution.py:52
  1271.1 10.8 add_convert_fusion
  (199 shorter events, 86.0 us)
Async XLA Ops:
  7.2 3.9 copy-start
  7.2 52.7 %all-gather.7.cloned.1.call-start = ((), (), s32[]{:S(2)}) async-start(), calls=%async_computation.2 | async-start | bytes 7077888 | tf_op jit(solution)/shard_map/all_gather | solution.py:168
  9.6 99.5 %all-gather.9.cloned.1.call-start = ((), (), s32[]{:S(2)}) async-start(), calls=%async_computation.3 | async-start | bytes 5242880 | tf_op jit(solution)/shard_map/all_gather | solution.py:195
  11.0 58.9 %copy-start.24 = (bf16[4,16,3,512]{3,0,2,1:T(4,128)(2,1)}, bf16[4,16,3,512]{3,0,2,1:T(4,128)(2,1)S(1)}, u32[]{:S(2)}) copy-start(bf16[4,16,3,512]{3,0,2,1:T(4,128)(2,1)S(1)} %convolution_convert_fusion.13) | copy-start | bytes 589828
  16.3 53.7 %copy-start.36 = (bf16[4,16,256]{2,1,0:T(8,128)(2,1)}, bf16[4,16,256]{2,1,0:T(8,128)(2,1)S(1)}, u32[]{:S(2)}) copy-start(bf16[4,16,256]{2,1,0:T(8,128)(2,1)S(1)} %convolution_convert_fusion.22) | copy-start | bytes 98308
  74.5 71.3 %all-gather.11.cloned.1.call-start = ((), (), s32[]{:S(2)}) async-start(), calls=%async_computation.4 | async-start | bytes 5242880 | tf_op jit(solution)/shard_map/all_gather | solution.py:196
  75.9 106.3 %all-gather.13.cloned.1.call-start = ((), (), s32[]{:S(2)}) async-start(), calls=%async_computation.5 | async-start | bytes 2359296 | tf_op jit(solution)/shard_map/all_gather | solution.py:169
  76.4 268.4 %all-reduce.7.cloned.1.call-start = ((), (), s32[]{:S(2)}) async-start(), calls=%async_computation.6 | async-start | bytes 8388608 | tf_op jit(solution)/shard_map/psum | solution.py:52
  151.9 6.0 copy-start.2
  169.0 5.8 copy-start.2
  182.1 12.7 copy-start.17
  182.1 7.8 copy-start.39
  182.1 7.8 copy-start.40
  188.6 211.6 %all-gather.15.cloned.1.call-start = ((), (), s32[]{:S(2)}) async-start(), calls=%async_computation.7 | async-start | bytes 9437184 | tf_op jit(solution)/shard_map/all_gather | solution.py:216
  189.1 269.0 %all-gather.17.cloned.1.call-start = ((), (), s32[]{:S(2)}) async-start(), calls=%async_computation.8 | async-start | bytes 9437184 | tf_op jit(solution)/shard_map/all_gather | solution.py:217
  189.9 438.3 %all-reduce.9.cloned.1.call-start = ((), (), s32[]{:S(2)}) async-start(), calls=%async_computation.9 | async-start | bytes 8388608 | tf_op jit(solution)/shard_map/psum | solution.py:52
  225.8 124.5 %copy-start.31 = (bf16[4,256,16]{1,2,0:T(8,128)(2,1)}, bf16[4,256,16]{1,2,0:T(8,128)(2,1)S(1)}, u32[]{:S(2)}) copy-start(bf16[4,256,16]{1,2,0:T(8,128)(2,1)S(1)} %psum.113) | copy-start | bytes 98308
  350.3 3.5 copy-start.6
  350.3 1.0 copy-start.43
  350.3 1.0 copy-start.44
  353.8 2.1 copy-start.12
  355.9 62.3 %copy-start.27 = (bf16[4,256,16]{1,2,0:T(8,128)(2,1)}, bf16[4,256,16]{1,2,0:T(8,128)(2,1)S(1)}, u32[]{:S(2)}) copy-start(bf16[4,256,16]{1,2,0:T(8,128)(2,1)S(1)} %convolution_convert_fusion.21) | copy-start | bytes 98308
  458.2 13.9 %copy-start.26 = (bf16[8,16,2048]{2,1,0:T(8,128)(2,1)S(1)}, bf16[8,16,2048]{2,1,0:T(8,128)(2,1)}, u32[]{:S(2)}) copy-start(bf16[8,16,2048]{2,1,0:T(8,128)(2,1)} %param.40) | copy-start | bytes 1572868
  472.0 369.9 %all-reduce.11.cloned.1.call-start = ((), (), s32[]{:S(2)}) async-start(), calls=%async_computation.10 | async-start | bytes 8388608 | tf_op jit(solution)/shard_map/psum | solution.py:52
  498.0 136.4 %copy-start.33 = (bf16[4,256,16]{1,2,0:T(8,128)(2,1)}, bf16[4,256,16]{1,2,0:T(8,128)(2,1)S(1)}, u32[]{:S(2)}) copy-start(bf16[4,256,16]{1,2,0:T(8,128)(2,1)S(1)} %psum.115) | copy-start | bytes 98308
  634.4 7.8 copy-start.7
  634.4 5.2 copy-start.16
  634.4 5.2 copy-start.42
  635.4 6.8 copy-start.45
  646.9 25.8 %copy-start.10 = (bf16[4,256,2048]{2,1,0:T(8,128)(2,1)}, bf16[4,256,2048]{2,1,0:T(8,128)(2,1)S(1)}, u32[]{:S(2)}) copy-start(bf16[4,256,2048]{2,1,0:T(8,128)(2,1)S(1)} %get-tuple-element.270) | copy-start | bytes 12582916
  648.1 24.6 %copy-start.29 = (bf16[4,256,16]{1,2,0:T(8,128)(2,1)}, bf16[4,256,16]{1,2,0:T(8,128)(2,1)S(1)}, u32[]{:S(2)}) copy-start(bf16[4,256,16]{1,2,0:T(8,128)(2,1)S(1)} %convolution_convert_fusion.19) | copy-start | bytes 98308
  686.8 271.9 %reduce-scatter.3.cloned.1.call-start = ((), (), s32[]{:S(2)}) async-start(), calls=%async_computation.11 | async-start | bytes 5242880 | tf_op jit(solution)/shard_map/reduce_scatter | solution.py:304
  852.9 7.7 copy-start.14
  853.0 8.9 copy-start.46
  860.7 3.6 copy-start.13
  864.8 1.0 copy-start.19
  870.9 6.3 copy-start.8
  874.0 3.3 copy-start.3
  879.3 2.0 copy-start.5
  883.9 6.0 copy-start.4
  892.7 6.3 copy-start.8
  895.7 3.3 copy-start.3
  901.0 2.0 copy-start.5
  905.6 6.6 copy-start.4
  915.0 1.1 copy-start.28
  915.0 4.1 copy-start.41
  915.0 90.7 %reduce-scatter.5.cloned.1.call-start = ((), (), s32[]{:S(2)}) async-start(), calls=%async_computation.12 | async-start | bytes 5242880 | tf_op jit(solution)/shard_map/reduce_scatter | solution.py:307
  915.7 11.0 copy-start.34
  915.8 197.3 %all-reduce.15.cloned.1.call-start = ((), (), s32[]{:S(2)}) async-start(), calls=%async_computation.14 | async-start | bytes 7340032 | tf_op jit(solution)/shard_map/psum | solution.py:366
  916.1 10.7 copy-start.11
  920.9 8.4 copy-start.15
  920.9 8.4 copy-start.30
  926.8 5.1 copy-start.9
  927.4 6.3 copy-start.18
  927.4 7.8 copy-start.32
  934.1 74.9 %copy-start.22 = (bf16[256,4,1,512]{3,0,2,1:T(8,128)(2,1)S(1)}, bf16[256,4,1,512]{3,0,2,1:T(8,128)(2,1)}, u32[]{:S(2)}) copy-start(bf16[256,4,1,512]{3,0,2,1:T(8,128)(2,1)} %copy.156) | copy-start | bytes 3145732
  934.1 74.9 %copy-start.37 = (bf16[4,16,256]{2,1,0:T(8,128)(2,1)S(1)}, bf16[4,16,256]{2,1,0:T(8,128)(2,1)}, u32[]{:S(2)}) copy-start(bf16[4,16,256]{2,1,0:T(8,128)(2,1)} %copy-done.36) | copy-start | bytes 98308
  938.0 73.0 %copy-start.25 = (bf16[4,16,3,512]{3,0,2,1:T(4,128)(2,1)S(1)}, bf16[4,16,3,512]{3,0,2,1:T(4,128)(2,1)}, u32[]{:S(2)}) copy-start(bf16[4,16,3,512]{3,0,2,1:T(4,128)(2,1)} %copy-done.24) | copy-start | bytes 589828
  1011.0 27.9 %copy-start.23 = (bf16[256,4,1,512]{3,0,2,1:T(8,128)(2,1)S(1)}, bf16[256,4,1,512]{3,0,2,1:T(8,128)(2,1)}, u32[]{:S(2)}) copy-start(bf16[256,4,1,512]{3,0,2,1:T(8,128)(2,1)} %stack.13) | copy-start | bytes 3145732
  1038.8 232.2 %all-reduce.13.cloned.1.call-start = ((), (), s32[]{:S(2)}) async-start(), calls=%async_computation.13 | async-start | bytes 8388608 | tf_op jit(solution)/shard_map/psum | solution.py:52
  1050.4 220.7 %copy-start.21 = (bf16[4,16,2048]{2,0,1:T(4,128)(2,1)S(1)}, bf16[4,16,2048]{2,0,1:T(4,128)(2,1)}, u32[]{:S(2)}) copy-start(bf16[4,16,2048]{2,0,1:T(4,128)(2,1)} %copy-done.20) | copy-start | bytes 786436
  1113.0 14.0 %copy-start.35 = (bf16[8,16,3,512]{3,0,2,1:T(8,128)(2,1)S(1)}, bf16[8,16,3,512]{3,0,2,1:T(8,128)(2,1)}, u32[]{:S(2)}) copy-start(bf16[8,16,3,512]{3,0,2,1:T(8,128)(2,1)} %get-tuple-element.259) | copy-start | bytes 1179652
  1113.0 15.0 %copy-start.38 = (bf16[8,16,512]{2,0,1:T(8,128)(2,1)S(1)}, bf16[8,16,512]{2,0,1:T(8,128)(2,1)}, u32[]{:S(2)}) copy-start(bf16[8,16,512]{2,0,1:T(8,128)(2,1)} %get-tuple-element.260) | copy-start | bytes 393220
  1128.0 153.8 %copy-start.1 = (bf16[8,16,2048]{2,1,0:T(8,128)(2,1)S(1)}, bf16[8,16,2048]{2,1,0:T(8,128)(2,1)}, u32[]{:S(2)}) copy-start(bf16[8,16,2048]{2,1,0:T(8,128)(2,1)} %param.34) | copy-start | bytes 1572868
  (1 other events, 0.7 us)
Sparse Core Ops, SparseCore 0:
  10.5 49.3 all-gather.6
  74.6 34.4 all-gather.8
  111.3 34.4 all-gather.10
  147.5 28.1 all-gather.12
  188.7 156.0 all-reduce.6
  346.7 53.3 all-gather.14
  402.2 55.9 all-gather.16
  472.1 155.9 all-reduce.8
  686.9 154.9 all-reduce.10
  915.1 43.4 reduce-scatter.2
  961.2 44.4 reduce-scatter.4
  1039.0 73.9 all-reduce.14
  1115.9 155.0 all-reduce.12
where the time goes:
time: 1290 us
  waiting for transfers between devices  840 us (65%)
  matrix products  251 us (19%)
  blocking collectives  87.9 us (7%)
  local copies, waits for them, and re-layouts  60.7 us (5%)
  other arithmetic  32.8 us (3%)
  between operations  14.7 us (1%)
    psum x4, waiting for transfers between devices, sum_heads(): lax.psum(parts[0].astype(jnp.bfloat16), 'tensor').astype(jnp.float32)  525 us
    psum x4, blocking collectives, sum_heads(): lax.psum(parts[1].astype(jnp.bfloat16), 'tensor').astype(jnp.float32)  87.9 us
    psum x1, waiting for transfers between devices, per_device(): lax.psum(mixing_down_part.astype(jnp.bfloat16), ('dp', 'ctx'))  62.6 us
    reduce_scatter x1, waiting for transfers between devices, per_device(): lax.psum_scatter(value_parts.astype(jnp.bfloat16), 'ctx', scatter_dimensi...  43.8 us
    all_gather x1, waiting for transfers between devices, per_device(): lax.all_gather(mixing_weight, ('dp', 'ctx'), axis=0, tiled=True)  43.6 us
    all_gather x1, waiting for transfers between devices, per_device(): lax.all_gather(contract_weight, ('dp', 'ctx'), axis=1, tiled=True)  40 us
    all_gather x1, waiting for transfers between devices, per_device(): lax.all_gather(expand_weight, ('dp', 'ctx'), axis=0, tiled=True)  39.8 us
    unnamed x96, local copies, waits for them, and re-layouts  32.6 us
  transfers between devices with their start and end apart: 13, of which 12 were waited for; matrix products, arithmetic and copies ran while one was open for 11% of the time, Pallas kernels for 0%

commit v1 on v0

v1 whole, which is shorter than its diff:
```python
import functools
import math

import jax
import jax.numpy as jnp
from jax import lax
from jax.experimental import pallas as pl
from jax.experimental.pallas import tpu as pltpu
from jax.sharding import PartitionSpec as P

HEAD_DIM = 128
NADAPT = 8
CHUNK_ROWS = 128


BF = jnp.bfloat16
F32 = jnp.float32
MESH_IDS = pl.DeviceIdType.MESH
RANK_ROWS = 16
GELU_C = 0.7978845608028654
GELU_A = 0.044715


def dot_nn(a, b):
    return lax.dot_general(a, b, (((1,), (0,)), ((), ())), preferred_element_type=F32)


def dot_nt(a, b):
    return lax.dot_general(a, b, (((1,), (1,)), ((), ())), preferred_element_type=F32)


def dot_tn(a, b):
    return lax.dot_general(a, b, (((0,), (0,)), ((), ())), preferred_element_type=F32)


def tile(index, size):
    return pl.ds(pl.multiple_of(index * size, size), size)


def middle_kernel(
    sizes,
    context,
    hidden,
    cotangent,
    w_out,
    w_exp,
    w_con,
    od,
    ou,
    ed,
    eu,
    cd,
    cu,
    gains,
    hidden_out,
    first_low,
    active,
    second_low,
    before_grad,
    attn_low,
    context_grad,
    out_rank,
    exp_rank,
    con_rank,
    con_rank_grad,
    exp_rank_grad,
    out_rank_grad,
    acc,
    red_up,
    red_down,
    normed,
    spreads,
    slope,
    second,
    stage_d,
    stage_f,
    rows_in,
    rank_buf,
    in_sem,
    out_sem,
    red_send,
    red_recv,
    cast_send,
    cast_recv,
):
    ranks, chunks, rows, per_seq, period = sizes
    half = rows // 2
    width = hidden.shape[1]
    units = w_exp.shape[1]
    heads = w_out.shape[0]
    block = min(16, half)
    tile_f = math.gcd(units, 256)
    tile_d = math.gcd(width, 256)
    tile_h = math.gcd(heads, 256)
    me = lax.axis_index("tensor")

    barrier = pltpu.get_barrier_semaphore()

    @pl.when(me > 0)
    def _():
        pl.semaphore_signal(barrier, inc=1, device_id={"tensor": me - 1}, device_id_type=MESH_IDS)

    @pl.when(me < ranks - 1)
    def _():
        pl.semaphore_signal(barrier, inc=1, device_id={"tensor": me + 1}, device_id_type=MESH_IDS)

    pl.semaphore_wait(
        barrier, jnp.minimum(me, 1) + jnp.minimum(ranks - 1 - me, 1)
    )

    def job_of(number, rounds):
        safe = jnp.maximum(number, 0)
        chunk = safe % period
        valid = (number >= 0) & (chunk < chunks) & (safe < rounds * period)
        return valid, jnp.minimum(chunk, chunks - 1)

    def comm(tick, way):
        upward = way == 0
        place = me if upward else ranks - 1 - me
        ahead = me + 1 if upward else me - 1
        behind = me - 1 if upward else me + 1
        red = red_up if upward else red_down
        part = pl.ds(way * half, half)

        def red_copy(c):
            return pltpu.make_async_remote_copy(
                src_ref=red.at[c],
                dst_ref=red.at[c],
                send_sem=red_send.at[way, c],
                recv_sem=red_recv.at[way, c],
                device_id={"tensor": ahead},
                device_id_type=MESH_IDS,
            )

        def cast_copy(c):
            return pltpu.make_async_remote_copy(
                src_ref=acc.at[c, part],
                dst_ref=acc.at[c, part],
                send_sem=cast_send.at[way, c],
                recv_sem=cast_recv.at[way, c],
                device_id={"tensor": behind},
                device_id_type=MESH_IDS,
            )

        old_red, c_old = job_of(tick - 2 - place, 3)

        @pl.when(old_red & (place < ranks - 1))
        def _():
            red_copy(c_old).wait_send()

        old_cast, c_cast = job_of(tick - 2 * ranks + place, 3)

        @pl.when(old_cast & (place > 0))
        def _():
            cast_copy(c_cast).wait_send()

        now_red, c = job_of(tick - 1 - place, 3)

        @pl.when(now_red & (place == 0))
        def _():
            red[c] = acc[c, part, :]

        @pl.when(now_red & (place > 0))
        def _():
            red_copy(c).wait_recv()

        @pl.when(now_red & (place > 0) & (place < ranks - 1))
        def _():
            @pl.loop(0, half // block)
            def _(i):
                rs = tile(i, block)
                own = acc[c, pl.ds(pl.multiple_of(way * half + i * block, block), block), :]
                red[c, rs, :] = (red[c, rs, :].astype(F32) + own.astype(F32)).astype(BF)

        @pl.when(now_red & (place < ranks - 1))
        def _():
            red_copy(c).start()

        @pl.when(now_red & (place == ranks - 1))
        def _():
            @pl.loop(0, half // block)
            def _(i):
                rs = tile(i, block)
                own_rs = pl.ds(pl.multiple_of(way * half + i * block, block), block)
                acc[c, own_rs, :] = (
                    red[c, rs, :].astype(F32) + acc[c, own_rs, :].astype(F32)
                ).astype(BF)

            cast_copy(c).start()

        now_cast, cc = job_of(tick - (2 * ranks - 1 - place), 3)

        @pl.when(now_cast & (place < ranks - 1))
        def _():
            cast_copy(cc).wait_recv()

        @pl.when(now_cast & (place > 0) & (place < ranks - 1))
        def _():
            cast_copy(cc).start()

    def rows_of(c):
        return tile(c, rows)

    def bring(source, c):
        return pltpu.make_async_copy(source.at[rows_of(c)], rows_in, in_sem)

    def keep(index, source, target, c):
        return pltpu.make_async_copy(source, target.at[rows_of(c)], out_sem.at[index])

    def mean(values):
        return jnp.sum(values, axis=-1, keepdims=True) * (1.0 / width)

    def attend_part(c, s):
        mine = context[rows_of(c), :]
        low = dot_nt(mine, od[s]).astype(BF)
        out_rank[rows_of(c), :] = low

        @pl.loop(0, width // tile_d)
        def _(i):
            cs = tile(i, tile_d)
            acc[c, :, cs] = (dot_nn(mine, w_out[:, cs]) + dot_nn(low, ou[s, :, cs])).astype(BF)

    def forward_first(c, s):
        bring(hidden, c).wait()

        @pl.loop(0, rows // block)
        def _(i):
            rs = tile(i, block)
            total = rows_in[rs, :].astype(F32) + acc[c, rs, :].astype(F32)
            centred = total - mean(total)
            spread = lax.rsqrt(mean(centred * centred) + 1e-06)
            n = centred * spread
            normed[c, rs, :] = n.astype(BF)
            spreads[c, rs, :] = jnp.broadcast_to(spread, (block, 128))
            stage_d[rs, :] = (n * gains[0:1, :] + gains[1:2, :]).astype(BF)

        low = dot_nt(stage_d[...], ed[s]).astype(BF)
        exp_rank[rows_of(c), :] = low
        rank_buf[...] = low

        @pl.loop(0, units // tile_f)
        def _(i):
            cs = tile(i, tile_f)
            b = dot_nn(stage_d[...], w_exp[:, cs]) + dot_nn(rank_buf[...], eu[s, :, cs])
            square = b * b
            t = jnp.tanh(GELU_C * b * (1.0 + GELU_A * square))
            upper = 0.5 * (1.0 + t)
            stage_f[:, cs] = (b * upper).astype(BF)
            slope[c, :, cs] = (
                upper
                + (0.5 * GELU_C) * b * (1.0 - t * t) * (1.0 + (3.0 * GELU_A) * square)
            ).astype(BF)

    def forward_second(c, s):
        low = dot_nt(stage_f[...], cd[s]).astype(BF)
        con_rank[rows_of(c), :] = low
        rank_buf[...] = low

        @pl.loop(0, width // tile_d)
        def _(i):
            cs = tile(i, tile_d)
            acc[c, :, cs] = (
                dot_nn(stage_f[...], w_con[:, cs]) + dot_nn(rank_buf[...], cu[s, :, cs])
            ).astype(BF)

        keep(0, stage_d, first_low, c).start()
        keep(1, stage_f, active, c).start()

    def back_first(c, s):
        bring(cotangent, c).wait()

        @pl.loop(0, rows // block)
        def _(i):
            rs = tile(i, block)
            first = normed[c, rs, :].astype(F32) * gains[0:1, :] + gains[1:2, :]
            total = first + acc[c, rs, :].astype(F32)
            centred = total - mean(total)
            spread = lax.rsqrt(mean(centred * centred) + 1e-06)
            n = centred * spread
            stage_d[rs, :] = (n * gains[2:3, :] + gains[3:4, :]).astype(BF)
            g = rows_in[rs, :].astype(F32) * gains[2:3, :]
            second[c, rs, :] = (spread * (g - mean(g) - n * mean(g * n))).astype(BF)

        low = dot_nt(second[c], cu[s]).astype(BF)
        con_rank_grad[rows_of(c), :] = low
        rank_buf[...] = low

        @pl.loop(0, units // tile_f)
        def _(i):
            cs = tile(i, tile_f)
            da = dot_nt(second[c], w_con[cs, :]) + dot_nn(rank_buf[...], cd[s, :, cs])
            stage_f[:, cs] = (da * slope[c, :, cs].astype(F32)).astype(BF)

    def back_second(c, s):
        low = dot_nt(stage_f[...], eu[s]).astype(BF)
        exp_rank_grad[rows_of(c), :] = low
        rank_buf[...] = low

        @pl.loop(0, width // tile_d)
        def _(i):
            cs = tile(i, tile_d)
            acc[c, :, cs] = (
                dot_nt(stage_f[...], w_exp[cs, :]) + dot_nn(rank_buf[...], ed[s, :, cs])
            ).astype(BF)

        keep(0, stage_d, hidden_out, c).start()
        keep(1, stage_f, before_grad, c).start()
        keep(2, second.at[c], second_low, c).start()

    def last_first(c, s):
        @pl.loop(0, rows // block)
        def _(i):
            rs = tile(i, block)
            n = normed[c, rs, :].astype(F32)
            g = (second[c, rs, :].astype(F32) + acc[c, rs, :].astype(F32)) * gains[0:1, :]
            spread = spreads[c, rs, 0:1]
            stage_d[rs, :] = (spread * (g - mean(g) - n * mean(g * n))).astype(BF)

    def last_second(c, s):
        low = dot_nt(stage_d[...], ou[s]).astype(BF)
        out_rank_grad[rows_of(c), :] = low
        rank_buf[...] = low

        @pl.loop(0, heads // tile_h)
        def _(i):
            cs = tile(i, tile_h)
            context_grad[rows_of(c), cs] = (
                dot_nt(stage_d[...], w_out[cs, :]) + dot_nn(rank_buf[...], od[s, :, cs])
            ).astype(BF)

        keep(0, stage_d, attn_low, c).start()

    @pl.loop(0, 3 * period + chunks)
    def _(tick):
        stage = tick // period
        valid, c = job_of(tick, 4)
        s = c // per_seq
        last_valid, last_c = job_of(tick - 1, 4)
        last_stage = jnp.maximum(tick - 1, 0) // period

        comm(tick, 0)

        @pl.when(last_valid & (last_stage >= 1))
        def _():
            keep(0, stage_d, first_low, last_c).wait()

        @pl.when(last_valid & (last_stage >= 1) & (last_stage <= 2))
        def _():
            keep(1, stage_f, active, last_c).wait()

        @pl.when(last_valid & (last_stage == 2))
        def _():
            keep(2, second.at[last_c], second_low, last_c).wait()

        pl.when(valid & (stage == 1))(lambda: forward_first(c, s))
        pl.when(valid & (stage == 2))(lambda: back_first(c, s))
        pl.when(valid & (stage == 3))(lambda: last_first(c, s))

        comm(tick, 1)

        pl.when(valid & (stage == 0))(lambda: attend_part(c, s))
        pl.when(valid & (stage == 1))(lambda: forward_second(c, s))
        pl.when(valid & (stage == 2))(lambda: back_second(c, s))
        pl.when(valid & (stage == 3))(lambda: last_second(c, s))

        next_valid, next_c = job_of(tick + 1, 4)
        next_stage = (tick + 1) // period
        pl.when(next_valid & (next_stage == 1))(lambda: bring(hidden, next_c).start())
        pl.when(next_valid & (next_stage == 2))(lambda: bring(cotangent, next_c).start())

    keep(0, stage_d, attn_low, chunks - 1).wait()


def middle(context, hidden, cotangent, w_out, w_exp, w_con, picked, gains, tok):
    od, ou, ed, eu, cd, cu = picked
    total, width = hidden.shape
    heads, units = w_out.shape[0], w_exp.shape[1]
    ranks = lax.axis_size("tensor")
    rank = od.shape[1]
    rows = math.gcd(tok, CHUNK_ROWS)
    chunks = total // rows
    period = max(chunks, 2 * ranks)
    sizes = (ranks, chunks, rows, tok // rows, period)
    vm = pl.BlockSpec(memory_space=pltpu.VMEM)
    hb = pl.BlockSpec(memory_space=pl.ANY)
    half = rows // 2

    def shape(*dims):
        return jax.ShapeDtypeStruct(dims, BF)

    return pl.pallas_call(
        functools.partial(middle_kernel, sizes),
        out_shape=(
            shape(total, width),
            shape(total, width),
            shape(total, units),
            shape(total, width),
            shape(total, units),
            shape(total, width),
            shape(total, heads),
        )
        + (shape(total, rank),) * 6,
        in_specs=[vm, hb, hb] + [vm] * 10,
        out_specs=(hb,) * 6 + (vm,) * 7,
        scratch_shapes=[
            pltpu.VMEM((chunks, rows, width), BF),
            pltpu.VMEM((chunks, half, width), BF),
            pltpu.VMEM((chunks, half, width), BF),
            pltpu.VMEM((chunks, rows, width), BF),
            pltpu.VMEM((chunks, rows, 128), F32),
            pltpu.VMEM((chunks, rows, units), BF),
            pltpu.VMEM((chunks, rows, width), BF),
            pltpu.VMEM((rows, width), BF),
            pltpu.VMEM((rows, units), BF),
            pltpu.VMEM((rows, width), BF),
            pltpu.VMEM((rows, rank), BF),
            pltpu.SemaphoreType.DMA(()),
            pltpu.SemaphoreType.DMA((3,)),
            pltpu.SemaphoreType.DMA((2, chunks)),
            pltpu.SemaphoreType.DMA((2, chunks)),
            pltpu.SemaphoreType.DMA((2, chunks)),
            pltpu.SemaphoreType.DMA((2, chunks)),
        ],
        compiler_params=pltpu.CompilerParams(
            collective_id=0, has_side_effects=True, vmem_limit_bytes=60 * 2**20
        ),
        cost_estimate=pl.CostEstimate(
            flops=8 * total * width * units + 4 * total * width * heads,
            bytes_accessed=16 * total * width,
            transcendentals=total * units,
        ),
    )(context, hidden, cotangent, w_out, w_exp, w_con, od, ou, ed, eu, cd, cu, gains)


def pick_rows(onehot_low, table):
    return jnp.einsum(
        "sn,n...->s...", onehot_low, table, preferred_element_type=jnp.float32
    ).astype(jnp.bfloat16)


def split_blocks(values, block_rows):
    return values.reshape((values.shape[0] // block_rows, block_rows) + values.shape[1:])


def attend_fold(queries, score_scale, state_now, shard_rows):
    key_rows, value_rows = shard_rows
    block_rows = math.gcd(key_rows.shape[0], 512)

    def attend_advance(state, pair):
        running_max, running_sum, weighted = state
        key_block, value_block = pair
        scores = (
            jnp.einsum("tshd,kshd->tshk", queries, key_block, preferred_element_type=jnp.float32)
            * score_scale
        )
        new_max = jnp.maximum(running_max, jnp.max(scores, axis=-1))
        factor = jnp.exp(running_max - new_max)
        raised = jnp.exp(scores - new_max[..., None])
        running_sum = running_sum * factor + jnp.sum(raised, axis=-1)
        weighted = weighted * factor[..., None] + jnp.einsum(
            "tshk,kshd->tshd",
            raised.astype(jnp.bfloat16),
            value_block,
            preferred_element_type=jnp.float32,
        )
        return ((new_max, running_sum, weighted), None)

    state_now, _ = lax.scan(
        attend_advance,
        state_now,
        (split_blocks(key_rows, block_rows), split_blocks(value_rows, block_rows)),
    )
    return state_now


def score_grads(
    query_block, grad_block, log_block, delta_block, key_block, value_block, score_scale
):
    scores = (
        jnp.einsum("tshd,kshd->tshk", query_block, key_block, preferred_element_type=jnp.float32)
        * score_scale
    )
    probs = jnp.exp(scores - log_block[..., None])
    dprobs = jnp.einsum(
        "tshd,kshd->tshk", grad_block, value_block, preferred_element_type=jnp.float32
    )
    dscores = (probs * (dprobs - delta_block[..., None])).astype(jnp.bfloat16)
    return (probs.astype(jnp.bfloat16), dscores)


def key_sweep(queries, grad_out, log_total, delta_rows, key_all, value_all, score_scale):
    block_rows = math.gcd(key_all.shape[0], 512)

    def key_advance(query_grad, pair):
        key_block, value_block = pair
        probs, dscores = score_grads(
            queries, grad_out, log_total, delta_rows, key_block, value_block, score_scale
        )
        query_grad = query_grad + score_scale * jnp.einsum(
            "tshk,kshd->tshd", dscores, key_block, preferred_element_type=jnp.float32
        )
        key_part = score_scale * jnp.einsum(
            "tshk,tshd->kshd", dscores, queries, preferred_element_type=jnp.float32
        )
        value_part = jnp.einsum(
            "tshk,tshd->kshd", probs, grad_out, preferred_element_type=jnp.float32
        )
        return (query_grad, (key_part, value_part))

    start_grad = jnp.zeros(queries.shape, jnp.float32)
    query_grad, (key_parts, value_parts) = lax.scan(
        key_advance,
        start_grad,
        (split_blocks(key_all, block_rows), split_blocks(value_all, block_rows)),
    )
    return (query_grad, key_parts.reshape(key_all.shape), value_parts.reshape(value_all.shape))


def per_device(
    hidden_in,
    output_cotangent,
    adapter_index,
    mixing_weight,
    output_weight,
    expand_weight,
    contract_weight,
    first_gain,
    first_shift,
    second_gain,
    second_shift,
    mixing_down,
    mixing_up,
    output_down,
    output_up,
    expand_down,
    expand_up,
    contract_down,
    contract_up,
):
    seq_count, tok_count, model_width = hidden_in.shape
    local_heads = mixing_weight.shape[2] // HEAD_DIM
    score_scale = HEAD_DIM ** (-0.5)
    head_shape = (tok_count, seq_count, local_heads, HEAD_DIM)
    adapter_ids = jnp.arange(NADAPT, dtype=jnp.int32)
    onehot = (adapter_index == adapter_ids[None, :]).astype(jnp.float32)
    onehot_low = onehot.astype(jnp.bfloat16)
    mixing_down_sel = pick_rows(onehot_low, mixing_down)
    mixing_up_sel = pick_rows(onehot_low, mixing_up)
    output_down_sel = pick_rows(onehot_low, output_down)
    output_up_sel = pick_rows(onehot_low, output_up)
    expand_down_sel = pick_rows(onehot_low, expand_down)
    expand_up_sel = pick_rows(onehot_low, expand_up)
    contract_down_sel = pick_rows(onehot_low, contract_down)
    contract_up_sel = pick_rows(onehot_low, contract_up)
    mixing_full, output_full = (
        lax.all_gather(mixing_weight, ("dp", "ctx"), axis=0, tiled=True),
        lax.all_gather(output_weight, ("dp", "ctx"), axis=1, tiled=True),
    )
    expand_full, contract_full = (
        lax.all_gather(expand_weight, ("dp", "ctx"), axis=0, tiled=True),
        lax.all_gather(contract_weight, ("dp", "ctx"), axis=1, tiled=True),
    )
    mixing_rank = jnp.einsum(
        "std,srd->str", hidden_in, mixing_down_sel, preferred_element_type=jnp.float32
    ).astype(jnp.bfloat16)
    projected = jnp.einsum(
        "std,dcf->tscf", hidden_in, mixing_full, preferred_element_type=jnp.float32
    )
    projected = projected + jnp.einsum(
        "str,srcf->tscf", mixing_rank, mixing_up_sel, preferred_element_type=jnp.float32
    )
    projected = projected.astype(jnp.bfloat16)
    queries = projected[:, :, 0].reshape(head_shape)
    key_rows = projected[:, :, 1].reshape(head_shape)
    value_rows = projected[:, :, 2].reshape(head_shape)
    start_state = (
        jnp.full(head_shape[:3], -1e30, jnp.float32),
        jnp.zeros(head_shape[:3], jnp.float32),
        jnp.zeros(head_shape, jnp.float32),
    )
    running_max, running_sum, weighted = attend_fold(
        queries,
        score_scale,
        start_state,
        (
            lax.all_gather(key_rows, "ctx", axis=0, tiled=True),
            lax.all_gather(value_rows, "ctx", axis=0, tiled=True),
        ),
    )
    attended = weighted / running_sum[..., None]
    log_total = running_max + jnp.log(running_sum)
    context = attended.reshape(tok_count, seq_count, -1).astype(jnp.bfloat16)
    rows_all = seq_count * tok_count
    context = context.swapaxes(0, 1).reshape(rows_all, -1)
    gains = jnp.stack([first_gain, first_shift, second_gain, second_shift])
    hidden_rows = hidden_in.reshape(rows_all, model_width)
    picked = (
        output_down_sel,
        output_up_sel,
        expand_down_sel,
        expand_up_sel,
        contract_down_sel,
        contract_up_sel,
    )
    (
        out_rows,
        first_low,
        active_low,
        second_low,
        before_low,
        attn_low,
        context_grad,
        output_rank,
        expand_rank,
        contract_rank,
        contract_rank_grad,
        expand_rank_grad,
        output_rank_grad,
    ) = middle(
        context,
        hidden_rows,
        output_cotangent.reshape(rows_all, model_width),
        output_full,
        expand_full,
        contract_full,
        picked,
        gains,
        tok_count,
    )
    shared = lax.psum(jnp.concatenate([output_rank, contract_rank, expand_rank_grad], axis=1), "tensor")
    rank = output_rank.shape[1]
    output_rank, contract_rank, expand_rank_grad = (
        shared[:, :rank],
        shared[:, rank : 2 * rank],
        shared[:, 2 * rank :],
    )
    row_hot = jnp.repeat(onehot_low, tok_count, axis=0)

    def table_grad(ranks, values):
        wide = (row_hot[:, :, None] * ranks[:, None, :]).reshape(rows_all, -1)
        part = jnp.einsum("nk,nd->kd", wide, values, preferred_element_type=jnp.float32)
        return part.astype(jnp.bfloat16).reshape(NADAPT, rank, values.shape[1])

    grad_out = context_grad.reshape(seq_count, tok_count, -1).swapaxes(0, 1).reshape(head_shape)
    delta_rows = jnp.sum(grad_out.astype(jnp.float32) * attended, axis=-1)
    key_all, value_all = (
        lax.all_gather(key_rows, "ctx", axis=0, tiled=True),
        lax.all_gather(value_rows, "ctx", axis=0, tiled=True),
    )
    query_grad, key_parts, value_parts = key_sweep(
        queries, grad_out, log_total, delta_rows, key_all, value_all, score_scale
    )
    key_grad, value_grad = (
        lax.psum_scatter(
            key_parts.astype(jnp.bfloat16), "ctx", scatter_dimension=0, tiled=True
        ).astype(jnp.float32),
        lax.psum_scatter(
            value_parts.astype(jnp.bfloat16), "ctx", scatter_dimension=0, tiled=True
        ).astype(jnp.float32),
    )
    grad_stack = jnp.stack([query_grad, key_grad, value_grad], axis=2).astype(jnp.bfloat16)
    grad_stack = grad_stack.reshape(tok_count, seq_count, 3, -1)
    rank_part = jnp.einsum(
        "tscf,srcf->str", grad_stack, mixing_up_sel, preferred_element_type=jnp.float32
    ).astype(jnp.bfloat16)
    input_part = jnp.einsum(
        "tscf,dcf->std", grad_stack, mixing_full, preferred_element_type=jnp.float32
    )
    input_part = input_part + jnp.einsum(
        "str,srd->std", rank_part, mixing_down_sel, preferred_element_type=jnp.float32
    )
    input_back = lax.psum(input_part.astype(jnp.bfloat16), "tensor").astype(jnp.float32)
    mixing_rank_low = lax.psum(rank_part, "tensor")
    input_low = (
        attn_low.reshape(hidden_in.shape).astype(jnp.float32) + input_back
    ).astype(jnp.bfloat16)
    grad_rows = grad_stack.swapaxes(0, 1).reshape(rows_all, -1)
    parts = (
        table_grad(mixing_rank_low.reshape(rows_all, rank), hidden_rows),
        table_grad(mixing_rank.reshape(rows_all, rank), grad_rows).reshape(
            (NADAPT, rank) + grad_stack.shape[2:]
        ),
        table_grad(output_rank_grad, context),
        table_grad(output_rank, attn_low),
        table_grad(expand_rank_grad, first_low),
        table_grad(expand_rank, before_low),
        table_grad(contract_rank_grad, active_low),
        table_grad(contract_rank, second_low),
    )
    summed = tuple(lax.psum(part, ("dp", "ctx")).astype(jnp.float32) for part in parts)
    return (out_rows.reshape(hidden_in.shape), input_low) + summed


def solution(mesh):
    return jax.shard_map(
        per_device,
        mesh=mesh,
        in_specs=(
            P("dp", "ctx", None),
            P("dp", "ctx", None),
            P("dp", None),
            P(("dp", "ctx"), None, "tensor"),
            P("tensor", ("dp", "ctx")),
            P(("dp", "ctx"), "tensor"),
            P("tensor", ("dp", "ctx")),
            P(),
            P(),
            P(),
            P(),
            P(),
            P(None, None, None, "tensor"),
            P(None, None, "tensor"),
            P(),
            P(),
            P(None, None, "tensor"),
            P(None, None, "tensor"),
            P(),
        ),
        out_specs=(
            P("dp", "ctx", None),
            P("dp", "ctx", None),
            P(),
            P(None, None, None, "tensor"),
            P(None, None, "tensor"),
            P(),
            P(),
            P(None, None, "tensor"),
            P(None, None, "tensor"),
            P(),
        ),
        check_vma=False,
    )
```

time: 1290 us -> 1050 us (0.81)
  waiting for transfers between devices: 840 us -> 481 us
  Pallas kernels: 0 us -> 318 us
  matrix products: 251 us -> 108 us
  blocking collectives: 87.9 us -> 21.2 us
    psum x5 -> x2, waiting for transfers between devices: 588 us -> 193 us  [the longest x1 124 us: per_device(): lax.psum(jnp.concatenate([output_rank, contract_rank, expand_rank_grad],...]
    pallas_call x0 -> x1, Pallas kernels: none -> 318 us  [middle(): pl.pallas_call(functools.partial(middle_kernel, sizes), out_shape=(shape(...]
    dot_general x36 -> x10, matrix products: 170 us -> 27.8 us  [the longest x8 15.6 us: table_grad(): jnp.einsum('nk,nd->kd', wide, values, preferred_element_type=jnp.float32)]
    psum x4 -> x1, blocking collectives: 87.9 us -> 21.2 us  [per_device(): mixing_rank_low = lax.psum(rank_part, 'tensor')]
    reduce_scatter x1, waiting for transfers between devices: 18.8 us -> 44.5 us  [per_device(): lax.psum_scatter(key_parts.astype(jnp.bfloat16), 'ctx', scatter_dimension...]
    all_gather x1, waiting for transfers between devices: 40 us -> 57.7 us  [per_device(): lax.all_gather(contract_weight, ('dp', 'ctx'), axis=1, tiled=True)]
    unnamed x96 -> x85, local copies, waits for them, and re-layouts: 32.6 us -> 19.8 us
  transfers between devices with their start and end apart: 13 -> 10, of which waited for: 12 -> 9; matrix products, arithmetic and copies ran while one was open for 11% -> 8% of each run, Pallas kernels for 0% -> 0%
where the time goes in v1:
time: 1050 us
  waiting for transfers between devices  481 us (46%)
  Pallas kernels  318 us (30%)
  matrix products  108 us (10%)
  local copies, waits for them, and re-layouts  64.8 us (6%)
  other arithmetic  38.3 us (4%)
  blocking collectives  21.2 us (2%)
  between operations  14.9 us (1%)
    pallas_call x1, Pallas kernels, middle(): pl.pallas_call(functools.partial(middle_kernel, sizes), out_shape=(shape(...  318 us
    psum x1, waiting for transfers between devices, per_device(): lax.psum(jnp.concatenate([output_rank, contract_rank, expand_rank_grad],...  124 us
    psum x1, waiting for transfers between devices, per_device(): lax.psum(part, ('dp', 'ctx')).astype(jnp.float32)  69.5 us
    all_gather x1, waiting for transfers between devices, per_device(): lax.all_gather(contract_weight, ('dp', 'ctx'), axis=1, tiled=True)  57.7 us
    all_gather x1, waiting for transfers between devices, per_device(): lax.all_gather(expand_weight, ('dp', 'ctx'), axis=0, tiled=True)  48.3 us
    reduce_scatter x1, waiting for transfers between devices, per_device(): lax.psum_scatter(key_parts.astype(jnp.bfloat16), 'ctx', scatter_dimension...  44.5 us
    all_gather x1, waiting for transfers between devices, per_device(): lax.all_gather(mixing_weight, ('dp', 'ctx'), axis=0, tiled=True)  43.6 us
    reduce_scatter x1, waiting for transfers between devices, per_device(): lax.psum_scatter(value_parts.astype(jnp.bfloat16), 'ctx', scatter_dimensi...  39.3 us
  transfers between devices with their start and end apart: 10, of which 9 were waited for; matrix products, arithmetic and copies ran while one was open for 8% of the time, Pallas kernels for 0%

profile of v1, /device:TPU:0, one launch (start us, length us, event | category | flops | bytes accessed | tf_op | source)
XLA Modules:
  0.0 1047.4 jit_solution(8259517636955667981)
XLA Ops:
  7.2 2.3 copy.112
  12.9 3.4 convolution_convert_fusion.10
  16.3 43.6 %all-gather.7.cloned.1.call-done = bf16[2048,3,512]{0,2,1:T(8,128)(2,1)} async-done(((bf16[256,3,512]{0,2,1:T(8,128)(2,1)}), bf16[2048,3,512]{0,2,1:T(8,128)(2,1)}) %all-gather.7.cloned.1.call-update) | async-done | bytes 6291472 | tf_op jit(solution)/shard_map/all_gather | solution.py:556
  59.9 10.1 fusion.46
  72.2 2.3 copy.117
  80.6 1.5 fusion.60
  89.3 19.9 %all-gather.9.cloned.1.call-done = bf16[1024,4,4,128]{3,0,2,1:T(8,128)(2,1)} async-done(((bf16[256,4,4,128]{3,0,2,1:T(8,128)(2,1)}), bf16[1024,4,4,128]{3,0,2,1:T(8,128)(2,1)}) %all-gather.9.cloned.1.call-update) | async-done | bytes 4194320 | tf_op jit(solution)/shard_map/all_gather | solution.py:586
  109.2 4.7 copy.119
  113.8 32.0 %all-gather.11.cloned.1.call-done = bf16[1024,4,4,128]{3,0,2,1:T(8,128)(2,1)} async-done(((bf16[256,4,4,128]{3,0,2,1:T(8,128)(2,1)}), bf16[1024,4,4,128]{3,0,2,1:T(8,128)(2,1)}) %all-gather.11.cloned.1.call-update) | async-done | bytes 4194320 | tf_op jit(solution)/shard_map/all_gather | solution.py:587
  145.8 34.7 %while.30 = (s32[]{:T(128)}, f32[256,4,4]{0,2,1:T(4,128)S(1)}, f32[256,4,4]{0,2,1:T(4,128)S(1)}, f32[256,4,4,128]{0,3,2,1:T(8,128)}, bf16[2,512,4,4,128]{4,1,3,2...) while((s32[]{:T(128)}, f32[256,4,4]{0,2,1:T(4,128)S(1)}, ...), condition=%wide.region_3.4_spmd.clone, body=%wide.region_0.3_spmd.clone.sunk | while | flops 1092112384 | bytes 68419736 | solution.py:468
  145.8 6.2 bitcast_reduce_fusion.2
  152.0 5.1 fusion.137
  158.1 4.9 bitcast_add_fusion.6
  163.0 6.2 bitcast_reduce_fusion.2
  169.2 4.9 fusion.137
  175.0 5.5 bitcast_add_fusion.6
  180.5 1.8 fusion.53
  183.6 48.3 %all-gather.15.cloned.1.call-done.w_exp = bf16[2048,2048]{1,0:T(8,128)(2,1)} async-done(((bf16[256,2048]{1,0:T(8,128)(2,1)}), bf16[2048,2048]{1,0:T(8,128)(2,1)}) %all-gather.15.cloned.1.call-update) | async-done | bytes 8388624 | tf_op jit(solution)/shard_map/all_gather | solution.py:560
  232.0 57.7 %all-gather.17.cloned.1.call-done.w_con = bf16[2048,2048]{1,0:T(8,128)(2,1)} async-done(((bf16[2048,256]{1,0:T(8,128)(2,1)}), bf16[2048,2048]{1,0:T(8,128)(2,1)}) %all-gather.17.cloned.1.call-update) | async-done | bytes 8388624 | tf_op jit(solution)/shard_map/all_gather | solution.py:561
  289.7 318.5 %shard_map.258 = (bf16[1024,2048]{1,0:T(8,128)(2,1)}, bf16[1024,2048]{1,0:T(8,128)(2,1)}, bf16[1024,2048]{1,0:T(8,128)(2,1)}, bf16[1024,2048]{1,0:T(8,128)(2,1)}...) custom-call(bf16[1024,512]{1,0:T(8,128)(2,1)} %bitcast.266, ...), custom_call_target="tpu_custom_call" | custom-call | flops 38654705664 | bytes 33554432 | tf_op jit(solution)/shard_map/pallas_call | solution.py:391
  609.7 2.3 multiply_reduce_fusion
  612.0 1.6 copy.139
  613.7 46.9 %while.31 = (s32[]{:T(128)}, f32[256,4,4,128]{0,3,2,1:T(8,128)}, bf16[2,512,4,4,128]{4,1,0,3,2:T(8,128)(2,1)}, bf16[2,512,4,4,128]{4,1,0,3,2:T(8,128)(2,1)}, bf1...) while((s32[]{:T(128)}, f32[256,4,4,128]{0,3,2,1:T(8,128)}, ...), condition=%wide.region_6.7_spmd.clone, body=%wide.region_5.6_spmd.clone.sunk | while | flops 2703753216 | bytes 186696048 | solution.py:511
  613.7 3.0 fusion.149
  616.7 3.3 copy-done.3
  620.0 3.4 fusion.150
  623.4 5.2 bitcast_add_fusion.7
  628.7 2.6 bitcast_dynamic-update-slice_fusion.4
  631.3 1.8 copy-done.14
  633.0 1.8 bitcast_dynamic-update-slice_fusion.5
  634.9 2.0 copy-done.15
  636.8 3.0 fusion.149
  639.8 3.3 copy-done.3
  643.1 3.4 fusion.150
  646.6 5.8 bitcast_add_fusion.7
  652.4 2.6 bitcast_dynamic-update-slice_fusion.4
  655.0 1.8 copy-done.14
  656.8 1.8 bitcast_dynamic-update-slice_fusion.5
  658.6 2.0 copy-done.15
  665.7 39.3 %reduce-scatter.5.cloned.1.call-done = bf16[256,4,4,128]{3,0,2,1:T(8,128)(2,1)} async-done(((bf16[1024,4,4,128]{3,0,2,1:T(8,128)(2,1)}), bf16[256,4,4,128]{3,0,2,1:T(8,128)(2,1)}) %reduce-scatter.5.cloned.1.call-update) | async-done | bytes 1048592 | tf_op jit(solution)/shard_map/reduce_scatter | solution.py:657
  705.0 2.0 copy.144
  708.3 44.5 %reduce-scatter.3.cloned.1.call-done = bf16[256,4,4,128]{3,0,2,1:T(8,128)(2,1)} async-done(((bf16[1024,4,4,128]{3,0,2,1:T(8,128)(2,1)}), bf16[256,4,4,128]{3,0,2,1:T(8,128)(2,1)}) %reduce-scatter.3.cloned.1.call-update) | async-done | bytes 1048592 | tf_op jit(solution)/shard_map/reduce_scatter | solution.py:654
  752.8 2.0 copy.142
  756.1 2.6 fusion.52
  758.7 8.8 fusion.49
  767.5 3.4 fusion.44
  772.2 3.2 fusion.89
  775.5 6.0 copy.150
  781.5 4.3 copy.177
  785.8 21.2 %psum.78 = bf16[1024,16]{0,1:T(8,128)(2,1)S(1)} all-reduce(bf16[1024,16]{0,1:T(8,128)(2,1)S(1)} %bitcast.293), channel_id=1, replica_groups=mesh['dp'=2,'ctx'=4,'tensor'=4] {'tensor'}, use_global_device_ids=true, to_apply=%region_10.11 | all-reduce | flops 16384 | bytes 65536 | tf_op jit(solution)/shard_map/psum | solution.py:673
  807.0 123.5 %all-reduce.7.cloned.1.call-done = (bf16[1024,48]{0,1:T(8,128)(2,1)}, bf16[4,256,2048]{2,1,0:T(8,128)(2,1)}) async-done(((bf16[1024,48]{0,1:T(8,128)(2,1)}, bf16[4,256,2048]{2,1,0:T(8,128)(2,1)}), (bf16[1024,48]{0,1:T(8,128)(2,1)}, bf16[4,256,2048]{2,1,0:T(8,128)(2,1)})) %all-reduce.7.cloned.1.call-update) | async-done | bytes 4292624 | tf_op jit(solution)/shard_map/psum | solution.py:630
  931.7 3.1 convolution_convert_fusion.5
  935.9 3.8 convolution_convert_fusion.6
  942.2 1.5 convolution_convert_fusion.3
  943.8 1.5 convolution_convert_fusion.2
  945.3 1.5 convolution_convert_fusion.1
  946.8 1.5 convolution_convert_fusion
  948.4 7.8 fusion.45
  956.2 69.5 %all-reduce.5.cloned.1.call-done = (bf16[8,16,3,512]{3,2,1,0:T(4,128)(2,1)}, bf16[8,16,2048]{2,1,0:T(8,128)(2,1)}, bf16[8,16,512]{2,1,0:T(8,128)(2,1)}, bf16[8,1...) async-done(((bf16[8,16,3,512]{3,2,1,0:T(4,128)(2,1)}, ...) | async-done | bytes 3670032 | tf_op jit(solution)/shard_map/psum | solution.py:690
  1025.7 2.2 convert_element_type.165
  1027.9 2.1 copy.157
  1030.0 1.8 convert_element_type.170
  1031.8 2.1 convert_element_type.172
  1038.2 2.0 copy.251
  (184 shorter events, 41.0 us)
Async XLA Ops:
  7.2 3.9 copy-start
  7.2 52.7 %all-gather.7.cloned.1.call-start = ((), (), s32[]{:S(2)}) async-start(), calls=%async_computation.2 | async-start | bytes 7077888 | tf_op jit(solution)/shard_map/all_gather | solution.py:556
  9.6 99.6 %all-gather.9.cloned.1.call-start = ((), (), s32[]{:S(2)}) async-start(), calls=%async_computation.3 | async-start | bytes 5242880 | tf_op jit(solution)/shard_map/all_gather | solution.py:586
  11.0 58.9 %copy-start.21 = (bf16[4,16,3,512]{3,0,2,1:T(4,128)(2,1)}, bf16[4,16,3,512]{3,0,2,1:T(4,128)(2,1)S(1)}, u32[]{:S(2)}) copy-start(bf16[4,16,3,512]{3,0,2,1:T(4,128)(2,1)S(1)} %convolution_convert_fusion.8) | copy-start | bytes 589828
  16.3 53.7 %copy-start.30 = (bf16[4,16,256]{2,1,0:T(8,128)(2,1)}, bf16[4,16,256]{2,1,0:T(8,128)(2,1)S(1)}, u32[]{:S(2)}) copy-start(bf16[4,16,256]{2,1,0:T(8,128)(2,1)S(1)} %convolution_convert_fusion.10) | copy-start | bytes 98308
  72.2 6.2 copy-start.38
  72.2 6.2 copy-start.39
  72.2 7.0 copy-start.27
  74.5 71.3 %all-gather.11.cloned.1.call-start = ((), (), s32[]{:S(2)}) async-start(), calls=%async_computation.4 | async-start | bytes 5242880 | tf_op jit(solution)/shard_map/all_gather | solution.py:587
  75.9 7.1 copy-start.28
  75.9 8.4 copy-start.29
  75.9 107.7 %all-gather.13.cloned.1.call-start = ((), (), s32[]{:S(2)}) async-start(), calls=%async_computation.5 | async-start | bytes 2359296 | tf_op jit(solution)/shard_map/all_gather | solution.py:557
  76.5 155.5 %all-gather.15.cloned.1.call-start = ((), (), s32[]{:S(2)}) async-start(), calls=%async_computation.6 | async-start | bytes 9437184 | tf_op jit(solution)/shard_map/all_gather | solution.py:560
  77.1 10.9 %copy-start.41 = (f32[2048]{0:T(1024)S(1)}, f32[2048]{0:T(1024)}, u32[]{:S(2)}) copy-start(f32[2048]{0:T(1024)} %param.33) | copy-start | bytes 24580
  77.1 10.9 %copy-start.42 = (f32[2048]{0:T(1024)S(1)}, f32[2048]{0:T(1024)}, u32[]{:S(2)}) copy-start(f32[2048]{0:T(1024)} %param.32) | copy-start | bytes 24580
  77.1 10.9 %copy-start.43 = (f32[2048]{0:T(1024)S(1)}, f32[2048]{0:T(1024)}, u32[]{:S(2)}) copy-start(f32[2048]{0:T(1024)} %param.31) | copy-start | bytes 24580
  77.1 10.9 %copy-start.44 = (f32[2048]{0:T(1024)S(1)}, f32[2048]{0:T(1024)}, u32[]{:S(2)}) copy-start(f32[2048]{0:T(1024)} %param.30) | copy-start | bytes 24580
  77.2 212.5 %all-gather.17.cloned.1.call-start = ((), (), s32[]{:S(2)}) async-start(), calls=%async_computation.7 | async-start | bytes 9437184 | tf_op jit(solution)/shard_map/all_gather | solution.py:561
  77.7 627.3 %reduce-scatter.5.cloned.1.call-start = ((), (), s32[]{:S(2)}) async-start(), calls=%async_computation.9 | async-start | bytes 5242880 | tf_op jit(solution)/shard_map/reduce_scatter | solution.py:657
  152.0 6.0 copy-start.2
  169.2 5.8 copy-start.2
  609.7 2.3 copy-start.8
  613.7 6.3 copy-start.5
  616.7 3.3 copy-start.3
  623.4 5.2 copy-start.4
  623.4 7.8 slice-start
  628.7 2.6 slice-start.1
  628.7 4.3 copy-start.14
  634.9 2.0 copy-start.15
  636.8 6.3 copy-start.5
  639.8 3.3 copy-start.3
  646.6 5.8 copy-start.4
  646.6 8.4 slice-start
  652.4 2.6 slice-start.1
  652.4 4.3 copy-start.14
  658.6 2.0 copy-start.15
  660.6 1.0 copy-start.37
  660.6 1.2 copy-start.36
  660.6 1.3 copy-start.35
  660.6 1.8 copy-start.6
  660.6 92.2 %reduce-scatter.3.cloned.1.call-start = ((), (), s32[]{:S(2)}) async-start(), calls=%async_computation.8 | async-start | bytes 5242880 | tf_op jit(solution)/shard_map/reduce_scatter | solution.py:654
  661.4 269.2 %all-reduce.7.cloned.1.call-start = ((), (), s32[]{:S(2)}) async-start(), calls=%async_computation.11 | async-start | bytes 8585216 | tf_op jit(solution)/shard_map/psum | solution.py:630
  665.7 90.4 %copy-start.22 = (bf16[4,16,3,512]{3,0,2,1:T(4,128)(2,1)S(1)}, bf16[4,16,3,512]{3,0,2,1:T(4,128)(2,1)}, u32[]{:S(2)}) copy-start(bf16[4,16,3,512]{3,0,2,1:T(4,128)(2,1)} %copy-done.21) | copy-start | bytes 589828
  756.1 2.6 copy-start.17
  756.1 2.6 copy-start.18
  758.7 8.8 copy-start.20
  770.9 0.8 copy-start.31
  770.9 0.8 copy-start.40
  770.9 1.0 copy-start.34
  770.9 1.1 copy-start.33
  770.9 1.2 copy-start.32
  770.9 254.7 %all-reduce.5.cloned.1.call-start = ((), (), s32[]{:S(2)}) async-start(), calls=%async_computation.10 | async-start | bytes 7602176 | tf_op jit(solution)/shard_map/psum | solution.py:690
  931.6 8.1 copy-start.16
  935.9 4.8 copy-start.7
  939.7 2.5 copy-start.12
  940.7 3.1 copy-start.11
  942.2 3.1 copy-start.10
  943.8 3.1 copy-start.9
  1025.7 8.3 copy-start.26
  1025.7 9.3 copy-start.25
  1025.7 10.4 copy-start.24
  1027.9 9.2 copy-start.23
  1030.0 8.2 copy-start.13
  1037.2 3.1 copy-start.1
  (1 other events, 0.7 us)
Sparse Core Ops, SparseCore 0:
  10.5 49.3 all-gather.6
  74.7 34.4 all-gather.8
  111.3 34.4 all-gather.10
  147.6 28.1 all-gather.12
  177.5 54.3 all-gather.14
  233.7 55.9 all-gather.16
  660.7 44.2 reduce-scatter.4
  708.3 44.4 reduce-scatter.2
  771.1 159.4 all-reduce.6
  948.5 77.1 all-reduce.4

commit v2 on v1

v2 whole, which is shorter than its diff:
```python
import functools
import math

import jax
import jax.numpy as jnp
from jax import lax
from jax.experimental import pallas as pl
from jax.experimental.pallas import tpu as pltpu
from jax.sharding import PartitionSpec as P

HEAD_DIM = 128
NADAPT = 8
CHUNK_ROWS = 128
LAST_ROWS = 64
VMEM_BYTES = 62 * 2**20
VMEM_LAST = 48 * 2**20


BF = jnp.bfloat16
F32 = jnp.float32
MESH_IDS = pl.DeviceIdType.MESH
RANK_ROWS = 16
GELU_C = 0.7978845608028654
GELU_A = 0.044715


def dot_nn(a, b):
    return lax.dot_general(a, b, (((1,), (0,)), ((), ())), preferred_element_type=F32)


def dot_nt(a, b):
    return lax.dot_general(a, b, (((1,), (1,)), ((), ())), preferred_element_type=F32)


def dot_tn(a, b):
    return lax.dot_general(a, b, (((0,), (0,)), ((), ())), preferred_element_type=F32)


def tile(index, size):
    return pl.ds(pl.multiple_of(index * size, size), size)


def chain(
    ranks, half, block, me, acc, red_up, red_down, red_send, red_recv, cast_send, cast_recv, job_of
):
    def comm(tick, way):
        upward = way == 0
        place = me if upward else ranks - 1 - me
        ahead = me + 1 if upward else me - 1
        behind = me - 1 if upward else me + 1
        red = red_up if upward else red_down
        part = pl.ds(way * half, half)

        def red_copy(c):
            return pltpu.make_async_remote_copy(
                src_ref=red.at[c],
                dst_ref=red.at[c],
                send_sem=red_send.at[way, c],
                recv_sem=red_recv.at[way, c],
                device_id={"tensor": ahead},
                device_id_type=MESH_IDS,
            )

        def cast_copy(c):
            return pltpu.make_async_remote_copy(
                src_ref=acc.at[c, part],
                dst_ref=acc.at[c, part],
                send_sem=cast_send.at[way, c],
                recv_sem=cast_recv.at[way, c],
                device_id={"tensor": behind},
                device_id_type=MESH_IDS,
            )

        old_red, c_old = job_of(tick - 2 - place)

        @pl.when(old_red & (place < ranks - 1))
        def _():
            red_copy(c_old).wait_send()

        old_cast, c_cast = job_of(tick - 2 * ranks + place)

        @pl.when(old_cast & (place > 0))
        def _():
            cast_copy(c_cast).wait_send()

        now_red, c = job_of(tick - 1 - place)

        @pl.when(now_red & (place == 0))
        def _():
            red[c] = acc[c, part, :]

        @pl.when(now_red & (place > 0))
        def _():
            red_copy(c).wait_recv()

        @pl.when(now_red & (place > 0) & (place < ranks - 1))
        def _():
            @pl.loop(0, half // block)
            def _(i):
                rs = tile(i, block)
                own = acc[c, pl.ds(pl.multiple_of(way * half + i * block, block), block), :]
                red[c, rs, :] = (red[c, rs, :].astype(F32) + own.astype(F32)).astype(BF)

        @pl.when(now_red & (place < ranks - 1))
        def _():
            red_copy(c).start()

        @pl.when(now_red & (place == ranks - 1))
        def _():
            @pl.loop(0, half // block)
            def _(i):
                rs = tile(i, block)
                own_rs = pl.ds(pl.multiple_of(way * half + i * block, block), block)
                acc[c, own_rs, :] = (
                    red[c, rs, :].astype(F32) + acc[c, own_rs, :].astype(F32)
                ).astype(BF)

            cast_copy(c).start()

        now_cast, cc = job_of(tick - (2 * ranks - 1 - place))

        @pl.when(now_cast & (place < ranks - 1))
        def _():
            cast_copy(cc).wait_recv()

        @pl.when(now_cast & (place > 0) & (place < ranks - 1))
        def _():
            cast_copy(cc).start()
    return comm


def middle_kernel(
    sizes,
    local_qkv,
    hidden,
    cotangent,
    shard_out,
    shard_exp,
    shard_con,
    od,
    ou,
    ed,
    eu,
    cd,
    cu,
    gains,
    hidden_out,
    first_low,
    active,
    second_low,
    before_grad,
    attn_low,
    context_grad,
    out_rank,
    exp_rank,
    con_rank,
    con_rank_grad,
    exp_rank_grad,
    out_rank_grad,
    context,
    unit_qkv,
    unit_out,
    w_out,
    w_exp,
    w_con,
    acc,
    red_up,
    red_down,
    normed,
    spreads,
    slope,
    second,
    stage_d,
    stage_f,
    rows_in,
    rank_buf,
    in_sem,
    out_sem,
    red_send,
    red_recv,
    cast_send,
    cast_recv,
    peer_send,
    peer_recv,
    twin_send,
    twin_recv,
    own_sem,
    qkv_send,
    qkv_recv,
    ctx_send,
    ctx_recv,
    unit_sem,
):
    ranks, dps, ctxs, chunks, rows, per_seq, period = sizes
    half = rows // 2
    width = hidden.shape[1]
    hidden_units = w_exp.shape[1]
    heads = w_out.shape[0]
    block = min(16, half)
    tile_f = math.gcd(hidden_units, 256)
    tile_d = math.gcd(width, 256)
    tile_h = math.gcd(heads, 256)
    me = lax.axis_index("tensor")
    dp = lax.axis_index("dp")
    ctx = lax.axis_index("ctx")
    pairs = ctxs // 2
    core = ctx % 2
    chips = dps * pairs
    chip = dp * pairs + ctx // 2
    twin = {"ctx": ctx + 1 - 2 * core}
    lead = per_seq
    units, seq_all = unit_qkv.shape[0], unit_qkv.shape[2]
    tok = seq_all // ctxs
    local_heads = local_qkv.shape[1]

    def chip_block(step, which):
        row, column = step // pairs, step % pairs
        from_dp = (dp + dps - row) % dps
        from_chip = (ctx // 2 + pairs - column) % pairs
        return from_dp * ctxs + from_chip * 2 + which

    enter(me, ranks, [{"ctx": (ctx + d) % ctxs} for d in range(1, ctxs)]
          + [{"dp": (dp + e) % dps, "ctx": 2 * f + core}
             for e in range(1, dps) for f in range(pairs)])

    shards = (shard_out, shard_exp, shard_con)
    fulls = (w_out, w_exp, w_con)

    def block_of(w, index):
        if w == 1:
            return fulls[w].at[tile(index, shards[w].shape[0])]
        return fulls[w].at[:, tile(index, shards[w].shape[1])]

    def peer_copy(w, step):
        row, column = step // pairs, step % pairs
        block = block_of(w, chip_block(column, core))
        if row:
            target = {"dp": (dp + row) % dps}
        else:
            target = {"ctx": (ctx + 2 * column) % ctxs}
        own = block_of(w, chip_block(0, core))
        return pltpu.make_async_remote_copy(
            src_ref=block if row and column else shards[w],
            dst_ref=block if row else own,
            send_sem=peer_send.at[w, step],
            recv_sem=peer_recv.at[w, step],
            device_id=target,
            device_id_type=MESH_IDS,
        )

    def peer_arrival(w, step):
        row = step // pairs
        if row:
            target = {"dp": (dp + row) % dps}
        else:
            target = {"ctx": (ctx + 2 * step) % ctxs}
        return pltpu.make_async_remote_copy(
            src_ref=shards[w],
            dst_ref=block_of(w, chip_block(step, core)),
            send_sem=peer_send.at[w, step],
            recv_sem=peer_recv.at[w, step],
            device_id=target,
            device_id_type=MESH_IDS,
        )

    def twin_copy(w, step):
        block = block_of(w, chip_block(step, core))
        return pltpu.make_async_remote_copy(
            src_ref=shards[w] if step == 0 else block,
            dst_ref=block,
            send_sem=twin_send.at[w, step],
            recv_sem=twin_recv.at[w, step],
            device_id=twin,
            device_id_type=MESH_IDS,
        )

    def twin_arrival(w, step):
        block = block_of(w, chip_block(step, 1 - core))
        return pltpu.make_async_remote_copy(
            src_ref=block,
            dst_ref=block,
            send_sem=twin_send.at[w, step],
            recv_sem=twin_recv.at[w, step],
            device_id=twin,
            device_id_type=MESH_IDS,
        )

    def own_copy(w):
        return pltpu.make_async_copy(shards[w], block_of(w, chip_block(0, core)), own_sem.at[w])

    def weight_start(w):
        for step in list(range(pairs, chips, pairs)) + list(range(1, pairs)):
            peer_copy(w, step).start()
        twin_copy(w, 0).start()
        own_copy(w).start()

    def weight_relay(w):
        for step in range(1, pairs):
            peer_arrival(w, step).wait_recv()
            twin_copy(w, step).start()
            for row in range(1, dps):
                peer_copy(w, row * pairs + step).start()

    def weight_forward(w):
        for step in range(pairs, chips):
            peer_arrival(w, step).wait_recv()
            twin_copy(w, step).start()

    def weight_finish(w):
        own_copy(w).wait()
        for step in range(chips):
            twin_arrival(w, step).wait_recv()

    def weight_sent(w):
        for step in range(1, chips):
            peer_copy(w, step).wait_send()
        for step in range(chips):
            twin_copy(w, step).wait_send()

    def unit_place(device, u):
        return (device // local_heads) * units + u, device % local_heads

    def qkv_copy(u, step):
        peer = (ctx + step) % ctxs
        s, h = unit_place(peer, u)
        return pltpu.make_async_remote_copy(
            src_ref=local_qkv.at[s, h],
            dst_ref=unit_qkv.at[u, :, tile(ctx, tok)],
            send_sem=qkv_send.at[u, step],
            recv_sem=qkv_recv.at[u, step],
            device_id={"ctx": peer},
            device_id_type=MESH_IDS,
        )

    def qkv_arrival(u, step):
        return pltpu.make_async_remote_copy(
            src_ref=local_qkv.at[0, 0],
            dst_ref=unit_qkv.at[u, :, tile((ctx + ctxs - step) % ctxs, tok)],
            send_sem=qkv_send.at[u, step],
            recv_sem=qkv_recv.at[u, step],
            device_id={"ctx": (ctx + step) % ctxs},
            device_id_type=MESH_IDS,
        )

    def qkv_own(u):
        s, h = unit_place(ctx, u)
        return pltpu.make_async_copy(
            local_qkv.at[s, h], unit_qkv.at[u, :, tile(ctx, tok)], unit_sem.at[0, u]
        )

    def context_place(device, u):
        s, h = unit_place(device, u)
        return context.at[tile(s, tok), tile(h, HEAD_DIM)]

    def context_copy(u, step):
        peer = (ctx + step) % ctxs
        return pltpu.make_async_remote_copy(
            src_ref=unit_out.at[u, tile(peer, tok)],
            dst_ref=context_place(ctx, u),
            send_sem=ctx_send.at[u, step],
            recv_sem=ctx_recv.at[u, step],
            device_id={"ctx": peer},
            device_id_type=MESH_IDS,
        )

    def context_arrival(u, step):
        return pltpu.make_async_remote_copy(
            src_ref=unit_out.at[u, tile(ctx, tok)],
            dst_ref=context_place((ctx + ctxs - step) % ctxs, u),
            send_sem=ctx_send.at[u, step],
            recv_sem=ctx_recv.at[u, step],
            device_id={"ctx": (ctx + step) % ctxs},
            device_id_type=MESH_IDS,
        )

    def context_own(u):
        return pltpu.make_async_copy(
            unit_out.at[u, tile(ctx, tok)], context_place(ctx, u), unit_sem.at[1, u]
        )

    def attend(u):
        qkv_own(u).wait()
        for step in range(1, ctxs):
            qkv_arrival(u, step).wait_recv()
        part = math.gcd(seq_all, 256)

        @pl.loop(0, seq_all // part)
        def _(i):
            rs = tile(i, part)
            scores = dot_nt(unit_qkv[u, 0, rs, :], unit_qkv[u, 1]) * (HEAD_DIM ** (-0.5))
            largest = jnp.max(scores, axis=-1, keepdims=True)
            raised = jnp.exp(scores - largest)
            total = jnp.sum(raised, axis=-1, keepdims=True)
            mixed = dot_nn(raised.astype(BF), unit_qkv[u, 2])
            unit_out[u, rs, :] = (mixed / total).astype(BF)

        for step in range(1, ctxs):
            context_copy(u, step).start()
        context_own(u).start()

    def context_ready(u):
        context_own(u).wait()
        for step in range(1, ctxs):
            context_arrival(u, step).wait_recv()

    weight_start(0)
    for u in range(units):
        qkv_own(u).start()
        for step in range(1, ctxs):
            qkv_copy(u, step).start()
    weight_start(1)
    weight_start(2)
    weight_relay(0)

    def job_of(number, rounds):
        safe = jnp.maximum(number, 0)
        chunk = safe % period
        valid = (number >= 0) & (chunk < chunks) & (safe < rounds * period)
        return valid, jnp.minimum(chunk, chunks - 1)

    comm = chain(
        ranks,
        half,
        block,
        me,
        acc,
        red_up,
        red_down,
        red_send,
        red_recv,
        cast_send,
        cast_recv,
        lambda number: job_of(number, 3),
    )

    def rows_of(c):
        return tile(c, rows)

    def bring(source, c):
        return pltpu.make_async_copy(source.at[rows_of(c)], rows_in, in_sem)

    def keep(index, source, target, c):
        return pltpu.make_async_copy(source, target.at[rows_of(c)], out_sem.at[index])

    def mean(values):
        return jnp.sum(values, axis=-1, keepdims=True) * (1.0 / width)

    def attend_part(c, s):
        mine = context[rows_of(c), :]
        low = dot_nt(mine, od[s]).astype(BF)
        out_rank[rows_of(c), :] = low

        @pl.loop(0, width // tile_d)
        def _(i):
            cs = tile(i, tile_d)
            acc[c, :, cs] = (dot_nn(mine, w_out[:, cs]) + dot_nn(low, ou[s, :, cs])).astype(BF)

    def forward_first(c, s):
        bring(hidden, c).wait()

        @pl.loop(0, rows // block)
        def _(i):
            rs = tile(i, block)
            total = rows_in[rs, :].astype(F32) + acc[c, rs, :].astype(F32)
            centred = total - mean(total)
            spread = lax.rsqrt(mean(centred * centred) + 1e-06)
            n = centred * spread
            normed[c, rs, :] = n.astype(BF)
            spreads[c, rs, :] = jnp.broadcast_to(spread, (block, 128))
            stage_d[rs, :] = (n * gains[0:1, :] + gains[1:2, :]).astype(BF)

        low = dot_nt(stage_d[...], ed[s]).astype(BF)
        exp_rank[rows_of(c), :] = low
        rank_buf[...] = low

        @pl.loop(0, hidden_units // tile_f)
        def _(i):
            cs = tile(i, tile_f)
            b = dot_nn(stage_d[...], w_exp[:, cs]) + dot_nn(rank_buf[...], eu[s, :, cs])
            square = b * b
            t = jnp.tanh(GELU_C * b * (1.0 + GELU_A * square))
            upper = 0.5 * (1.0 + t)
            stage_f[:, cs] = (b * upper).astype(BF)
            slope[c, :, cs] = (
                upper
                + (0.5 * GELU_C) * b * (1.0 - t * t) * (1.0 + (3.0 * GELU_A) * square)
            ).astype(BF)

    def forward_second(c, s):
        low = dot_nt(stage_f[...], cd[s]).astype(BF)
        con_rank[rows_of(c), :] = low
        rank_buf[...] = low

        @pl.loop(0, width // tile_d)
        def _(i):
            cs = tile(i, tile_d)
            acc[c, :, cs] = (
                dot_nn(stage_f[...], w_con[:, cs]) + dot_nn(rank_buf[...], cu[s, :, cs])
            ).astype(BF)

        keep(0, stage_d, first_low, c).start()
        keep(1, stage_f, active, c).start()

    def back_first(c, s):
        bring(cotangent, c).wait()

        @pl.loop(0, rows // block)
        def _(i):
            rs = tile(i, block)
            first = normed[c, rs, :].astype(F32) * gains[0:1, :] + gains[1:2, :]
            total = first + acc[c, rs, :].astype(F32)
            centred = total - mean(total)
            spread = lax.rsqrt(mean(centred * centred) + 1e-06)
            n = centred * spread
            stage_d[rs, :] = (n * gains[2:3, :] + gains[3:4, :]).astype(BF)
            g = rows_in[rs, :].astype(F32) * gains[2:3, :]
            second[c, rs, :] = (spread * (g - mean(g) - n * mean(g * n))).astype(BF)

        low = dot_nt(second[c], cu[s]).astype(BF)
        con_rank_grad[rows_of(c), :] = low
        rank_buf[...] = low

        @pl.loop(0, hidden_units // tile_f)
        def _(i):
            cs = tile(i, tile_f)
            da = dot_nt(second[c], w_con[cs, :]) + dot_nn(rank_buf[...], cd[s, :, cs])
            stage_f[:, cs] = (da * slope[c, :, cs].astype(F32)).astype(BF)

    def back_second(c, s):
        low = dot_nt(stage_f[...], eu[s]).astype(BF)
        exp_rank_grad[rows_of(c), :] = low
        rank_buf[...] = low

        @pl.loop(0, width // tile_d)
        def _(i):
            cs = tile(i, tile_d)
            acc[c, :, cs] = (
                dot_nt(stage_f[...], w_exp[cs, :]) + dot_nn(rank_buf[...], ed[s, :, cs])
            ).astype(BF)

        keep(0, stage_d, hidden_out, c).start()
        keep(1, stage_f, before_grad, c).start()
        keep(2, second.at[c], second_low, c).start()

    def last_first(c, s):
        @pl.loop(0, rows // block)
        def _(i):
            rs = tile(i, block)
            n = normed[c, rs, :].astype(F32)
            g = (second[c, rs, :].astype(F32) + acc[c, rs, :].astype(F32)) * gains[0:1, :]
            spread = spreads[c, rs, 0:1]
            stage_d[rs, :] = (spread * (g - mean(g) - n * mean(g * n))).astype(BF)

    def last_second(c, s):
        low = dot_nt(stage_d[...], ou[s]).astype(BF)
        out_rank_grad[rows_of(c), :] = low
        rank_buf[...] = low

        @pl.loop(0, heads // tile_h)
        def _(i):
            cs = tile(i, tile_h)
            context_grad[rows_of(c), cs] = (
                dot_nt(stage_d[...], w_out[cs, :]) + dot_nn(rank_buf[...], od[s, :, cs])
            ).astype(BF)

        keep(0, stage_d, attn_low, c).start()

    @pl.loop(0, lead + 3 * period + chunks)
    def _(now):
        tick = now - lead
        stage = jnp.maximum(tick, 0) // period
        valid, c = job_of(tick, 4)
        s = c // per_seq
        last_valid, last_c = job_of(tick - 1, 4)
        last_stage = jnp.maximum(tick - 1, 0) // period

        comm(tick, 0)

        @pl.when(last_valid & (last_stage >= 1))
        def _():
            keep(0, stage_d, first_low, last_c).wait()

        @pl.when(last_valid & (last_stage >= 1) & (last_stage <= 2))
        def _():
            keep(1, stage_f, active, last_c).wait()

        @pl.when(last_valid & (last_stage == 2))
        def _():
            keep(2, second.at[last_c], second_low, last_c).wait()

        pl.when(now == 1)(lambda: weight_forward(0))

        @pl.when(now == lead + period - 4)
        def _():
            weight_relay(1)
            weight_relay(2)

        pl.when(now == lead + period - 1)(lambda: weight_forward(1))

        @pl.when(now == lead + period)
        def _():
            weight_forward(2)
            weight_finish(1)
            weight_finish(2)

        pl.when((now % per_seq == 0) & (now < units * per_seq))(lambda: attend(now // per_seq))
        pl.when(now == lead)(lambda: weight_finish(0))
        pl.when((tick >= 0) & (tick % per_seq == 0) & (tick < units * per_seq))(
            lambda: context_ready(s)
        )

        pl.when(valid & (stage == 1))(lambda: forward_first(c, s))
        pl.when(valid & (stage == 2))(lambda: back_first(c, s))
        pl.when(valid & (stage == 3))(lambda: last_first(c, s))

        comm(tick, 1)

        pl.when(valid & (stage == 0))(lambda: attend_part(c, s))
        pl.when(valid & (stage == 1))(lambda: forward_second(c, s))
        pl.when(valid & (stage == 2))(lambda: back_second(c, s))
        pl.when(valid & (stage == 3))(lambda: last_second(c, s))

        next_valid, next_c = job_of(tick + 1, 4)
        next_stage = jnp.maximum(tick + 1, 0) // period
        pl.when(next_valid & (next_stage == 1))(lambda: bring(hidden, next_c).start())
        pl.when(next_valid & (next_stage == 2))(lambda: bring(cotangent, next_c).start())

    keep(0, stage_d, attn_low, chunks - 1).wait()
    for w in range(3):
        weight_sent(w)
    for u in range(units):
        for step in range(1, ctxs):
            qkv_copy(u, step).wait_send()
            context_copy(u, step).wait_send()


def enter(me, ranks, others):
    barrier = pltpu.get_barrier_semaphore()

    @pl.when(me > 0)
    def _():
        pl.semaphore_signal(barrier, inc=1, device_id={"tensor": me - 1}, device_id_type=MESH_IDS)

    @pl.when(me < ranks - 1)
    def _():
        pl.semaphore_signal(barrier, inc=1, device_id={"tensor": me + 1}, device_id_type=MESH_IDS)

    for other in others:
        pl.semaphore_signal(barrier, inc=1, device_id=other, device_id_type=MESH_IDS)
    pl.semaphore_wait(
        barrier, len(others) + jnp.minimum(me, 1) + jnp.minimum(ranks - 1 - me, 1)
    )


def middle(local_qkv, hidden, cotangent, shards, picked, gains, tok):
    od, ou, ed, eu, cd, cu = picked
    total, width = hidden.shape
    heads, hidden_units = shards[0].shape[0], shards[1].shape[1]
    ranks, dps, ctxs = (lax.axis_size(name) for name in ("tensor", "dp", "ctx"))
    seqs, local_heads = local_qkv.shape[:2]
    units = seqs * local_heads // ctxs
    rank = od.shape[1]
    rows = math.gcd(tok, CHUNK_ROWS)
    chunks = total // rows
    period = max(chunks, 2 * ranks)
    sizes = (ranks, dps, ctxs, chunks, rows, tok // rows, period)
    chips = dps * ctxs // 2
    vm = pl.BlockSpec(memory_space=pltpu.VMEM)
    hb = pl.BlockSpec(memory_space=pl.ANY)
    half = rows // 2
    dma = pltpu.SemaphoreType.DMA

    def shape(*dims):
        return jax.ShapeDtypeStruct(dims, BF)

    return pl.pallas_call(
        functools.partial(middle_kernel, sizes),
        out_shape=(
            shape(total, width),
            shape(total, width),
            shape(total, hidden_units),
            shape(total, width),
            shape(total, hidden_units),
            shape(total, width),
            shape(total, heads),
        )
        + (shape(total, rank),) * 6
        + (
            shape(total, heads),
            shape(units, 3, tok * ctxs, HEAD_DIM),
            shape(units, tok * ctxs, HEAD_DIM),
        ),
        in_specs=[vm, hb, hb, hb, hb, hb] + [vm] * 7,
        out_specs=(hb,) * 6 + (vm,) * 10,
        scratch_shapes=[
            pltpu.VMEM((heads, width), BF),
            pltpu.VMEM((width, hidden_units), BF),
            pltpu.VMEM((hidden_units, width), BF),
            pltpu.VMEM((chunks, rows, width), BF),
            pltpu.VMEM((chunks, half, width), BF),
            pltpu.VMEM((chunks, half, width), BF),
            pltpu.VMEM((chunks, rows, width), BF),
            pltpu.VMEM((chunks, rows, 128), F32),
            pltpu.VMEM((chunks, rows, hidden_units), BF),
            pltpu.VMEM((chunks, rows, width), BF),
            pltpu.VMEM((rows, width), BF),
            pltpu.VMEM((rows, hidden_units), BF),
            pltpu.VMEM((rows, width), BF),
            pltpu.VMEM((rows, rank), BF),
            dma(()),
            dma((3,)),
            dma((2, chunks)),
            dma((2, chunks)),
            dma((2, chunks)),
            dma((2, chunks)),
            dma((3, chips)),
            dma((3, chips)),
            dma((3, chips)),
            dma((3, chips)),
            dma((3,)),
            dma((units, ctxs)),
            dma((units, ctxs)),
            dma((units, ctxs)),
            dma((units, ctxs)),
            dma((2, units)),
        ],
        compiler_params=pltpu.CompilerParams(
            collective_id=0, has_side_effects=True, vmem_limit_bytes=VMEM_BYTES
        ),
        cost_estimate=pl.CostEstimate(
            flops=8 * total * width * hidden_units + 4 * total * width * heads,
            bytes_accessed=16 * total * width,
            transcendentals=total * hidden_units,
        ),
    )(local_qkv, hidden, cotangent, *shards, od, ou, ed, eu, cd, cu, gains)


def mixing_kernel(
    sizes,
    context_grad,
    unit_qkv,
    unit_out,
    mixing,
    mu,
    md,
    attn_low,
    input_grad,
    grads,
    rank_part,
    unit_go,
    unit_grad,
    sum_k,
    sum_v,
    acc,
    red_up,
    red_down,
    stage_d,
    rows_in,
    rank_buf,
    in_sem,
    out_sem,
    red_send,
    red_recv,
    cast_send,
    cast_recv,
    go_send,
    go_recv,
    grad_send,
    grad_recv,
    unit_sem,
):
    ranks, ctxs, chunks, rows, per_seq, group = sizes
    half = rows // 2
    width = mixing.shape[0]
    heads = grads.shape[2]
    local_heads = heads // HEAD_DIM
    units, seq_all = unit_go.shape[0], unit_go.shape[1]
    tok = seq_all // ctxs
    block = min(16, half)
    tile_d = math.gcd(width, 256)
    scale = HEAD_DIM ** (-0.5)
    me = lax.axis_index("tensor")
    ctx = lax.axis_index("ctx")

    enter(me, ranks, [{"ctx": (ctx + d) % ctxs} for d in range(1, ctxs)])

    def unit_place(device, u):
        return (device // local_heads) * units + u, device % local_heads

    def go_copy(u, step):
        peer = (ctx + step) % ctxs
        s, h = unit_place(peer, u)
        return pltpu.make_async_remote_copy(
            src_ref=context_grad.at[tile(s, tok), tile(h, HEAD_DIM)],
            dst_ref=unit_go.at[u, tile(ctx, tok)],
            send_sem=go_send.at[u, step],
            recv_sem=go_recv.at[u, step],
            device_id={"ctx": peer},
            device_id_type=MESH_IDS,
        )

    def go_arrival(u, step):
        return pltpu.make_async_remote_copy(
            src_ref=context_grad.at[tile(0, tok), tile(0, HEAD_DIM)],
            dst_ref=unit_go.at[u, tile((ctx + ctxs - step) % ctxs, tok)],
            send_sem=go_send.at[u, step],
            recv_sem=go_recv.at[u, step],
            device_id={"ctx": (ctx + step) % ctxs},
            device_id_type=MESH_IDS,
        )

    def go_own(u):
        s, h = unit_place(ctx, u)
        return pltpu.make_async_copy(
            context_grad.at[tile(s, tok), tile(h, HEAD_DIM)],
            unit_go.at[u, tile(ctx, tok)],
            unit_sem.at[0, u],
        )

    def grads_place(device, u):
        s, h = unit_place(device, u)
        return grads.at[:, tile(s, tok), tile(h, HEAD_DIM)]

    def grad_copy(u, step):
        peer = (ctx + step) % ctxs
        return pltpu.make_async_remote_copy(
            src_ref=unit_grad.at[u, :, tile(peer, tok)],
            dst_ref=grads_place(ctx, u),
            send_sem=grad_send.at[u, step],
            recv_sem=grad_recv.at[u, step],
            device_id={"ctx": peer},
            device_id_type=MESH_IDS,
        )

    def grad_arrival(u, step):
        return pltpu.make_async_remote_copy(
            src_ref=unit_grad.at[u, :, tile(ctx, tok)],
            dst_ref=grads_place((ctx + ctxs - step) % ctxs, u),
            send_sem=grad_send.at[u, step],
            recv_sem=grad_recv.at[u, step],
            device_id={"ctx": (ctx + step) % ctxs},
            device_id_type=MESH_IDS,
        )

    def grad_own(u):
        return pltpu.make_async_copy(
            unit_grad.at[u, :, tile(ctx, tok)], grads_place(ctx, u), unit_sem.at[1, u]
        )

    def attend_back(u):
        go_own(u).wait()
        for step in range(1, ctxs):
            go_arrival(u, step).wait_recv()
        part = math.gcd(seq_all, 256)
        sum_k[...] = jnp.zeros_like(sum_k)
        sum_v[...] = jnp.zeros_like(sum_v)

        @pl.loop(0, seq_all // part)
        def _(i):
            rs = tile(i, part)
            queries = unit_qkv[u, 0, rs, :]
            go = unit_go[u, rs, :]
            scores = dot_nt(queries, unit_qkv[u, 1]) * scale
            raised = jnp.exp(scores - jnp.max(scores, axis=-1, keepdims=True))
            probs = raised * (1.0 / jnp.sum(raised, axis=-1, keepdims=True))
            delta = jnp.sum(
                go.astype(F32) * unit_out[u, rs, :].astype(F32), axis=-1, keepdims=True
            )
            dscores = (probs * (dot_nt(go, unit_qkv[u, 2]) - delta)).astype(BF)
            unit_grad[u, 0, rs, :] = (scale * dot_nn(dscores, unit_qkv[u, 1])).astype(BF)
            sum_k[...] += dot_tn(dscores, queries)
            sum_v[...] += dot_tn(probs.astype(BF), go)

        unit_grad[u, 1] = (scale * sum_k[...]).astype(BF)
        unit_grad[u, 2] = sum_v[...].astype(BF)
        for step in range(1, ctxs):
            grad_copy(u, step).start()
        grad_own(u).start()

    def grads_ready(u):
        grad_own(u).wait()
        for step in range(1, ctxs):
            grad_arrival(u, step).wait_recv()

    for u in range(units):
        go_own(u).start()
        for step in range(1, ctxs):
            go_copy(u, step).start()

    def job_of(number):
        return (number >= 0) & (number < chunks), jnp.clip(number, 0, chunks - 1)

    comm = chain(
        ranks, half, block, me, acc, red_up, red_down, red_send, red_recv, cast_send, cast_recv, job_of
    )

    def rows_of(c):
        return tile(c, rows)

    def bring(c):
        return pltpu.make_async_copy(attn_low.at[rows_of(c)], rows_in, in_sem)

    def keep(c):
        return pltpu.make_async_copy(stage_d, input_grad.at[rows_of(c)], out_sem)

    def back_part(c, s):
        rs = pl.ds(pl.multiple_of(c * rows, group * rows), group * rows)
        low = jnp.zeros((group * rows, mu.shape[1]), F32)
        for j in range(3):
            low = low + dot_nt(grads[j, rs, :], mu[s, :, pl.ds(j * heads, heads)])
        low = low.astype(BF)
        rank_part[rs, :] = low
        rank_buf[...] = low

        @pl.loop(0, width // tile_d)
        def _(i):
            cs = tile(i, tile_d)
            total = dot_nn(rank_buf[...], md[s, :, cs])
            for j in range(3):
                total = total + dot_nt(grads[j, rs, :], mixing[cs, pl.ds(j * heads, heads)])
            total = total.astype(BF)
            for k in range(group):
                acc[c + k, :, cs] = total[k * rows : (k + 1) * rows, :]

    def final_part(c):
        bring(c).wait()

        @pl.loop(0, rows // block)
        def _(i):
            rs = tile(i, block)
            stage_d[rs, :] = (rows_in[rs, :].astype(F32) + acc[c, rs, :].astype(F32)).astype(BF)

        keep(c).start()

    delay = 2 * ranks

    @pl.loop(0, per_seq + chunks + delay)
    def _(now):
        tick = now - per_seq
        valid, c = job_of(tick)
        final, c_final = job_of(tick - delay)
        before, c_before = job_of(tick - delay - 1)
        coming, c_coming = job_of(tick - delay + 1)
        s = c // per_seq

        comm(tick, 0)

        pl.when((now % per_seq == 0) & (now < units * per_seq))(lambda: attend_back(now // per_seq))
        pl.when((tick >= 0) & (tick % per_seq == 0) & (tick < units * per_seq))(
            lambda: grads_ready(s)
        )
        comm(tick, 1)

        pl.when(valid & (tick % group == 0))(lambda: back_part(c, s))

        pl.when(before)(lambda: keep(c_before).wait())
        pl.when(final)(lambda: final_part(c_final))
        pl.when(coming)(lambda: bring(c_coming).start())

    keep(chunks - 1).wait()
    for u in range(units):
        for step in range(1, ctxs):
            go_copy(u, step).wait_send()
            grad_copy(u, step).wait_send()


def mixing_back(context_grad, unit_qkv, unit_out, mixing, picked, attn_low):
    mu, md = picked
    total, width = attn_low.shape
    heads = context_grad.shape[1]
    ranks, ctxs = (lax.axis_size(name) for name in ("tensor", "ctx"))
    units, _, seq_all, _ = unit_qkv.shape
    tok = seq_all // ctxs
    rank = mu.shape[1]
    rows = math.gcd(tok, LAST_ROWS)
    chunks = total // rows
    per_seq = tok // rows
    group = math.gcd(per_seq, 2)
    half = rows // 2
    sizes = (ranks, ctxs, chunks, rows, per_seq, group)
    vm = pl.BlockSpec(memory_space=pltpu.VMEM)
    hb = pl.BlockSpec(memory_space=pl.ANY)
    dma = pltpu.SemaphoreType.DMA
    return pl.pallas_call(
        functools.partial(mixing_kernel, sizes),
        out_shape=(
            jax.ShapeDtypeStruct((total, width), BF),
            jax.ShapeDtypeStruct((3, total, heads), BF),
            jax.ShapeDtypeStruct((total, rank), BF),
        ),
        in_specs=[vm] * 6 + [hb],
        out_specs=(hb, vm, vm),
        scratch_shapes=[
            pltpu.VMEM((units, seq_all, HEAD_DIM), BF),
            pltpu.VMEM((units, 3, seq_all, HEAD_DIM), BF),
            pltpu.VMEM((seq_all, HEAD_DIM), F32),
            pltpu.VMEM((seq_all, HEAD_DIM), F32),
            pltpu.VMEM((chunks, rows, width), BF),
            pltpu.VMEM((chunks, half, width), BF),
            pltpu.VMEM((chunks, half, width), BF),
            pltpu.VMEM((rows, width), BF),
            pltpu.VMEM((rows, width), BF),
            pltpu.VMEM((group * rows, rank), BF),
            dma(()),
            dma(()),
            dma((2, chunks)),
            dma((2, chunks)),
            dma((2, chunks)),
            dma((2, chunks)),
            dma((units, ctxs)),
            dma((units, ctxs)),
            dma((units, ctxs)),
            dma((units, ctxs)),
            dma((2, units)),
        ],
        compiler_params=pltpu.CompilerParams(
            collective_id=1, has_side_effects=True, vmem_limit_bytes=VMEM_LAST
        ),
        cost_estimate=pl.CostEstimate(
            flops=6 * total * width * heads + 10 * units * seq_all * seq_all * HEAD_DIM,
            bytes_accessed=8 * total * width,
            transcendentals=units * seq_all * seq_all,
        ),
    )(context_grad, unit_qkv, unit_out, mixing, mu, md, attn_low)


def pick_rows(onehot_low, table):
    return jnp.einsum(
        "sn,n...->s...", onehot_low, table, preferred_element_type=jnp.float32
    ).astype(jnp.bfloat16)


def per_device(
    hidden_in,
    output_cotangent,
    adapter_index,
    mixing_weight,
    output_weight,
    expand_weight,
    contract_weight,
    first_gain,
    first_shift,
    second_gain,
    second_shift,
    mixing_down,
    mixing_up,
    output_down,
    output_up,
    expand_down,
    expand_up,
    contract_down,
    contract_up,
):
    seq_count, tok_count, model_width = hidden_in.shape
    local_heads = mixing_weight.shape[2] // HEAD_DIM
    local_width = mixing_weight.shape[2]
    rows_all = seq_count * tok_count
    adapter_ids = jnp.arange(NADAPT, dtype=jnp.int32)
    onehot_low = (adapter_index == adapter_ids[None, :]).astype(jnp.bfloat16)
    mixing_down_sel = pick_rows(onehot_low, mixing_down)
    mixing_up_sel = pick_rows(onehot_low, mixing_up)
    output_down_sel = pick_rows(onehot_low, output_down)
    output_up_sel = pick_rows(onehot_low, output_up)
    expand_down_sel = pick_rows(onehot_low, expand_down)
    expand_up_sel = pick_rows(onehot_low, expand_up)
    contract_down_sel = pick_rows(onehot_low, contract_down)
    contract_up_sel = pick_rows(onehot_low, contract_up)
    rank = mixing_down.shape[1]
    mixing_flat = mixing_weight.reshape(mixing_weight.shape[0], 3 * local_width)
    mixing_full = lax.all_gather(mixing_flat, ("dp", "ctx"), axis=0, tiled=True)
    hidden_rows = hidden_in.reshape(rows_all, model_width)
    mixing_rank = jnp.einsum(
        "std,srd->str", hidden_in, mixing_down_sel, preferred_element_type=jnp.float32
    ).astype(jnp.bfloat16)
    mixing_up_flat = mixing_up_sel.reshape(seq_count, rank, 3 * local_width)
    projected = jnp.einsum(
        "std,df->stf", hidden_in, mixing_full, preferred_element_type=jnp.float32
    )
    projected = projected + jnp.einsum(
        "str,srf->stf", mixing_rank, mixing_up_flat, preferred_element_type=jnp.float32
    )
    projected = projected.astype(jnp.bfloat16)
    local_qkv = projected.reshape(seq_count, tok_count, 3, local_heads, HEAD_DIM).transpose(
        0, 3, 2, 1, 4
    )
    gains = jnp.stack([first_gain, first_shift, second_gain, second_shift])
    (
        out_rows,
        first_low,
        active_low,
        second_low,
        before_low,
        attn_low,
        context_grad,
        output_rank,
        expand_rank,
        contract_rank,
        contract_rank_grad,
        expand_rank_grad,
        output_rank_grad,
        context,
        unit_qkv,
        unit_out,
    ) = middle(
        local_qkv,
        hidden_rows,
        output_cotangent.reshape(rows_all, model_width),
        (output_weight, expand_weight, contract_weight),
        (
            output_down_sel,
            output_up_sel,
            expand_down_sel,
            expand_up_sel,
            contract_down_sel,
            contract_up_sel,
        ),
        gains,
        tok_count,
    )
    input_rows, grads, mixing_rank_grad = mixing_back(
        context_grad, unit_qkv, unit_out, mixing_full, (mixing_up_flat, mixing_down_sel), attn_low
    )
    shared = lax.psum(
        jnp.concatenate([output_rank, contract_rank, expand_rank_grad], axis=1), "tensor"
    )
    output_rank, contract_rank, expand_rank_grad = (
        shared[:, :rank],
        shared[:, rank : 2 * rank],
        shared[:, 2 * rank :],
    )
    mixing_rank_grad = lax.psum(mixing_rank_grad, "tensor")
    row_hot = jnp.repeat(onehot_low, tok_count, axis=0)

    def table_grad(ranks, values):
        wide = (row_hot[:, :, None] * ranks[:, None, :]).reshape(rows_all, -1)
        part = jnp.einsum("nk,nd->kd", wide, values, preferred_element_type=jnp.float32)
        return part.astype(jnp.bfloat16).reshape(NADAPT, rank, values.shape[1])

    early = (
        table_grad(output_rank_grad, context),
        table_grad(output_rank, attn_low),
        table_grad(expand_rank_grad, first_low),
        table_grad(expand_rank, before_low),
        table_grad(contract_rank_grad, active_low),
        table_grad(contract_rank, second_low),
    )
    mixing_ranks = mixing_rank.reshape(rows_all, rank)
    late = (
        table_grad(mixing_rank_grad, hidden_rows),
        jnp.stack([table_grad(mixing_ranks, grads[j]) for j in range(3)], axis=2),
    )
    early = lax.psum(early, ("dp", "ctx"))
    late = lax.psum(late, ("dp", "ctx"))
    summed = tuple(part.astype(jnp.float32) for part in late + early)
    return (
        out_rows.reshape(hidden_in.shape),
        input_rows.reshape(hidden_in.shape),
    ) + summed


def solution(mesh):
    return jax.shard_map(
        per_device,
        mesh=mesh,
        in_specs=(
            P("dp", "ctx", None),
            P("dp", "ctx", None),
            P("dp", None),
            P(("dp", "ctx"), None, "tensor"),
            P("tensor", ("dp", "ctx")),
            P(("dp", "ctx"), "tensor"),
            P("tensor", ("dp", "ctx")),
            P(),
            P(),
            P(),
            P(),
            P(),
            P(None, None, None, "tensor"),
            P(None, None, "tensor"),
            P(),
            P(),
            P(None, None, "tensor"),
            P(None, None, "tensor"),
            P(),
        ),
        out_specs=(
            P("dp", "ctx", None),
            P("dp", "ctx", None),
            P(),
            P(None, None, None, "tensor"),
            P(None, None, "tensor"),
            P(),
            P(),
            P(None, None, "tensor"),
            P(None, None, "tensor"),
            P(),
        ),
        check_vma=False,
    )
```

time: 1050 us -> 788 us (0.75)
  waiting for transfers between devices: 481 us -> 109 us
  Pallas kernels: 318 us -> 558 us
  matrix products: 108 us -> 33.4 us
  local copies, waits for them, and re-layouts: 64.8 us -> 32 us
  other arithmetic: 38.3 us -> 14.8 us
    all_gather x6 -> x1, waiting for transfers between devices: 202 us -> 34.6 us  [per_device(): mixing_full = lax.all_gather(mixing_flat, ('dp', 'ctx'), axis=0, tiled=True)]
    pallas_call x0 -> x1, Pallas kernels: none -> 145 us  [mixing_back(): pl.pallas_call(functools.partial(mixing_kernel, sizes), out_shape=(jax.Sh...]
    psum x1, waiting for transfers between devices: 124 us -> 0.01 us  [per_device(): lax.psum(jnp.concatenate([output_rank, contract_rank, expand_rank_grad],...]
    pallas_call x1, Pallas kernels: 318 us -> 412 us  [middle(): pl.pallas_call(functools.partial(middle_kernel, sizes), out_shape=(shape(...]
    reduce_scatter x2 -> x0, waiting for transfers between devices: 83.8 us -> none  [the longest x1 44.5 us: per_device(): lax.psum_scatter(key_parts.astype(jnp.bfloat16), 'ctx', scatter_dimension...]
    dot_general x19 -> x2, matrix products: 81.4 us -> 12.7 us  [the longest x1 10 us: per_device(): jnp.einsum('std,df->stf', hidden_in, mixing_full, preferred_element_type=...]
    while x34 -> x0, local copies, waits for them, and re-layouts: 15.8 us -> none
    reduce_sum x3 -> x0, other arithmetic: 12.4 us -> none  [the longest x2 10.1 us: attend_advance(): running_sum = running_sum * factor + jnp.sum(raised, axis=-1)]
  transfers between devices with their start and end apart: 10 -> 3, of which waited for: 9 -> 2; matrix products, arithmetic and copies ran while one was open for 8% -> 2% of each run, Pallas kernels for 0% -> 18%
where the time goes in v2:
time: 788 us; the launch traced here: 787 us
  Pallas kernels  558 us (71%)
  waiting for transfers between devices  109 us (14%)
  matrix products  33.4 us (4%)
  local copies, waits for them, and re-layouts  32 us (4%)
  blocking collectives  26 us (3%)
  other arithmetic  14.8 us (2%)
  between operations  14.1 us (2%)
    pallas_call x1, Pallas kernels, middle(): pl.pallas_call(functools.partial(middle_kernel, sizes), out_shape=(shape(...  412 us
    pallas_call x1, Pallas kernels, mixing_back(): pl.pallas_call(functools.partial(mixing_kernel, sizes), out_shape=(jax.Sh...  145 us
    psum x1, waiting for transfers between devices, per_device(): late = lax.psum(late, ('dp', 'ctx'))  74.6 us
    all_gather x1, waiting for transfers between devices, per_device(): mixing_full = lax.all_gather(mixing_flat, ('dp', 'ctx'), axis=0, tiled=True)  34.6 us
    psum x1, blocking collectives, per_device(): mixing_rank_grad = lax.psum(mixing_rank_grad, 'tensor')  26 us
  transfers between devices with their start and end apart: 3, of which 2 were waited for; matrix products, arithmetic and copies ran while one was open for 2% of the time, Pallas kernels for 18%

profile of v2, /device:TPU:0, one launch (start us, length us, event | category | flops | bytes accessed | tf_op | source)
XLA Modules:
  0.0 787.3 jit_solution(15209168387398431798)
XLA Ops:
  7.3 1.5 copy.80
  8.7 1.2 copy.81
  10.0 1.2 fusion.21
  11.2 0.6 copy.142.od
  11.8 0.4 convolution_convert_fusion.6
  12.3 0.3 reshape.132.mu
  12.6 0.5 fusion.18
  13.1 0.2 copy.141.md
  13.3 3.5 convolution_convert_fusion.11
  16.8 0.5 fusion.16
  17.3 0.9 copy.140.ou
  18.1 0.5 fusion.14
  18.6 0.9 copy.139.ed
  19.4 0.5 fusion.12
  19.9 0.9 copy.138.eu
  20.8 0.5 fusion.10
  21.2 0.9 copy.137.cd
  22.1 0.5 fusion.8
  22.6 0.9 copy.136.cu
  23.5 0.7 pad_maximum_fusion.2.gains
  24.2 34.6 %all-gather.2.cloned.1.call-done.mixing = bf16[2048,1536]{1,0:T(8,128)(2,1)} async-done(((bf16[256,1536]{1,0:T(8,128)(2,1)}), bf16[2048,1536]{1,0:T(8,128)(2,1)}) %all-gather.2.cloned.1.call-update) | async-done | bytes 6291472 | tf_op jit(solution)/shard_map/all_gather | solution.py:1070
  58.8 10.0 %fusion = f32[4,256,1536]{2,1,0:T(8,128)S(1)} fusion(bf16[4,256,2048]{2,1,0:T(8,128)(2,1)} %param.19, bf16[2048,1536]{1,0:T(8,128)(2,1)} %all-gather.2.cloned.1.call-done.mixing), kind=kOutput, calls=%fused_computation | convolution fusion | flops 6442450944 | bytes 16777216 | tf_op jit(solution)/shard_map/std,df->stf/dot_general | solution.py:1076
  68.8 2.7 add_convert_fusion
  71.5 4.6 copy.86
  76.1 4.6 copy.87
  80.7 412.4 %shard_map.258 = (bf16[1024,2048]{1,0:T(8,128)(2,1)}, bf16[1024,2048]{1,0:T(8,128)(2,1)}, bf16[1024,2048]{1,0:T(8,128)(2,1)}, bf16[1024,2048]{1,0:T(8,128)(2,1)}...) custom-call(bf16[4,4,3,256,128]{4,3,2,1,0:T(8,128)(2,1)} %bitcast.92, ...), custom_call_target="tpu_custom_call" | custom-call | flops 38654705664 | bytes 33554432 | tf_op jit(solution)/shard_map/pallas_call | solution.py:676
  493.1 1.1 copy.106
  494.2 1.1 copy.107
  495.2 1.1 copy.108
  496.3 0.7 pad_maximum_fusion.1
  497.0 1.2 copy-done.4
  498.2 1.2 copy-done.5
  499.5 145.3 %shard_map.259 = (bf16[1024,2048]{1,0:T(8,128)(2,1)}, bf16[3,1024,512]{2,1,0:T(8,128)(2,1)S(1)}, bf16[1024,16]{1,0:T(8,128)(2,1)S(1)}) custom-call(bf16[1024,512]{1,0:T(8,128)(2,1)S(1)} %copy-done.4, bf16[4,3,1024,128]{3,2,1,0:T(8,128)(2,1)} %get-tuple-element.31.unit_qkv, bf16[4,1024,128]{2,1,0:T(8,128)(2,1)S(1)} %copy-done.5, ...), custom_call_target="tpu_custom_call" | custom-call | flops 11811160064 | bytes 16777216 | tf_op jit(solution)/shard_map/pallas_call | solution.py:984
  644.8 1.7 copy-done.2
  646.4 0.1 copy.105
  646.5 0.1 copy.109
  646.6 0.1 copy.110
  646.8 26.0 %psum.70 = bf16[1024,16]{1,0:T(8,128)(2,1)S(1)} all-reduce(bf16[1024,16]{1,0:T(8,128)(2,1)S(1)} %get-tuple-element.35), channel_id=1, replica_groups=mesh['dp'=2,'ctx'=4,'tensor'=4] {'tensor'}, use_global_device_ids=true, to_apply=%region_0.0 | all-reduce | flops 16384 | bytes 65536 | tf_op jit(solution)/shard_map/psum | solution.py:1131
  672.8 0.1 copy.100
  672.9 0.9 fusion.35
  674.0 0.2 broadcast_multiply_fusion
  674.1 2.1 convolution_convert_fusion.8
  676.3 0.3 convolution_convert_fusion.9
  676.6 0.3 convolution_convert_fusion.10
  677.0 1.5 convolution_convert_fusion.4
  678.5 1.5 convolution_convert_fusion.5
  680.0 1.5 convolution_convert_fusion.1
  681.6 1.5 convolution_convert_fusion.2
  683.1 1.5 convolution_convert_fusion.3
  684.6 1.0 convolution_convert_fusion.7
  685.6 1.5 convolution_convert_fusion
  687.1 0.8 pad_maximum_fusion
  688.0 74.6 %all-reduce.6.cloned.1.call-done = (bf16[8,16,2048]{2,1,0:T(8,128)(2,1)}, bf16[8,16,3,512]{3,1,2,0:T(8,128)(2,1)}, bf16[8,16,512]{2,1,0:T(8,128)(2,1)}, bf16[8,1...) async-done(((bf16[8,16,2048]{2,1,0:T(8,128)(2,1)}, ...) | async-done | bytes 3670032 | tf_op jit(solution)/shard_map/psum | solution.py:1153
  762.6 1.8 convert_element_type.109
  764.3 2.2 convert_element_type.102
  766.5 2.0 convert_element_type.107
  768.5 2.3 convert_element_type.111
  770.7 1.1 convert_element_type.113
  771.8 1.1 convert_element_type.115
  772.9 1.1 convert_element_type.117
  773.9 1.1 convert_element_type.119
  775.0 2.1 copy.156
  777.2 1.6 copy-done.13
  778.7 2.0 copy.157
  (73 shorter events, 0.6 us)
Async XLA Ops:
  7.2 5.4 copy-start
  7.2 4.6 copy-start.28
  7.2 4.6 copy-start.24
  7.2 51.5 %all-gather.2.cloned.1.call-start = ((), (), s32[]{:S(2)}) async-start(), calls=%async_computation | async-start | bytes 7077888 | tf_op jit(solution)/shard_map/all_gather | solution.py:1070
  9.9 6.9 copy-start.19
  9.9 663.0 %all-reduce.4.cloned.1.call-start = ((), (), s32[]{:S(2)}) async-start(), calls=%async_computation.1 | async-start | bytes 196608 | tf_op jit(solution)/shard_map/psum | solution.py:1123
  12.2 5.9 copy-start.20
  12.6 6.9 copy-start.21
  13.2 7.5 copy-start.22
  13.2 8.9 %copy-start.23 = (bf16[8,16,2048]{2,1,0:T(8,128)(2,1)S(1)}, bf16[8,16,2048]{2,1,0:T(8,128)(2,1)}, u32[]{:S(2)}) copy-start(bf16[8,16,2048]{2,1,0:T(8,128)(2,1)} %param.37) | copy-start | bytes 1572868
  16.8 6.7 copy-start.29
  16.8 6.7 copy-start.30
  16.8 6.7 copy-start.31
  16.8 6.7 copy-start.32
  497.0 265.6 %all-reduce.6.cloned.1.call-start = ((), (), s32[]{:S(2)}) async-start(), calls=%async_computation.2 | async-start | bytes 7340032 | tf_op jit(solution)/shard_map/psum | solution.py:1153
  497.0 1.2 copy-start.4
  498.2 1.2 copy-start.5
  499.5 147.0 %copy-start.27 = (bf16[1024,16]{1,0:T(8,128)(2,1)S(1)}, bf16[1024,16]{1,0:T(8,128)(2,1)}, u32[]{:S(2)}) copy-start(bf16[1024,16]{1,0:T(8,128)(2,1)} %get-tuple-element.37) | copy-start | bytes 98308
  499.5 147.1 %copy-start.26 = (bf16[1024,16]{1,0:T(8,128)(2,1)S(1)}, bf16[1024,16]{1,0:T(8,128)(2,1)}, u32[]{:S(2)}) copy-start(bf16[1024,16]{1,0:T(8,128)(2,1)} %get-tuple-element.43) | copy-start | bytes 98308
  499.5 147.2 %copy-start.25 = (bf16[1024,16]{1,0:T(8,128)(2,1)S(1)}, bf16[1024,16]{1,0:T(8,128)(2,1)}, u32[]{:S(2)}) copy-start(bf16[1024,16]{1,0:T(8,128)(2,1)} %get-tuple-element.45) | copy-start | bytes 98308
  644.7 1.7 copy-start.2
  672.9 3.4 copy-start.3
  672.9 4.0 copy-start.11
  676.3 2.2 copy-start.6
  676.9 3.1 copy-start.10
  678.5 3.1 copy-start.9
  680.0 3.1 copy-start.8
  681.6 3.1 copy-start.14
  683.1 2.5 copy-start.7
  762.5 8.2 %copy-start.18 = (bf16[8,16,2048]{2,1,0:T(8,128)(2,1)S(1)}, bf16[8,16,2048]{2,1,0:T(8,128)(2,1)}, u32[]{:S(2)}) copy-start(bf16[8,16,2048]{2,1,0:T(8,128)(2,1)} %get-tuple-element.52) | copy-start | bytes 1572868
  762.5 9.2 %copy-start.17 = (bf16[8,16,2048]{2,1,0:T(8,128)(2,1)S(1)}, bf16[8,16,2048]{2,1,0:T(8,128)(2,1)}, u32[]{:S(2)}) copy-start(bf16[8,16,2048]{2,1,0:T(8,128)(2,1)} %get-tuple-element.53) | copy-start | bytes 1572868
  762.5 10.3 %copy-start.16 = (bf16[8,16,2048]{2,1,0:T(8,128)(2,1)S(1)}, bf16[8,16,2048]{2,1,0:T(8,128)(2,1)}, u32[]{:S(2)}) copy-start(bf16[8,16,2048]{2,1,0:T(8,128)(2,1)} %get-tuple-element.54) | copy-start | bytes 1572868
  764.3 9.6 %copy-start.15 = (bf16[8,16,2048]{2,1,0:T(8,128)(2,1)S(1)}, bf16[8,16,2048]{2,1,0:T(8,128)(2,1)}, u32[]{:S(2)}) copy-start(bf16[8,16,2048]{2,1,0:T(8,128)(2,1)} %get-tuple-element.55) | copy-start | bytes 1572868
  768.4 6.6 copy-start.12
  775.0 3.7 copy-start.13
  775.0 5.7 copy-start.1
Sparse Core Ops, SparseCore 0:
  10.5 48.2 all-gather.1
  497.1 35.5 all-reduce.3
  688.1 74.4 all-reduce.5

commit v3 on v2

--- a/solution.py
+++ b/solution.py
@@ -14,6 +14,7 @@
 LAST_ROWS = 64
 VMEM_BYTES = 62 * 2**20
 VMEM_LAST = 48 * 2**20
+PIECES = 4
 
 
 BF = jnp.bfloat16
@@ -131,12 +132,14 @@
 
 def middle_kernel(
     sizes,
-    local_qkv,
     hidden,
     cotangent,
+    shard_mix,
     shard_out,
     shard_exp,
     shard_con,
+    md,
+    mu,
     od,
     ou,
     ed,
@@ -144,32 +147,30 @@
     cd,
     cu,
     gains,
+    unit_rank,
     hidden_out,
     first_low,
     active,
     second_low,
     before_grad,
     attn_low,
+    mixing,
     context_grad,
-    out_rank,
-    exp_rank,
-    con_rank,
-    con_rank_grad,
-    exp_rank_grad,
-    out_rank_grad,
+    part_ranks,
+    full_ranks,
     context,
     unit_qkv,
     unit_out,
+    local_qkv,
     w_out,
     w_exp,
     w_con,
     acc,
     red_up,
     red_down,
-    normed,
+    stash,
     spreads,
-    slope,
-    second,
+    rank_in,
     stage_d,
     stage_f,
     rows_in,
@@ -184,7 +185,12 @@
     peer_recv,
     twin_send,
     twin_recv,
+    side_send,
+    side_recv,
     own_sem,
+    rank_send,
+    rank_recv,
+    mix_sem,
     qkv_send,
     qkv_recv,
     ctx_send,
@@ -219,103 +225,175 @@
         from_chip = (ctx // 2 + pairs - column) % pairs
         return from_dp * ctxs + from_chip * 2 + which
 
-    enter(me, ranks, [{"ctx": (ctx + d) % ctxs} for d in range(1, ctxs)]
-          + [{"dp": (dp + e) % dps, "ctx": 2 * f + core}
-             for e in range(1, dps) for f in range(pairs)])
-
-    shards = (shard_out, shard_exp, shard_con)
-    fulls = (w_out, w_exp, w_con)
-
-    def block_of(w, index):
+    total = chunks * rows
+    enter(
+        [{"tensor": (me + d) % ranks} for d in range(1, ranks)]
+        + [{"ctx": (ctx + d) % ctxs} for d in range(1, ctxs)]
+        + [{"dp": (dp + d) % dps} for d in range(1, dps)]
+    )
+
+    shards = (shard_mix, shard_out, shard_exp, shard_con)
+    fulls = (stash, w_out, w_exp, w_con)
+    mix_width = shard_mix.shape[1]
+    mix_half = shard_mix.shape[0] // 2
+
+    def piece_of(w, p):
+        if w < 2:
+            return shards[w]
+        return shards[w].at[tile(p, shards[w].shape[0] // PIECES)]
+
+    def block_of(w, index, p):
+        deep, wide = shards[w].shape
+        if w == 0:
+            return stash.at[tile(index, deep), pl.ds(0, mix_width)]
         if w == 1:
-            return fulls[w].at[tile(index, shards[w].shape[0])]
-        return fulls[w].at[:, tile(index, shards[w].shape[1])]
-
-    def peer_copy(w, step):
+            return w_out.at[:, tile(index, wide)]
+        if w == 2:
+            return w_exp.at[tile(index * PIECES + p, deep // PIECES)]
+        return w_con.at[tile(p, deep // PIECES), tile(index, wide)]
+
+    def mix_piece(step, lower):
+        start = chip_block(step, core) * (2 * mix_half) + lower * mix_half
+        return stash.at[pl.ds(pl.multiple_of(start, mix_half), mix_half), pl.ds(0, mix_width)]
+
+    def peer_copy(w, step, p=0):
         row, column = step // pairs, step % pairs
-        block = block_of(w, chip_block(column, core))
+        block = block_of(w, chip_block(column, core), p)
         if row:
             target = {"dp": (dp + row) % dps}
         else:
             target = {"ctx": (ctx + 2 * column) % ctxs}
-        own = block_of(w, chip_block(0, core))
-        return pltpu.make_async_remote_copy(
-            src_ref=block if row and column else shards[w],
+        own = block_of(w, chip_block(0, core), p)
+        if w == 0 and row and column:
+            block = mix_piece(column, 0)
+        return pltpu.make_async_remote_copy(
+            src_ref=block if row and column else piece_of(w, p),
             dst_ref=block if row else own,
-            send_sem=peer_send.at[w, step],
-            recv_sem=peer_recv.at[w, step],
+            send_sem=peer_send.at[w, step, p],
+            recv_sem=peer_recv.at[w, step, p],
             device_id=target,
             device_id_type=MESH_IDS,
         )
 
-    def peer_arrival(w, step):
+    def peer_arrival(w, step, p=0):
         row = step // pairs
         if row:
             target = {"dp": (dp + row) % dps}
         else:
             target = {"ctx": (ctx + 2 * step) % ctxs}
-        return pltpu.make_async_remote_copy(
-            src_ref=shards[w],
-            dst_ref=block_of(w, chip_block(step, core)),
-            send_sem=peer_send.at[w, step],
-            recv_sem=peer_recv.at[w, step],
-            device_id=target,
-            device_id_type=MESH_IDS,
-        )
-
-    def twin_copy(w, step):
-        block = block_of(w, chip_block(step, core))
-        return pltpu.make_async_remote_copy(
-            src_ref=shards[w] if step == 0 else block,
-            dst_ref=block,
-            send_sem=twin_send.at[w, step],
-            recv_sem=twin_recv.at[w, step],
-            device_id=twin,
-            device_id_type=MESH_IDS,
-        )
-
-    def twin_arrival(w, step):
-        block = block_of(w, chip_block(step, 1 - core))
+        block = block_of(w, chip_block(step, core), p)
+        if w == 0 and row and step % pairs:
+            block = mix_piece(step, 0)
         return pltpu.make_async_remote_copy(
             src_ref=block,
             dst_ref=block,
-            send_sem=twin_send.at[w, step],
-            recv_sem=twin_recv.at[w, step],
+            send_sem=peer_send.at[w, step, p],
+            recv_sem=peer_recv.at[w, step, p],
+            device_id=target,
+            device_id_type=MESH_IDS,
+        )
+
+    def twin_copy(w, step, p=0):
+        block = block_of(w, chip_block(step, core), p)
+        return pltpu.make_async_remote_copy(
+            src_ref=piece_of(w, p) if step == 0 else block,
+            dst_ref=block,
+            send_sem=twin_send.at[w, step, p],
+            recv_sem=twin_recv.at[w, step, p],
             device_id=twin,
             device_id_type=MESH_IDS,
         )
 
-    def own_copy(w):
-        return pltpu.make_async_copy(shards[w], block_of(w, chip_block(0, core)), own_sem.at[w])
-
-    def weight_start(w):
-        for step in list(range(pairs, chips, pairs)) + list(range(1, pairs)):
-            peer_copy(w, step).start()
-        twin_copy(w, 0).start()
-        own_copy(w).start()
-
-    def weight_relay(w):
+    def twin_arrival(w, step, p=0):
+        block = block_of(w, chip_block(step, 1 - core), p)
+        return pltpu.make_async_remote_copy(
+            src_ref=block,
+            dst_ref=block,
+            send_sem=twin_send.at[w, step, p],
+            recv_sem=twin_recv.at[w, step, p],
+            device_id=twin,
+            device_id_type=MESH_IDS,
+        )
+
+    def own_copy(w, p=0):
+        return pltpu.make_async_copy(piece_of(w, p), block_of(w, chip_block(0, core), p), own_sem.at[w, p])
+
+    def side_copy(step):
+        row, column = step // pairs, step % pairs
+        piece = mix_piece(row * pairs, 1)
+        return pltpu.make_async_remote_copy(
+            src_ref=piece,
+            dst_ref=piece,
+            send_sem=side_send.at[step],
+            recv_sem=side_recv.at[step],
+            device_id={"ctx": (ctx + 2 * column) % ctxs},
+            device_id_type=MESH_IDS,
+        )
+
+    def side_arrival(step):
+        piece = mix_piece(step, 1)
+        return pltpu.make_async_remote_copy(
+            src_ref=piece,
+            dst_ref=piece,
+            send_sem=side_send.at[step],
+            recv_sem=side_recv.at[step],
+            device_id={"ctx": (ctx + 2 * (step % pairs)) % ctxs},
+            device_id_type=MESH_IDS,
+        )
+
+    def across_start(w, p=0):
+        for step in range(pairs, chips, pairs):
+            peer_copy(w, step, p).start()
+        twin_copy(w, 0, p).start()
+        own_copy(w, p).start()
+
+    def along_start(w, p=0):
         for step in range(1, pairs):
-            peer_arrival(w, step).wait_recv()
-            twin_copy(w, step).start()
+            peer_copy(w, step, p).start()
+
+    def weight_relay(w, p=0):
+        for step in range(1, pairs):
+            peer_arrival(w, step, p).wait_recv()
             for row in range(1, dps):
-                peer_copy(w, row * pairs + step).start()
-
-    def weight_forward(w):
+                peer_copy(w, row * pairs + step, p).start()
+            twin_copy(w, step, p).start()
+
+    def weight_forward(w, p=0):
         for step in range(pairs, chips):
-            peer_arrival(w, step).wait_recv()
-            twin_copy(w, step).start()
-
-    def weight_finish(w):
-        own_copy(w).wait()
+            peer_arrival(w, step, p).wait_recv()
+            twin_copy(w, step, p).start()
+
+    def mixing_gather():
+        along_start(0)
+        across_start(0)
+        weight_relay(0)
+        for row in range(1, dps):
+            peer_arrival(0, row * pairs).wait_recv()
+            for column in range(1, pairs):
+                side_copy(row * pairs + column).start()
+            twin_copy(0, row * pairs).start()
+        for row in range(1, dps):
+            for column in range(1, pairs):
+                step = row * pairs + column
+                peer_arrival(0, step).wait_recv()
+                side_arrival(step).wait_recv()
+                twin_copy(0, step).start()
+
+    def weight_finish(w, p=0):
+        own_copy(w, p).wait()
         for step in range(chips):
-            twin_arrival(w, step).wait_recv()
-
-    def weight_sent(w):
+            twin_arrival(w, step, p).wait_recv()
+
+    def side_sent():
+        for row in range(1, dps):
+            for column in range(1, pairs):
+                side_copy(row * pairs + column).wait_send()
+
+    def weight_sent(w, p=0):
         for step in range(1, chips):
-            peer_copy(w, step).wait_send()
+            peer_copy(w, step, p).wait_send()
         for step in range(chips):
-            twin_copy(w, step).wait_send()
+            twin_copy(w, step, p).wait_send()
 
     def unit_place(device, u):
         return (device // local_heads) * units + u, device % local_heads
@@ -403,14 +481,39 @@
         for step in range(1, ctxs):
             context_arrival(u, step).wait_recv()
 
-    weight_start(0)
-    for u in range(units):
+    def project_chunk(c):
+        bring(hidden, c).wait()
+        following = (c + 1) % chunks
+        s = c // per_seq
+        rs = tile(c % per_seq, rows)
+        low = dot_nt(rows_in[...], md[s]).astype(BF)
+        put_rank(3, c, low)
+        rank_buf[...] = low
+        heads_at_once = math.gcd(local_heads, 2)
+        step = heads_at_once * HEAD_DIM
+
+        @pl.loop(0, mix_width // step)
+        def _(i):
+            cs = tile(i, step)
+            values = dot_nn(rows_in[...], stash[0:width, cs]) + dot_nn(rank_buf[...], mu[s, :, cs])
+            values = values.astype(BF)
+            first = i * heads_at_once
+            for k in range(heads_at_once):
+                local_qkv[s, (first + k) % local_heads, (first + k) // local_heads, rs, :] = values[
+                    :, k * HEAD_DIM : (k + 1) * HEAD_DIM
+                ]
+
+        bring(hidden, following).start()
+
+    def project(s):
+        @pl.loop(0, per_seq)
+        def _(i):
+            project_chunk(s * per_seq + i)
+
+    def send_unit(u):
         qkv_own(u).start()
         for step in range(1, ctxs):
             qkv_copy(u, step).start()
-    weight_start(1)
-    weight_start(2)
-    weight_relay(0)
 
     def job_of(number, rounds):
         safe = jnp.maximum(number, 0)
@@ -436,11 +539,35 @@
     def rows_of(c):
         return tile(c, rows)
 
+    def spot(t, c, i=None):
+        start = t * total + c * rows
+        if i is None:
+            return pl.ds(pl.multiple_of(start, rows), rows)
+        return pl.ds(pl.multiple_of(start + i * block, block), block)
+
+    def mixing_keep():
+        return pltpu.make_async_copy(
+            stash.at[pl.ds(0, width), pl.ds(0, mix_width)], mixing, mix_sem
+        )
+
     def bring(source, c):
         return pltpu.make_async_copy(source.at[rows_of(c)], rows_in, in_sem)
 
     def keep(index, source, target, c):
         return pltpu.make_async_copy(source, target.at[rows_of(c)], out_sem.at[index])
+
+    def put_rank(t, c, low):
+        part_ranks[t, :, tile(c, rows)] = dot_nt(unit_rank[...], low).astype(BF)
+
+    def rank_copy(t, step):
+        return pltpu.make_async_remote_copy(
+            src_ref=part_ranks.at[t],
+            dst_ref=rank_in.at[t, step],
+            send_sem=rank_send.at[t, step],
+            recv_sem=rank_recv.at[t, step],
+            device_id={"tensor": (me + step) % ranks},
+            device_id_type=MESH_IDS,
+        )
 
     def mean(values):
         return jnp.sum(values, axis=-1, keepdims=True) * (1.0 / width)
@@ -448,7 +575,7 @@
     def attend_part(c, s):
         mine = context[rows_of(c), :]
         low = dot_nt(mine, od[s]).astype(BF)
-        out_rank[rows_of(c), :] = low
+        put_rank(0, c, low)
 
         @pl.loop(0, width // tile_d)
         def _(i):
@@ -465,12 +592,12 @@
             centred = total - mean(total)
             spread = lax.rsqrt(mean(centred * centred) + 1e-06)
             n = centred * spread
-            normed[c, rs, :] = n.astype(BF)
+            stash[spot(0, c, i), :] = n.astype(BF)
             spreads[c, rs, :] = jnp.broadcast_to(spread, (block, 128))
             stage_d[rs, :] = (n * gains[0:1, :] + gains[1:2, :]).astype(BF)
 
         low = dot_nt(stage_d[...], ed[s]).astype(BF)
-        exp_rank[rows_of(c), :] = low
+        put_rank(4, c, low)
         rank_buf[...] = low
 
         @pl.loop(0, hidden_units // tile_f)
@@ -481,14 +608,14 @@
             t = jnp.tanh(GELU_C * b * (1.0 + GELU_A * square))
             upper = 0.5 * (1.0 + t)
             stage_f[:, cs] = (b * upper).astype(BF)
-            slope[c, :, cs] = (
+            stash[spot(1, c), cs] = (
                 upper
                 + (0.5 * GELU_C) * b * (1.0 - t * t) * (1.0 + (3.0 * GELU_A) * square)
             ).astype(BF)
 
     def forward_second(c, s):
         low = dot_nt(stage_f[...], cd[s]).astype(BF)
-        con_rank[rows_of(c), :] = low
+        put_rank(1, c, low)
         rank_buf[...] = low
 
         @pl.loop(0, width // tile_d)
@@ -507,28 +634,28 @@
         @pl.loop(0, rows // block)
         def _(i):
             rs = tile(i, block)
-            first = normed[c, rs, :].astype(F32) * gains[0:1, :] + gains[1:2, :]
+            first = stash[spot(0, c, i), :].astype(F32) * gains[0:1, :] + gains[1:2, :]
             total = first + acc[c, rs, :].astype(F32)
             centred = total - mean(total)
             spread = lax.rsqrt(mean(centred * centred) + 1e-06)
             n = centred * spread
             stage_d[rs, :] = (n * gains[2:3, :] + gains[3:4, :]).astype(BF)
             g = rows_in[rs, :].astype(F32) * gains[2:3, :]
-            second[c, rs, :] = (spread * (g - mean(g) - n * mean(g * n))).astype(BF)
-
-        low = dot_nt(second[c], cu[s]).astype(BF)
-        con_rank_grad[rows_of(c), :] = low
+            stash[spot(2, c, i), :] = (spread * (g - mean(g) - n * mean(g * n))).astype(BF)
+
+        low = dot_nt(stash[spot(2, c), :], cu[s]).astype(BF)
+        put_rank(5, c, low)
         rank_buf[...] = low
 
         @pl.loop(0, hidden_units // tile_f)
         def _(i):
             cs = tile(i, tile_f)
-            da = dot_nt(second[c], w_con[cs, :]) + dot_nn(rank_buf[...], cd[s, :, cs])
-            stage_f[:, cs] = (da * slope[c, :, cs].astype(F32)).astype(BF)
+            da = dot_nt(stash[spot(2, c), :], w_con[cs, :]) + dot_nn(rank_buf[...], cd[s, :, cs])
+            stage_f[:, cs] = (da * stash[spot(1, c), cs].astype(F32)).astype(BF)
 
     def back_second(c, s):
         low = dot_nt(stage_f[...], eu[s]).astype(BF)
-        exp_rank_grad[rows_of(c), :] = low
+        put_rank(2, c, low)
         rank_buf[...] = low
 
         @pl.loop(0, width // tile_d)
@@ -540,20 +667,20 @@
 
         keep(0, stage_d, hidden_out, c).start()
         keep(1, stage_f, before_grad, c).start()
-        keep(2, second.at[c], second_low, c).start()
+        keep(2, stash.at[spot(2, c)], second_low, c).start()
 
     def last_first(c, s):
         @pl.loop(0, rows // block)
         def _(i):
             rs = tile(i, block)
-            n = normed[c, rs, :].astype(F32)
-            g = (second[c, rs, :].astype(F32) + acc[c, rs, :].astype(F32)) * gains[0:1, :]
+            n = stash[spot(0, c, i), :].astype(F32)
+            g = (stash[spot(2, c, i), :].astype(F32) + acc[c, rs, :].astype(F32)) * gains[0:1, :]
             spread = spreads[c, rs, 0:1]
             stage_d[rs, :] = (spread * (g - mean(g) - n * mean(g * n))).astype(BF)
 
     def last_second(c, s):
         low = dot_nt(stage_d[...], ou[s]).astype(BF)
-        out_rank_grad[rows_of(c), :] = low
+        put_rank(6, c, low)
         rank_buf[...] = low
 
         @pl.loop(0, heads // tile_h)
@@ -564,6 +691,24 @@
             ).astype(BF)
 
         keep(0, stage_d, attn_low, c).start()
+
+    seqs = chunks // per_seq
+    flowing = units == seqs
+    bring(hidden, 0).start()
+    mixing_gather()
+    weight_finish(0)
+    along_start(1)
+    across_start(1)
+    mixing_keep().start()
+    if flowing:
+        for u in range(min(2, units)):
+            project(u)
+            send_unit(u)
+    else:
+        pl.loop(0, seqs)(project)
+        for u in range(units):
+            send_unit(u)
+    weight_relay(1)
 
     @pl.loop(0, lead + 3 * period + chunks)
     def _(now):
@@ -586,25 +731,56 @@
 
         @pl.when(last_valid & (last_stage == 2))
         def _():
-            keep(2, second.at[last_c], second_low, last_c).wait()
-
-        pl.when(now == 1)(lambda: weight_forward(0))
-
-        @pl.when(now == lead + period - 4)
-        def _():
-            weight_relay(1)
-            weight_relay(2)
-
-        pl.when(now == lead + period - 1)(lambda: weight_forward(1))
+            keep(2, stash.at[spot(2, last_c)], second_low, last_c).wait()
+
+        pl.when(now == 1)(lambda: weight_forward(1))
+        if flowing:
+
+            @pl.when((now % per_seq == 0) & (now < (units - 2) * per_seq))
+            def _():
+                project(now // per_seq + 2)
+                send_unit(now // per_seq + 2)
+
+        @pl.when((now % per_seq == 0) & (now > 0) & (now <= PIECES * per_seq))
+        def _():
+            p = now // per_seq - 1
+            weight_relay(2, p)
+            weight_relay(3, p)
+
+        @pl.when((now % per_seq == 0) & (now < PIECES * per_seq))
+        def _():
+            for w in (2, 3):
+                along_start(w, now // per_seq)
+                across_start(w, now // per_seq)
+
+        @pl.when((now % per_seq == 1 % per_seq) & (now > per_seq) & (now <= PIECES * per_seq + 1))
+        def _():
+            p = (now - 1) // per_seq - 1
+            weight_forward(2, p)
+            weight_forward(3, p)
 
         @pl.when(now == lead + period)
         def _():
-            weight_forward(2)
-            weight_finish(1)
-            weight_finish(2)
+            for p in range(PIECES):
+                weight_finish(2, p)
+                weight_finish(3, p)
 
         pl.when((now % per_seq == 0) & (now < units * per_seq))(lambda: attend(now // per_seq))
-        pl.when(now == lead)(lambda: weight_finish(0))
+        pl.when(now == lead)(lambda: weight_finish(1))
+
+        @pl.when(now == lead + period - 2)
+        def _():
+            mixing_keep().wait()
+            weight_sent(0)
+            side_sent()
+
+        for t in range(3):
+
+            @pl.when(tick == (t + 1) * period)
+            def _(t=t):
+                for step in range(1, ranks):
+                    rank_copy(t, step).start()
+
         pl.when((tick >= 0) & (tick % per_seq == 0) & (tick < units * per_seq))(
             lambda: context_ready(s)
         )
@@ -622,44 +798,46 @@
 
         next_valid, next_c = job_of(tick + 1, 4)
         next_stage = jnp.maximum(tick + 1, 0) // period
-        pl.when(next_valid & (next_stage == 1))(lambda: bring(hidden, next_c).start())
+        pl.when(next_valid & (next_stage == 1) & (next_c > 0))(
+            lambda: bring(hidden, next_c).start()
+        )
         pl.when(next_valid & (next_stage == 2))(lambda: bring(cotangent, next_c).start())
 
     keep(0, stage_d, attn_low, chunks - 1).wait()
-    for w in range(3):
-        weight_sent(w)
+    for t in range(3):
+        value = part_ranks[t].astype(F32)
+        for step in range(1, ranks):
+            rank_copy(t, step).wait_recv()
+            value = value + rank_in[t, step].astype(F32)
+        full_ranks[t] = value.astype(BF)
+    for t in range(3):
+        for step in range(1, ranks):
+            rank_copy(t, step).wait_send()
+    weight_sent(1)
+    for p in range(PIECES):
+        weight_sent(2, p)
+        weight_sent(3, p)
     for u in range(units):
         for step in range(1, ctxs):
             qkv_copy(u, step).wait_send()
             context_copy(u, step).wait_send()
 
 
-def enter(me, ranks, others):
+def enter(others):
     barrier = pltpu.get_barrier_semaphore()
-
-    @pl.when(me > 0)
-    def _():
-        pl.semaphore_signal(barrier, inc=1, device_id={"tensor": me - 1}, device_id_type=MESH_IDS)
-
-    @pl.when(me < ranks - 1)
-    def _():
-        pl.semaphore_signal(barrier, inc=1, device_id={"tensor": me + 1}, device_id_type=MESH_IDS)
-
     for other in others:
         pl.semaphore_signal(barrier, inc=1, device_id=other, device_id_type=MESH_IDS)
-    pl.semaphore_wait(
-        barrier, len(others) + jnp.minimum(me, 1) + jnp.minimum(ranks - 1 - me, 1)
-    )
-
-
-def middle(local_qkv, hidden, cotangent, shards, picked, gains, tok):
-    od, ou, ed, eu, cd, cu = picked
+    pl.semaphore_wait(barrier, len(others))
+
+
+def middle(hidden, cotangent, shards, picked, gains, tok):
     total, width = hidden.shape
-    heads, hidden_units = shards[0].shape[0], shards[1].shape[1]
+    mix_width = shards[0].shape[1]
+    heads, hidden_units = shards[1].shape[0], shards[2].shape[1]
     ranks, dps, ctxs = (lax.axis_size(name) for name in ("tensor", "dp", "ctx"))
-    seqs, local_heads = local_qkv.shape[:2]
+    seqs, rank = picked[0].shape[:2]
+    local_heads = heads // HEAD_DIM
     units = seqs * local_heads // ctxs
-    rank = od.shape[1]
     rows = math.gcd(tok, CHUNK_ROWS)
     chunks = total // rows
     period = max(chunks, 2 * ranks)
@@ -682,27 +860,27 @@
             shape(total, width),
             shape(total, hidden_units),
             shape(total, width),
+            shape(width, mix_width),
             shape(total, heads),
-        )
-        + (shape(total, rank),) * 6
-        + (
+            shape(7, rank, total),
+            shape(3, rank, total),
             shape(total, heads),
             shape(units, 3, tok * ctxs, HEAD_DIM),
             shape(units, tok * ctxs, HEAD_DIM),
         ),
-        in_specs=[vm, hb, hb, hb, hb, hb] + [vm] * 7,
-        out_specs=(hb,) * 6 + (vm,) * 10,
+        in_specs=[hb] * 6 + [vm] * 10,
+        out_specs=(hb,) * 7 + (vm,) * 6,
         scratch_shapes=[
+            pltpu.VMEM((seqs, local_heads, 3, tok, HEAD_DIM), BF),
             pltpu.VMEM((heads, width), BF),
             pltpu.VMEM((width, hidden_units), BF),
             pltpu.VMEM((hidden_units, width), BF),
             pltpu.VMEM((chunks, rows, width), BF),
             pltpu.VMEM((chunks, half, width), BF),
             pltpu.VMEM((chunks, half, width), BF),
-            pltpu.VMEM((chunks, rows, width), BF),
+            pltpu.VMEM((3 * total, width), BF),
             pltpu.VMEM((chunks, rows, 128), F32),
-            pltpu.VMEM((chunks, rows, hidden_units), BF),
-            pltpu.VMEM((chunks, rows, width), BF),
+            pltpu.VMEM((3, ranks, rank, total), BF),
             pltpu.VMEM((rows, width), BF),
             pltpu.VMEM((rows, hidden_units), BF),
             pltpu.VMEM((rows, width), BF),
@@ -713,11 +891,16 @@
             dma((2, chunks)),
             dma((2, chunks)),
             dma((2, chunks)),
-            dma((3, chips)),
-            dma((3, chips)),
-            dma((3, chips)),
-            dma((3, chips)),
-            dma((3,)),
+            dma((4, chips, PIECES)),
+            dma((4, chips, PIECES)),
+            dma((4, chips, PIECES)),
+            dma((4, chips, PIECES)),
+            dma((chips,)),
+            dma((chips,)),
+            dma((4, PIECES)),
+            dma((3, ranks)),
+            dma((3, ranks)),
+            dma(()),
             dma((units, ctxs)),
             dma((units, ctxs)),
             dma((units, ctxs)),
@@ -732,7 +915,7 @@
             bytes_accessed=16 * total * width,
             transcendentals=total * hidden_units,
         ),
-    )(local_qkv, hidden, cotangent, *shards, od, ou, ed, eu, cd, cu, gains)
+    )(hidden, cotangent, *shards, *picked, gains, jnp.eye(rank, dtype=BF))
 
 
 def mixing_kernel(
@@ -744,9 +927,12 @@
     mu,
     md,
     attn_low,
+    unit_rank,
     input_grad,
     grads,
+    full_rank,
     rank_part,
+    rank_in,
     unit_go,
     unit_grad,
     sum_k,
@@ -768,6 +954,8 @@
     grad_send,
     grad_recv,
     unit_sem,
+    rank_send,
+    rank_recv,
 ):
     ranks, ctxs, chunks, rows, per_seq, group = sizes
     half = rows // 2
@@ -782,7 +970,10 @@
     me = lax.axis_index("tensor")
     ctx = lax.axis_index("ctx")
 
-    enter(me, ranks, [{"ctx": (ctx + d) % ctxs} for d in range(1, ctxs)])
+    enter(
+        [{"tensor": (me + d) % ranks} for d in range(1, ranks)]
+        + [{"ctx": (ctx + d) % ctxs} for d in range(1, ctxs)]
+    )
 
     def unit_place(device, u):
         return (device // local_heads) * units + u, device % local_heads
@@ -909,7 +1100,9 @@
         for j in range(3):
             low = low + dot_nt(grads[j, rs, :], mu[s, :, pl.ds(j * heads, heads)])
         low = low.astype(BF)
-        rank_part[rs, :] = low
+        rank_part[:, pl.ds(pl.multiple_of(c * rows, group * rows), group * rows)] = dot_nt(
+            unit_rank[...], low
+        ).astype(BF)
         rank_buf[...] = low
 
         @pl.loop(0, width // tile_d)
@@ -932,11 +1125,27 @@
 
         keep(c).start()
 
+    def rank_copy(step):
+        return pltpu.make_async_remote_copy(
+            src_ref=rank_part,
+            dst_ref=rank_in.at[step],
+            send_sem=rank_send.at[step],
+            recv_sem=rank_recv.at[step],
+            device_id={"tensor": (me + step) % ranks},
+            device_id_type=MESH_IDS,
+        )
+
     delay = 2 * ranks
 
     @pl.loop(0, per_seq + chunks + delay)
     def _(now):
         tick = now - per_seq
+
+        @pl.when(tick == chunks)
+        def _():
+            for step in range(1, ranks):
+                rank_copy(step).start()
+
         valid, c = job_of(tick)
         final, c_final = job_of(tick - delay)
         before, c_before = job_of(tick - delay - 1)
@@ -958,6 +1167,13 @@
         pl.when(coming)(lambda: bring(c_coming).start())
 
     keep(chunks - 1).wait()
+    value = rank_part[...].astype(F32)
+    for step in range(1, ranks):
+        rank_copy(step).wait_recv()
+        value = value + rank_in[step].astype(F32)
+    full_rank[...] = value.astype(BF)
+    for step in range(1, ranks):
+        rank_copy(step).wait_send()
     for u in range(units):
         for step in range(1, ctxs):
             go_copy(u, step).wait_send()
@@ -986,11 +1202,13 @@
         out_shape=(
             jax.ShapeDtypeStruct((total, width), BF),
             jax.ShapeDtypeStruct((3, total, heads), BF),
-            jax.ShapeDtypeStruct((total, rank), BF),
+            jax.ShapeDtypeStruct((rank, total), BF),
         ),
-        in_specs=[vm] * 6 + [hb],
+        in_specs=[vm] * 6 + [hb, vm],
         out_specs=(hb, vm, vm),
         scratch_shapes=[
+            pltpu.VMEM((rank, total), BF),
+            pltpu.VMEM((ranks, rank, total), BF),
             pltpu.VMEM((units, seq_all, HEAD_DIM), BF),
             pltpu.VMEM((units, 3, seq_all, HEAD_DIM), BF),
             pltpu.VMEM((seq_all, HEAD_DIM), F32),
@@ -1012,6 +1230,8 @@
             dma((units, ctxs)),
             dma((units, ctxs)),
             dma((2, units)),
+            dma((ranks,)),
+            dma((ranks,)),
         ],
         compiler_params=pltpu.CompilerParams(
             collective_id=1, has_side_effects=True, vmem_limit_bytes=VMEM_LAST
@@ -1021,7 +1241,7 @@
             bytes_accessed=8 * total * width,
             transcendentals=units * seq_all * seq_all,
         ),
-    )(context_grad, unit_qkv, unit_out, mixing, mu, md, attn_low)
+    )(context_grad, unit_qkv, unit_out, mixing, mu, md, attn_low, jnp.eye(rank, dtype=BF))
 
 
 def pick_rows(onehot_low, table):
@@ -1067,22 +1287,8 @@
     contract_up_sel = pick_rows(onehot_low, contract_up)
     rank = mixing_down.shape[1]
     mixing_flat = mixing_weight.reshape(mixing_weight.shape[0], 3 * local_width)
-    mixing_full = lax.all_gather(mixing_flat, ("dp", "ctx"), axis=0, tiled=True)
     hidden_rows = hidden_in.reshape(rows_all, model_width)
-    mixing_rank = jnp.einsum(
-        "std,srd->str", hidden_in, mixing_down_sel, preferred_element_type=jnp.float32
-    ).astype(jnp.bfloat16)
     mixing_up_flat = mixing_up_sel.reshape(seq_count, rank, 3 * local_width)
-    projected = jnp.einsum(
-        "std,df->stf", hidden_in, mixing_full, preferred_element_type=jnp.float32
-    )
-    projected = projected + jnp.einsum(
-        "str,srf->stf", mixing_rank, mixing_up_flat, preferred_element_type=jnp.float32
-    )
-    projected = projected.astype(jnp.bfloat16)
-    local_qkv = projected.reshape(seq_count, tok_count, 3, local_heads, HEAD_DIM).transpose(
-        0, 3, 2, 1, 4
-    )
     gains = jnp.stack([first_gain, first_shift, second_gain, second_shift])
     (
         out_rows,
@@ -1091,22 +1297,20 @@
         second_low,
         before_low,
         attn_low,
+        mixing_full,
         context_grad,
-        output_rank,
-        expand_rank,
-        contract_rank,
-        contract_rank_grad,
-        expand_rank_grad,
-        output_rank_grad,
+        part_ranks,
+        full_ranks,
         context,
         unit_qkv,
         unit_out,
     ) = middle(
-        local_qkv,
         hidden_rows,
         output_cotangent.reshape(rows_all, model_width),
-        (output_weight, expand_weight, contract_weight),
+        (mixing_flat, output_weight, expand_weight, contract_weight),
         (
+            mixing_down_sel,
+            mixing_up_flat,
             output_down_sel,
             output_up_sel,
             expand_down_sel,
@@ -1117,39 +1321,31 @@
         gains,
         tok_count,
     )
+    row_hot = jnp.repeat(onehot_low.T, tok_count, axis=1)
+
+    def table_grad(ranks, values):
+        wide = (row_hot[:, None, :] * ranks[None, :, :]).reshape(-1, rows_all)
+        part = jnp.einsum("kn,nd->kd", wide, values, preferred_element_type=jnp.float32)
+        return part.astype(jnp.bfloat16).reshape(NADAPT, rank, values.shape[1])
+
+    early = (
+        table_grad(part_ranks[6], context),
+        table_grad(full_ranks[0], attn_low),
+        table_grad(full_ranks[2], first_low),
+        table_grad(part_ranks[4], before_low),
+        table_grad(part_ranks[5], active_low),
+        table_grad(full_ranks[1], second_low),
+    )
+    early, context_grad = lax.optimization_barrier((early, context_grad))
     input_rows, grads, mixing_rank_grad = mixing_back(
         context_grad, unit_qkv, unit_out, mixing_full, (mixing_up_flat, mixing_down_sel), attn_low
     )
-    shared = lax.psum(
-        jnp.concatenate([output_rank, contract_rank, expand_rank_grad], axis=1), "tensor"
-    )
-    output_rank, contract_rank, expand_rank_grad = (
-        shared[:, :rank],
-        shared[:, rank : 2 * rank],
-        shared[:, 2 * rank :],
-    )
-    mixing_rank_grad = lax.psum(mixing_rank_grad, "tensor")
-    row_hot = jnp.repeat(onehot_low, tok_count, axis=0)
-
-    def table_grad(ranks, values):
-        wide = (row_hot[:, :, None] * ranks[:, None, :]).reshape(rows_all, -1)
-        part = jnp.einsum("nk,nd->kd", wide, values, preferred_element_type=jnp.float32)
-        return part.astype(jnp.bfloat16).reshape(NADAPT, rank, values.shape[1])
-
-    early = (
-        table_grad(output_rank_grad, context),
-        table_grad(output_rank, attn_low),
-        table_grad(expand_rank_grad, first_low),
-        table_grad(expand_rank, before_low),
-        table_grad(contract_rank_grad, active_low),
-        table_grad(contract_rank, second_low),
-    )
-    mixing_ranks = mixing_rank.reshape(rows_all, rank)
+    early = lax.psum(early, ("dp", "ctx"))
     late = (
         table_grad(mixing_rank_grad, hidden_rows),
-        jnp.stack([table_grad(mixing_ranks, grads[j]) for j in range(3)], axis=2),
+        jnp.stack([table_grad(part_ranks[3], grads[j]) for j in range(3)], axis=2),
     )
-    early = lax.psum(early, ("dp", "ctx"))
+    late, early = lax.optimization_barrier((late, early))
     late = lax.psum(late, ("dp", "ctx"))
     summed = tuple(part.astype(jnp.float32) for part in late + early)
     return (

time: 788 us -> 697 us (0.88)
  waiting for transfers between devices: 109 us -> 50.1 us
  blocking collectives: 26 us -> 0 us
  Pallas kernels: 558 us -> 579 us
  local copies, waits for them, and re-layouts: 32 us -> 17 us
  matrix products: 33.4 us -> 20.3 us
    all_gather x1 -> x0, waiting for transfers between devices: 34.6 us -> none  [per_device(): mixing_full = lax.all_gather(mixing_flat, ('dp', 'ctx'), axis=0, tiled=True)]
    psum x1 -> x0, blocking collectives: 26 us -> none  [per_device(): mixing_rank_grad = lax.psum(mixing_rank_grad, 'tensor')]
    psum x1, waiting for transfers between devices: 74.6 us -> 50 us  [per_device(): late = lax.psum(late, ('dp', 'ctx'))]
    dot_general x13 -> x10, matrix products: 29 us -> 13.4 us  [table_grad(): jnp.einsum('kn,nd->kd', wide, values, preferred_element_type=jnp.float32)]
    pallas_call x1, Pallas kernels: 145 us -> 161 us  [mixing_back(): pl.pallas_call(functools.partial(mixing_kernel, sizes), out_shape=(jax.Sh...]
  transfers between devices with their start and end apart: 3 -> 2, of which waited for: 2 -> 1; matrix products, arithmetic and copies ran while one was open for 2% -> 2% of each run, Pallas kernels for 18% -> 23%
where the time goes in v3:
time: 697 us; the launch traced here: 696 us
  Pallas kernels  579 us (83%)
  waiting for transfers between devices  50.1 us (7%)
  matrix products  20.3 us (3%)
  local copies, waits for them, and re-layouts  17 us (2%)
  other arithmetic  15.2 us (2%)
  between operations  14.4 us (2%)
    pallas_call x1, Pallas kernels, middle(): pl.pallas_call(functools.partial(middle_kernel, sizes), out_shape=(shape(...  419 us
    pallas_call x1, Pallas kernels, mixing_back(): pl.pallas_call(functools.partial(mixing_kernel, sizes), out_shape=(jax.Sh...  161 us
    psum x1, waiting for transfers between devices, per_device(): late = lax.psum(late, ('dp', 'ctx'))  50 us
  transfers between devices with their start and end apart: 2, of which 1 were waited for; matrix products, arithmetic and copies ran while one was open for 2% of the time, Pallas kernels for 23%

profile of v3, /device:TPU:0, one launch (start us, length us, event | category | flops | bytes accessed | tf_op | source)
XLA Modules:
  0.0 696.5 jit_solution(18081644341981905641)
XLA Ops:
  7.2 0.0 copy-start
  7.2 0.0 copy-start.24
  7.2 0.0 all-reduce.7.cloned.1.call-start
  7.3 0.6 fusion.21.unit_rank
  7.9 0.7 fusion.22
  8.5 1.4 convolution_convert_fusion.6
  9.9 0.1 copy.53
  10.0 0.0 copy-start.23
  10.0 0.9 reshape.124.mu
  11.0 1.2 fusion.16
  12.2 0.9 copy.100.md
  13.1 1.5 fusion.6
  14.6 0.9 copy.95.cu
  15.5 0.0 copy-start.28
  15.5 1.2 fusion.8
  16.6 0.9 copy.96.cd
  17.5 0.0 copy-done.19
  17.5 0.5 fusion.10
  18.0 0.9 copy.97.eu
  18.8 0.5 fusion.12
  19.3 0.9 copy.98.ed
  20.2 0.5 fusion.14
  20.6 0.9 copy.99.ou
  21.5 0.0 copy-done.23
  21.5 0.2 fusion.19
  21.7 0.6 copy.101.od
  22.4 0.3 copy.49
  22.6 1.2 copy.66.shard_mix
  23.8 0.1 broadcast_bitcast_fusion
  23.9 0.0 copy-done.25
  23.9 0.0 copy-done.26
  23.9 0.0 copy-done.27
  23.9 0.7 pad_maximum_fusion.1.gains
  24.6 418.5 %shard_map.258 = (bf16[1024,2048]{1,0:T(8,128)(2,1)}, bf16[1024,2048]{1,0:T(8,128)(2,1)}, bf16[1024,2048]{1,0:T(8,128)(2,1)}, bf16[1024,2048]{1,0:T(8,128)(2,1)}...) custom-call(bf16[1024,2048]{1,0:T(8,128)(2,1)} %bitcast.91, ...), custom_call_target="tpu_custom_call" | custom-call | flops 38654705664 | bytes 33554432 | tf_op jit(solution)/shard_map/pallas_call | solution.py:854
  443.1 1.0 slice_bitcast_fusion
  444.1 0.1 broadcast_multiply_fusion
  444.3 3.9 convolution_convert_fusion.1
  448.2 1.5 convolution_convert_fusion.2
  449.7 1.5 convolution_convert_fusion.3
  451.3 1.5 convolution_convert_fusion.4
  452.8 1.5 convolution_convert_fusion.5
  454.4 1.0 convolution_convert_fusion.10
  455.3 0.0 all-reduce.7.cloned.1.call-update
  455.4 0.0 all-reduce.5.cloned.1.call-start
  455.5 160.9 %shard_map.259 = (bf16[1024,2048]{1,0:T(8,128)(2,1)}, bf16[3,1024,512]{2,1,0:T(8,128)(2,1)S(1)}, bf16[16,1024]{1,0:T(8,128)(2,1)S(1)}) custom-call(bf16[1024,512]{1,0:T(8,128)(2,1)S(1)} %copy-done.5, bf16[4,3,1024,128]{3,2,1,0:T(8,128)(2,1)} %get-tuple-element.52.unit_qkv, bf16[4,1024,128]{2,1,0:T(8,128)(2,1)S(1)} %copy-done.6, ...), custom_call_target="tpu_custom_call" | custom-call | flops 11811160064 | bytes 16777216 | tf_op jit(solution)/shard_map/pallas_call | solution.py:1200
  616.3 0.0 copy-start.7
  616.3 0.3 convolution_convert_fusion.9
  616.7 0.3 convolution_convert_fusion.8
  617.0 0.3 convolution_convert_fusion.7
  617.3 0.8 pad_maximum_fusion
  618.1 0.6 copy-done.7
  618.7 1.5 convolution_convert_fusion
  620.2 0.0 all-reduce.5.cloned.1.call-update
  620.2 2.2 convert_element_type.111
  622.5 2.1 convert_element_type.112
  624.6 1.1 convert_element_type.113
  625.7 1.1 convert_element_type.114
  626.7 1.1 convert_element_type.115
  627.8 0.7 convert_element_type.110
  628.5 50.0 %all-reduce.5.cloned.1.call-done = (bf16[8,16,2048]{2,1,0:T(8,128)(2,1)}, bf16[8,16,3,512]{3,1,2,0:T(8,128)(2,1)}) async-done(((bf16[8,16,2048]{2,1,0:T(8,128)(2,1)}, bf16[8,16,3,512]{3,1,2,0:T(8,128)(2,1)}), (bf16[8,16,2048]{2,1,0:T(8,128)(2,1)}, bf16[8,16,3,512]{3,1,2,0:T(8,128)(2,1)})) %all-reduce.5.cloned.1.call-update) | async-done | bytes 917520 | tf_op jit(solution)/shard_map/psum | solution.py:1349
  678.6 2.1 convert_element_type.108
  680.7 2.0 convert_element_type.109
  682.7 4.9 copy.112
  687.6 2.0 copy.113
  (50 shorter events, 0.1 us)
Async XLA Ops:
  7.2 3.8 copy-start
  7.2 10.3 %copy-start.24 = (s32[4,1]{0,1:T(1,128)S(1)}, s32[4,1]{0,1:T(1,128)}, u32[]{:S(2)}) copy-start(s32[4,1]{0,1:T(1,128)} %param.21) | copy-start | bytes 52
  7.2 8.2 %copy-start.18 = (bf16[8,16,2048]{2,1,0:T(8,128)(2,1)S(1)}, bf16[8,16,2048]{2,1,0:T(8,128)(2,1)}, u32[]{:S(2)}) copy-start(bf16[8,16,2048]{2,1,0:T(8,128)(2,1)} %param.36) | copy-start | bytes 1572868
  7.2 10.3 %copy-start.19 = (bf16[8,16,2048]{2,1,0:T(8,128)(2,1)S(1)}, bf16[8,16,2048]{2,1,0:T(8,128)(2,1)}, u32[]{:S(2)}) copy-start(bf16[8,16,2048]{2,1,0:T(8,128)(2,1)} %param.35) | copy-start | bytes 1572868
  7.2 11.6 %copy-start.20 = (bf16[8,16,2048]{2,1,0:T(8,128)(2,1)S(1)}, bf16[8,16,2048]{2,1,0:T(8,128)(2,1)}, u32[]{:S(2)}) copy-start(bf16[8,16,2048]{2,1,0:T(8,128)(2,1)} %param.34) | copy-start | bytes 1572868
  7.2 613.0 %all-reduce.7.cloned.1.call-start = ((), (), s32[]{:S(2)}) async-start(), calls=%async_computation.1 | async-start | bytes 5505024 | tf_op jit(solution)/shard_map/psum | solution.py:1343
  10.0 11.5 %copy-start.23 = (bf16[8,16,512]{2,1,0:T(8,128)(2,1)S(1)}, bf16[8,16,512]{2,1,0:T(8,128)(2,1)}, u32[]{:S(2)}) copy-start(bf16[8,16,512]{2,1,0:T(8,128)(2,1)} %param.32) | copy-start | bytes 393220
  11.0 9.2 %copy-start.21 = (bf16[8,16,2048]{2,1,0:T(8,128)(2,1)S(1)}, bf16[8,16,2048]{2,1,0:T(8,128)(2,1)}, u32[]{:S(2)}) copy-start(bf16[8,16,2048]{2,1,0:T(8,128)(2,1)} %param.33) | copy-start | bytes 1572868
  11.0 11.4 %copy-start.14 = (bf16[256,3,512]{2,0,1:T(8,128)(2,1)S(1)}, bf16[256,3,512]{2,0,1:T(8,128)(2,1)}, u32[]{:S(2)}) copy-start(bf16[256,3,512]{2,0,1:T(8,128)(2,1)} %param.22) | copy-start | bytes 2359300
  15.5 8.4 %copy-start.25 = (f32[2048]{0:T(1024)S(1)}, f32[2048]{0:T(1024)}, u32[]{:S(2)}) copy-start(f32[2048]{0:T(1024)} %param.29) | copy-start | bytes 24580
  15.5 8.4 %copy-start.26 = (f32[2048]{0:T(1024)S(1)}, f32[2048]{0:T(1024)}, u32[]{:S(2)}) copy-start(f32[2048]{0:T(1024)} %param.28) | copy-start | bytes 24580
  15.5 8.4 %copy-start.27 = (f32[2048]{0:T(1024)S(1)}, f32[2048]{0:T(1024)}, u32[]{:S(2)}) copy-start(f32[2048]{0:T(1024)} %param.27) | copy-start | bytes 24580
  15.5 8.4 %copy-start.28 = (f32[2048]{0:T(1024)S(1)}, f32[2048]{0:T(1024)}, u32[]{:S(2)}) copy-start(f32[2048]{0:T(1024)} %param.26) | copy-start | bytes 24580
  443.1 5.1 copy-start.11
  444.3 5.5 copy-start.10
  448.2 3.1 copy-start.9
  449.7 3.1 copy-start.8
  451.3 3.1 copy-start.13
  452.8 2.6 copy-start.2
  452.8 2.6 copy-start.3
  452.8 2.6 copy-start.4
  452.8 2.6 copy-start.5
  452.8 2.6 copy-start.6
  455.4 223.2 %all-reduce.5.cloned.1.call-start = ((), (), s32[]{:S(2)}) async-start(), calls=%async_computation | async-start | bytes 1835008 | tf_op jit(solution)/shard_map/psum | solution.py:1349
  616.3 2.3 copy-start.7
  620.2 4.4 copy-start.17
  620.2 5.5 copy-start.16
  620.2 6.5 copy-start.15
  620.2 7.6 %copy-start.22 = (bf16[8,16,512]{2,1,0:T(8,128)(2,1)S(1)}, bf16[8,16,512]{2,1,0:T(8,128)(2,1)}, u32[]{:S(2)}) copy-start(bf16[8,16,512]{2,1,0:T(8,128)(2,1)} %get-tuple-element.66) | copy-start | bytes 393220
  682.7 4.9 copy-start.12
  682.7 7.0 copy-start.1
Sparse Core Ops, SparseCore 0:
  455.5 87.5 all-reduce.6
  620.4 58.1 all-reduce.4

commit v4 on v3

--- a/solution.py
+++ b/solution.py
@@ -928,11 +928,17 @@
     md,
     attn_low,
     unit_rank,
+    hidden,
+    mix_rank,
+    row_hot,
     input_grad,
     grads,
-    full_rank,
+    table_sum,
     rank_part,
     rank_in,
+    wide,
+    table_part,
+    table_in,
     unit_go,
     unit_grad,
     sum_k,
@@ -956,8 +962,12 @@
     unit_sem,
     rank_send,
     rank_recv,
+    part_send,
+    part_recv,
+    whole_send,
+    whole_recv,
 ):
-    ranks, ctxs, chunks, rows, per_seq, group = sizes
+    ranks, dps, ctxs, chunks, rows, per_seq, group = sizes
     half = rows // 2
     width = mixing.shape[0]
     heads = grads.shape[2]
@@ -969,10 +979,21 @@
     scale = HEAD_DIM ** (-0.5)
     me = lax.axis_index("tensor")
     ctx = lax.axis_index("ctx")
+    dp = lax.axis_index("dp")
+    parts = dps * ctxs
+    index = dp * ctxs + ctx
+    rank = mu.shape[1]
+    tables, _, part_width = table_part.shape
+    segments = parts // NADAPT
+    tile_g = math.gcd(part_width, 256)
+
+    def part_place(step):
+        other = (index + step) % parts
+        return {"dp": other // ctxs, "ctx": other % ctxs}
 
     enter(
         [{"tensor": (me + d) % ranks} for d in range(1, ranks)]
-        + [{"ctx": (ctx + d) % ctxs} for d in range(1, ctxs)]
+        + [part_place(d) for d in range(1, parts)]
     )
 
     def unit_place(device, u):
@@ -1135,6 +1156,78 @@
             device_id_type=MESH_IDS,
         )
 
+    def part_copy(step):
+        return pltpu.make_async_remote_copy(
+            src_ref=table_part.at[(index + step) % parts],
+            dst_ref=table_in.at[step],
+            send_sem=part_send.at[step],
+            recv_sem=part_recv.at[step],
+            device_id=part_place(step),
+            device_id_type=MESH_IDS,
+        )
+
+    def whole_copy(step):
+        return pltpu.make_async_remote_copy(
+            src_ref=table_sum.at[index],
+            dst_ref=table_sum.at[index],
+            send_sem=whole_send.at[step],
+            recv_sem=whole_recv.at[step],
+            device_id=part_place(step),
+            device_id_type=MESH_IDS,
+        )
+
+    def whole_arrival(step):
+        return pltpu.make_async_remote_copy(
+            src_ref=table_sum.at[index],
+            dst_ref=table_sum.at[(index + parts - step) % parts],
+            send_sem=whole_send.at[step],
+            recv_sem=whole_recv.at[step],
+            device_id=part_place(step),
+            device_id_type=MESH_IDS,
+        )
+
+    def put_table(column, values):
+        segment = column // part_width
+        cs = pl.ds(pl.multiple_of(column % part_width, tile_g), tile_g)
+        for n in range(NADAPT):
+            table_part[n * segments + segment, :, cs] = values[n * rank : (n + 1) * rank, :].astype(
+                BF
+            )
+
+    def make_tables():
+        value = rank_part[...].astype(F32)
+        for step in range(1, ranks):
+            rank_copy(step).wait_recv()
+            value = value + rank_in[step].astype(F32)
+        for n in range(NADAPT):
+            hot = row_hot[n : n + 1, :]
+            wide[0, pl.ds(n * rank, rank), :] = (value * hot).astype(BF)
+            wide[1, pl.ds(n * rank, rank), :] = (mix_rank[...].astype(F32) * hot).astype(BF)
+
+        @pl.loop(0, width // tile_g)
+        def _(i):
+            put_table(i * tile_g, dot_nn(wide[0], hidden[:, tile(i, tile_g)]))
+
+        for j in range(3):
+
+            @pl.loop(0, heads // tile_g)
+            def _(i):
+                put_table(
+                    width + j * heads + i * tile_g, dot_nn(wide[1], grads[j, :, tile(i, tile_g)])
+                )
+
+        for step in range(1, parts):
+            part_copy(step).start()
+
+    def sum_tables():
+        value = table_part[index].astype(F32)
+        for step in range(1, parts):
+            part_copy(step).wait_recv()
+            value = value + table_in[step].astype(F32)
+        table_sum[index] = value.astype(BF)
+        for step in range(1, parts):
+            whole_copy(step).start()
+
     delay = 2 * ranks
 
     @pl.loop(0, per_seq + chunks + delay)
@@ -1162,29 +1255,36 @@
 
         pl.when(valid & (tick % group == 0))(lambda: back_part(c, s))
 
+        pl.when(tick == chunks + 1)(make_tables)
+        pl.when(tick == chunks + 4)(sum_tables)
+
         pl.when(before)(lambda: keep(c_before).wait())
         pl.when(final)(lambda: final_part(c_final))
         pl.when(coming)(lambda: bring(c_coming).start())
 
     keep(chunks - 1).wait()
-    value = rank_part[...].astype(F32)
-    for step in range(1, ranks):
-        rank_copy(step).wait_recv()
-        value = value + rank_in[step].astype(F32)
-    full_rank[...] = value.astype(BF)
     for step in range(1, ranks):
         rank_copy(step).wait_send()
+    for step in range(1, parts):
+        whole_arrival(step).wait_recv()
+    for step in range(1, parts):
+        part_copy(step).wait_send()
+        whole_copy(step).wait_send()
     for u in range(units):
         for step in range(1, ctxs):
             go_copy(u, step).wait_send()
             grad_copy(u, step).wait_send()
 
 
-def mixing_back(context_grad, unit_qkv, unit_out, mixing, picked, attn_low):
+def mixing_back(
+    context_grad, unit_qkv, unit_out, mixing, picked, attn_low, hidden, mix_rank, row_hot
+):
     mu, md = picked
     total, width = attn_low.shape
     heads = context_grad.shape[1]
-    ranks, ctxs = (lax.axis_size(name) for name in ("tensor", "ctx"))
+    ranks, dps, ctxs = (lax.axis_size(name) for name in ("tensor", "dp", "ctx"))
+    parts = dps * ctxs
+    part_width = (width + 3 * heads) * NADAPT // parts
     units, _, seq_all, _ = unit_qkv.shape
     tok = seq_all // ctxs
     rank = mu.shape[1]
@@ -1193,7 +1293,7 @@
     per_seq = tok // rows
     group = math.gcd(per_seq, 2)
     half = rows // 2
-    sizes = (ranks, ctxs, chunks, rows, per_seq, group)
+    sizes = (ranks, dps, ctxs, chunks, rows, per_seq, group)
     vm = pl.BlockSpec(memory_space=pltpu.VMEM)
     hb = pl.BlockSpec(memory_space=pl.ANY)
     dma = pltpu.SemaphoreType.DMA
@@ -1202,13 +1302,16 @@
         out_shape=(
             jax.ShapeDtypeStruct((total, width), BF),
             jax.ShapeDtypeStruct((3, total, heads), BF),
-            jax.ShapeDtypeStruct((rank, total), BF),
+            jax.ShapeDtypeStruct((parts, rank, part_width), BF),
         ),
-        in_specs=[vm] * 6 + [hb, vm],
+        in_specs=[vm] * 6 + [hb] + [vm] * 4,
         out_specs=(hb, vm, vm),
         scratch_shapes=[
             pltpu.VMEM((rank, total), BF),
             pltpu.VMEM((ranks, rank, total), BF),
+            pltpu.VMEM((2, NADAPT * rank, total), BF),
+            pltpu.VMEM((parts, rank, part_width), BF),
+            pltpu.VMEM((parts, rank, part_width), BF),
             pltpu.VMEM((units, seq_all, HEAD_DIM), BF),
             pltpu.VMEM((units, 3, seq_all, HEAD_DIM), BF),
             pltpu.VMEM((seq_all, HEAD_DIM), F32),
@@ -1232,6 +1335,10 @@
             dma((2, units)),
             dma((ranks,)),
             dma((ranks,)),
+            dma((parts,)),
+            dma((parts,)),
+            dma((parts,)),
+            dma((parts,)),
         ],
         compiler_params=pltpu.CompilerParams(
             collective_id=1, has_side_effects=True, vmem_limit_bytes=VMEM_LAST
@@ -1241,7 +1348,19 @@
             bytes_accessed=8 * total * width,
             transcendentals=units * seq_all * seq_all,
         ),
-    )(context_grad, unit_qkv, unit_out, mixing, mu, md, attn_low, jnp.eye(rank, dtype=BF))
+    )(
+        context_grad,
+        unit_qkv,
+        unit_out,
+        mixing,
+        mu,
+        md,
+        attn_low,
+        jnp.eye(rank, dtype=BF),
+        hidden,
+        mix_rank,
+        row_hot,
+    )
 
 
 def pick_rows(onehot_low, table):
@@ -1337,16 +1456,23 @@
         table_grad(full_ranks[1], second_low),
     )
     early, context_grad = lax.optimization_barrier((early, context_grad))
-    input_rows, grads, mixing_rank_grad = mixing_back(
-        context_grad, unit_qkv, unit_out, mixing_full, (mixing_up_flat, mixing_down_sel), attn_low
+    input_rows, _, late = mixing_back(
+        context_grad,
+        unit_qkv,
+        unit_out,
+        mixing_full,
+        (mixing_up_flat, mixing_down_sel),
+        attn_low,
+        hidden_rows,
+        part_ranks[3],
+        row_hot.astype(jnp.float32),
     )
     early = lax.psum(early, ("dp", "ctx"))
+    late = late.reshape(NADAPT, -1, rank, late.shape[2]).swapaxes(1, 2).reshape(NADAPT, rank, -1)
     late = (
-        table_grad(mixing_rank_grad, hidden_rows),
-        jnp.stack([table_grad(part_ranks[3], grads[j]) for j in range(3)], axis=2),
+        late[:, :, :model_width],
+        late[:, :, model_width:].reshape(NADAPT, rank, 3, local_width),
     )
-    late, early = lax.optimization_barrier((late, early))
-    late = lax.psum(late, ("dp", "ctx"))
     summed = tuple(part.astype(jnp.float32) for part in late + early)
     return (
         out_rows.reshape(hidden_in.shape),

time: 697 us -> 649 us (0.931)
  waiting for transfers between devices: 50.1 us -> 0.02 us
    psum x1 -> x0, waiting for transfers between devices: 50 us -> none  [per_device(): late = lax.psum(late, ('dp', 'ctx'))]
  transfers between devices with their start and end apart: 2 -> 1, of which waited for: 1 -> 0; matrix products, arithmetic and copies ran while one was open for 2% -> 0% of each run, Pallas kernels for 23% -> 26%
where the time goes in v4:
time: 649 us; the launch traced here: 647 us
  Pallas kernels  585 us (90%)
  matrix products  17.8 us (3%)
  local copies, waits for them, and re-layouts  16.1 us (2%)
  between operations  14.3 us (2%)
  other arithmetic  13.7 us (2%)
    pallas_call x1, Pallas kernels, middle(): pl.pallas_call(functools.partial(middle_kernel, sizes), out_shape=(shape(...  419 us
    pallas_call x1, Pallas kernels, mixing_back(): pl.pallas_call(functools.partial(mixing_kernel, sizes), out_shape=(jax.Sh...  167 us
  transfers between devices with their start and end apart: 1, of which 0 were waited for; matrix products, arithmetic and copies ran while one was open for 0% of the time, Pallas kernels for 26%

profile of v4, /device:TPU:0, one launch (start us, length us, event | category | flops | bytes accessed | tf_op | source)
XLA Modules:
  0.0 647.1 jit_solution(17995842188268227743)
XLA Ops:
  7.2 0.0 copy-start
  7.2 0.0 copy-start.22
  7.2 0.0 copy-start.16
  7.2 0.0 copy-start.17
  7.2 0.0 copy-start.18
  7.2 0.0 all-reduce.3.cloned.1.call-start
  7.3 0.6 fusion.15.unit_rank
  7.9 0.7 fusion.19
  8.6 1.4 convolution_convert_fusion.5
  10.0 0.1 copy.51
  10.1 0.0 copy-start.21
  10.1 0.9 reshape.88.mu
  11.0 0.0 copy-done
  11.1 1.2 fusion.10
  12.3 0.9 copy.97.md
  13.1 1.5 fusion
  14.7 0.9 copy.92.cu
  15.5 0.0 copy-start.26
  15.5 1.2 fusion.2
  16.7 0.9 copy.93.cd
  17.6 0.0 copy-done.17
  17.6 0.5 fusion.4
  18.0 0.9 copy.94.eu
  18.9 0.5 fusion.6
  19.4 0.9 copy.95.ed
  20.2 0.5 fusion.8
  20.7 0.9 copy.96.ou
  21.5 0.2 fusion.13
  21.8 0.6 copy.98.od
  22.4 0.3 copy.47
  22.7 1.2 copy.64.shard_mix
  23.9 0.0 copy-done.23
  23.9 0.0 copy-done.25
  23.9 0.7 pad_maximum_fusion.gains
  24.5 418.5 %shard_map.258 = (bf16[1024,2048]{1,0:T(8,128)(2,1)}, bf16[1024,2048]{1,0:T(8,128)(2,1)}, bf16[1024,2048]{1,0:T(8,128)(2,1)}, bf16[1024,2048]{1,0:T(8,128)(2,1)}...) custom-call(bf16[1024,2048]{1,0:T(8,128)(2,1)} %bitcast.100, ...), custom_call_target="tpu_custom_call" | custom-call | flops 38654705664 | bytes 33554432 | tf_op jit(solution)/shard_map/pallas_call | solution.py:854
  443.0 1.0 slice_bitcast_fusion
  444.1 0.1 broadcast_in_dim.4
  444.1 0.1 broadcast_multiply_fusion
  444.3 3.9 convolution_convert_fusion
  448.2 1.5 convolution_convert_fusion.1
  449.7 1.5 convolution_convert_fusion.2
  451.2 0.0 copy-done.8
  451.2 1.5 convolution_convert_fusion.3
  452.8 0.0 copy-done.7
  452.8 0.0 copy-start.5
  452.8 0.0 copy-start.6
  452.8 1.5 convolution_convert_fusion.4
  454.3 0.0 copy-done.13
  454.3 1.0 convolution_convert_fusion.6
  455.3 0.0 all-reduce.3.cloned.1.call-update
  455.4 166.6 %shard_map.259 = (bf16[1024,2048]{1,0:T(8,128)(2,1)}, bf16[3,1024,512]{2,1,0:T(8,128)(2,1)}, bf16[8,16,3584]{2,1,0:T(8,128)(2,1)S(1)}) custom-call(bf16[1024,512]{1,0:T(8,128)(2,1)S(1)} %copy-done.5, bf16[4,3,1024,128]{3,2,1,0:T(8,128)(2,1)} %get-tuple-element.43.unit_qkv, bf16[4,1024,128]{2,1,0:T(8,128)(2,1)S(1)} %copy-done.6, ...), custom_call_target="tpu_custom_call" | custom-call | flops 11811160064 | bytes 16777216 | tf_op jit(solution)/shard_map/pallas_call | solution.py:1300
  622.0 0.1 slice_convert_fusion.1
  622.1 1.0 copy.99
  623.0 1.1 slice_convert_fusion
  624.1 2.3 convert_element_type.103
  626.4 2.1 convert_element_type.104
  628.5 2.1 convert_element_type.105
  630.6 2.1 convert_element_type.106
  632.7 1.1 convert_element_type.107
  633.8 0.7 convert_element_type.102
  634.5 0.0 copy-done.11
  634.5 2.1 copy.108
  636.7 1.6 copy-done.12
  638.2 2.0 copy.109
  (38 shorter events, 0.1 us)
Async XLA Ops:
  7.2 3.9 copy-start
  7.2 10.4 %copy-start.22 = (s32[4,1]{0,1:T(1,128)S(1)}, s32[4,1]{0,1:T(1,128)}, u32[]{:S(2)}) copy-start(s32[4,1]{0,1:T(1,128)} %param.21) | copy-start | bytes 52
  7.2 8.3 %copy-start.16 = (bf16[8,16,2048]{2,1,0:T(8,128)(2,1)S(1)}, bf16[8,16,2048]{2,1,0:T(8,128)(2,1)}, u32[]{:S(2)}) copy-start(bf16[8,16,2048]{2,1,0:T(8,128)(2,1)} %param.36) | copy-start | bytes 1572868
  7.2 10.3 %copy-start.17 = (bf16[8,16,2048]{2,1,0:T(8,128)(2,1)S(1)}, bf16[8,16,2048]{2,1,0:T(8,128)(2,1)}, u32[]{:S(2)}) copy-start(bf16[8,16,2048]{2,1,0:T(8,128)(2,1)} %param.35) | copy-start | bytes 1572868
  7.2 11.7 %copy-start.18 = (bf16[8,16,2048]{2,1,0:T(8,128)(2,1)S(1)}, bf16[8,16,2048]{2,1,0:T(8,128)(2,1)}, u32[]{:S(2)}) copy-start(bf16[8,16,2048]{2,1,0:T(8,128)(2,1)} %param.34) | copy-start | bytes 1572868
  7.2 616.8 %all-reduce.3.cloned.1.call-start = ((), (), s32[]{:S(2)}) async-start(), calls=%async_computation | async-start | bytes 5505024 | tf_op jit(solution)/shard_map/psum | solution.py:1470
  10.1 11.5 %copy-start.21 = (bf16[8,16,512]{2,1,0:T(8,128)(2,1)S(1)}, bf16[8,16,512]{2,1,0:T(8,128)(2,1)}, u32[]{:S(2)}) copy-start(bf16[8,16,512]{2,1,0:T(8,128)(2,1)} %param.32) | copy-start | bytes 393220
  11.0 9.2 %copy-start.19 = (bf16[8,16,2048]{2,1,0:T(8,128)(2,1)S(1)}, bf16[8,16,2048]{2,1,0:T(8,128)(2,1)}, u32[]{:S(2)}) copy-start(bf16[8,16,2048]{2,1,0:T(8,128)(2,1)} %param.33) | copy-start | bytes 1572868
  11.1 11.4 %copy-start.14 = (bf16[256,3,512]{2,0,1:T(8,128)(2,1)S(1)}, bf16[256,3,512]{2,0,1:T(8,128)(2,1)}, u32[]{:S(2)}) copy-start(bf16[256,3,512]{2,0,1:T(8,128)(2,1)} %param.22) | copy-start | bytes 2359300
  15.5 8.3 %copy-start.23 = (f32[2048]{0:T(1024)S(1)}, f32[2048]{0:T(1024)}, u32[]{:S(2)}) copy-start(f32[2048]{0:T(1024)} %param.29) | copy-start | bytes 24580
  15.5 8.3 %copy-start.24 = (f32[2048]{0:T(1024)S(1)}, f32[2048]{0:T(1024)}, u32[]{:S(2)}) copy-start(f32[2048]{0:T(1024)} %param.28) | copy-start | bytes 24580
  15.5 8.3 %copy-start.25 = (f32[2048]{0:T(1024)S(1)}, f32[2048]{0:T(1024)}, u32[]{:S(2)}) copy-start(f32[2048]{0:T(1024)} %param.27) | copy-start | bytes 24580
  15.5 8.3 %copy-start.26 = (f32[2048]{0:T(1024)S(1)}, f32[2048]{0:T(1024)}, u32[]{:S(2)}) copy-start(f32[2048]{0:T(1024)} %param.26) | copy-start | bytes 24580
  443.0 5.1 copy-start.10
  444.3 5.4 copy-start.9
  448.2 3.1 copy-start.8
  449.7 3.1 copy-start.7
  451.2 3.1 copy-start.13
  452.8 2.6 copy-start.2
  452.8 2.6 copy-start.3
  452.8 2.6 copy-start.4
  452.8 2.6 copy-start.5
  452.8 2.6 copy-start.6
  624.1 8.6 %copy-start.15 = (bf16[8,16,2048]{2,1,0:T(8,128)(2,1)S(1)}, bf16[8,16,2048]{2,1,0:T(8,128)(2,1)}, u32[]{:S(2)}) copy-start(bf16[8,16,2048]{2,1,0:T(8,128)(2,1)} %get-tuple-element.79) | copy-start | bytes 1572868
  624.1 9.7 %copy-start.20 = (bf16[8,16,512]{2,1,0:T(8,128)(2,1)S(1)}, bf16[8,16,512]{2,1,0:T(8,128)(2,1)}, u32[]{:S(2)}) copy-start(bf16[8,16,512]{2,1,0:T(8,128)(2,1)} %get-tuple-element.74) | copy-start | bytes 393220
  624.1 10.4 %copy-start.11 = (bf16[1024,2048]{1,0:T(8,128)(2,1)S(1)}, bf16[1024,2048]{1,0:T(8,128)(2,1)}, u32[]{:S(2)}) copy-start(bf16[1024,2048]{1,0:T(8,128)(2,1)} %get-tuple-element.32) | copy-start | bytes 12582916
  634.5 3.7 copy-start.12
  634.5 5.7 copy-start.1
Sparse Core Ops, SparseCore 0:
  455.4 86.0 all-reduce.2

commit v5 on v4

--- a/solution.py
+++ b/solution.py
@@ -11,9 +11,9 @@
 HEAD_DIM = 128
 NADAPT = 8
 CHUNK_ROWS = 128
-LAST_ROWS = 64
+LAST_ROWS = 128
 VMEM_BYTES = 62 * 2**20
-VMEM_LAST = 48 * 2**20
+VMEM_LAST = 56 * 2**20
 PIECES = 4
 
 
@@ -148,6 +148,7 @@
     cu,
     gains,
     unit_rank,
+    picks,
     hidden_out,
     first_low,
     active,
@@ -155,12 +156,13 @@
     before_grad,
     attn_low,
     mixing,
-    context_grad,
+    unit_go,
     part_ranks,
     full_ranks,
     context,
     unit_qkv,
     unit_out,
+    context_grad,
     local_qkv,
     w_out,
     w_exp,
@@ -195,6 +197,8 @@
     qkv_recv,
     ctx_send,
     ctx_recv,
+    go_send,
+    go_recv,
     unit_sem,
 ):
     ranks, dps, ctxs, chunks, rows, per_seq, period = sizes
@@ -456,6 +460,41 @@
             unit_out.at[u, tile(ctx, tok)], context_place(ctx, u), unit_sem.at[1, u]
         )
 
+    def go_copy(u, step):
+        peer = (ctx + step) % ctxs
+        s, h = unit_place(peer, u)
+        return pltpu.make_async_remote_copy(
+            src_ref=context_grad.at[tile(s, tok), tile(h, HEAD_DIM)],
+            dst_ref=unit_go.at[u, tile(ctx, tok)],
+            send_sem=go_send.at[u, step],
+            recv_sem=go_recv.at[u, step],
+            device_id={"ctx": peer},
+            device_id_type=MESH_IDS,
+        )
+
+    def go_arrival(u, step):
+        return pltpu.make_async_remote_copy(
+            src_ref=context_grad.at[tile(0, tok), tile(0, HEAD_DIM)],
+            dst_ref=unit_go.at[u, tile((ctx + ctxs - step) % ctxs, tok)],
+            send_sem=go_send.at[u, step],
+            recv_sem=go_recv.at[u, step],
+            device_id={"ctx": (ctx + step) % ctxs},
+            device_id_type=MESH_IDS,
+        )
+
+    def go_own(u):
+        s, h = unit_place(ctx, u)
+        return pltpu.make_async_copy(
+            context_grad.at[tile(s, tok), tile(h, HEAD_DIM)],
+            unit_go.at[u, tile(ctx, tok)],
+            unit_sem.at[2, u],
+        )
+
+    def go_start(u):
+        for step in range(1, ctxs):
+            go_copy(u, step).start()
+        go_own(u).start()
+
     def attend(u):
         qkv_own(u).wait()
         for step in range(1, ctxs):
@@ -486,7 +525,7 @@
         following = (c + 1) % chunks
         s = c // per_seq
         rs = tile(c % per_seq, rows)
-        low = dot_nt(rows_in[...], md[s]).astype(BF)
+        low = dot_nt(rows_in[...], md[picks[s]]).astype(BF)
         put_rank(3, c, low)
         rank_buf[...] = low
         heads_at_once = math.gcd(local_heads, 2)
@@ -495,7 +534,7 @@
         @pl.loop(0, mix_width // step)
         def _(i):
             cs = tile(i, step)
-            values = dot_nn(rows_in[...], stash[0:width, cs]) + dot_nn(rank_buf[...], mu[s, :, cs])
+            values = dot_nn(rows_in[...], stash[0:width, cs]) + dot_nn(rank_buf[...], mu[picks[s], :, cs])
             values = values.astype(BF)
             first = i * heads_at_once
             for k in range(heads_at_once):
@@ -574,13 +613,13 @@
 
     def attend_part(c, s):
         mine = context[rows_of(c), :]
-        low = dot_nt(mine, od[s]).astype(BF)
+        low = dot_nt(mine, od[picks[s]]).astype(BF)
         put_rank(0, c, low)
 
         @pl.loop(0, width // tile_d)
         def _(i):
             cs = tile(i, tile_d)
-            acc[c, :, cs] = (dot_nn(mine, w_out[:, cs]) + dot_nn(low, ou[s, :, cs])).astype(BF)
+            acc[c, :, cs] = (dot_nn(mine, w_out[:, cs]) + dot_nn(low, ou[picks[s], :, cs])).astype(BF)
 
     def forward_first(c, s):
         bring(hidden, c).wait()
@@ -596,14 +635,14 @@
             spreads[c, rs, :] = jnp.broadcast_to(spread, (block, 128))
             stage_d[rs, :] = (n * gains[0:1, :] + gains[1:2, :]).astype(BF)
 
-        low = dot_nt(stage_d[...], ed[s]).astype(BF)
+        low = dot_nt(stage_d[...], ed[picks[s]]).astype(BF)
         put_rank(4, c, low)
         rank_buf[...] = low
 
         @pl.loop(0, hidden_units // tile_f)
         def _(i):
             cs = tile(i, tile_f)
-            b = dot_nn(stage_d[...], w_exp[:, cs]) + dot_nn(rank_buf[...], eu[s, :, cs])
+            b = dot_nn(stage_d[...], w_exp[:, cs]) + dot_nn(rank_buf[...], eu[picks[s], :, cs])
             square = b * b
             t = jnp.tanh(GELU_C * b * (1.0 + GELU_A * square))
             upper = 0.5 * (1.0 + t)
@@ -614,7 +653,7 @@
             ).astype(BF)
 
     def forward_second(c, s):
-        low = dot_nt(stage_f[...], cd[s]).astype(BF)
+        low = dot_nt(stage_f[...], cd[picks[s]]).astype(BF)
         put_rank(1, c, low)
         rank_buf[...] = low
 
@@ -622,7 +661,7 @@
         def _(i):
             cs = tile(i, tile_d)
             acc[c, :, cs] = (
-                dot_nn(stage_f[...], w_con[:, cs]) + dot_nn(rank_buf[...], cu[s, :, cs])
+                dot_nn(stage_f[...], w_con[:, cs]) + dot_nn(rank_buf[...], cu[picks[s], :, cs])
             ).astype(BF)
 
         keep(0, stage_d, first_low, c).start()
@@ -643,18 +682,18 @@
             g = rows_in[rs, :].astype(F32) * gains[2:3, :]
             stash[spot(2, c, i), :] = (spread * (g - mean(g) - n * mean(g * n))).astype(BF)
 
-        low = dot_nt(stash[spot(2, c), :], cu[s]).astype(BF)
+        low = dot_nt(stash[spot(2, c), :], cu[picks[s]]).astype(BF)
         put_rank(5, c, low)
         rank_buf[...] = low
 
         @pl.loop(0, hidden_units // tile_f)
         def _(i):
             cs = tile(i, tile_f)
-            da = dot_nt(stash[spot(2, c), :], w_con[cs, :]) + dot_nn(rank_buf[...], cd[s, :, cs])
+            da = dot_nt(stash[spot(2, c), :], w_con[cs, :]) + dot_nn(rank_buf[...], cd[picks[s], :, cs])
             stage_f[:, cs] = (da * stash[spot(1, c), cs].astype(F32)).astype(BF)
 
     def back_second(c, s):
-        low = dot_nt(stage_f[...], eu[s]).astype(BF)
+        low = dot_nt(stage_f[...], eu[picks[s]]).astype(BF)
         put_rank(2, c, low)
         rank_buf[...] = low
 
@@ -662,7 +701,7 @@
         def _(i):
             cs = tile(i, tile_d)
             acc[c, :, cs] = (
-                dot_nt(stage_f[...], w_exp[cs, :]) + dot_nn(rank_buf[...], ed[s, :, cs])
+                dot_nt(stage_f[...], w_exp[cs, :]) + dot_nn(rank_buf[...], ed[picks[s], :, cs])
             ).astype(BF)
 
         keep(0, stage_d, hidden_out, c).start()
@@ -679,7 +718,7 @@
             stage_d[rs, :] = (spread * (g - mean(g) - n * mean(g * n))).astype(BF)
 
     def last_second(c, s):
-        low = dot_nt(stage_d[...], ou[s]).astype(BF)
+        low = dot_nt(stage_d[...], ou[picks[s]]).astype(BF)
         put_rank(6, c, low)
         rank_buf[...] = low
 
@@ -687,7 +726,7 @@
         def _(i):
             cs = tile(i, tile_h)
             context_grad[rows_of(c), cs] = (
-                dot_nt(stage_d[...], w_out[cs, :]) + dot_nn(rank_buf[...], od[s, :, cs])
+                dot_nt(stage_d[...], w_out[cs, :]) + dot_nn(rank_buf[...], od[picks[s], :, cs])
             ).astype(BF)
 
         keep(0, stage_d, attn_low, c).start()
@@ -795,6 +834,8 @@
         pl.when(valid & (stage == 1))(lambda: forward_second(c, s))
         pl.when(valid & (stage == 2))(lambda: back_second(c, s))
         pl.when(valid & (stage == 3))(lambda: last_second(c, s))
+        if flowing:
+            pl.when(valid & (stage == 3) & (c % per_seq == per_seq - 1))(lambda: go_start(s))
 
         next_valid, next_c = job_of(tick + 1, 4)
         next_stage = jnp.maximum(tick + 1, 0) // period
@@ -818,9 +859,16 @@
         weight_sent(2, p)
         weight_sent(3, p)
     for u in range(units):
+        if not flowing:
+            go_start(u)
         for step in range(1, ctxs):
             qkv_copy(u, step).wait_send()
             context_copy(u, step).wait_send()
+    for u in range(units):
+        go_own(u).wait()
+        for step in range(1, ctxs):
+            go_arrival(u, step).wait_recv()
+            go_copy(u, step).wait_send()
 
 
 def enter(others):
@@ -830,12 +878,12 @@
     pl.semaphore_wait(barrier, len(others))
 
 
-def middle(hidden, cotangent, shards, picked, gains, tok):
+def middle(hidden, cotangent, shards, picked, gains, tok, picks):
     total, width = hidden.shape
     mix_width = shards[0].shape[1]
     heads, hidden_units = shards[1].shape[0], shards[2].shape[1]
     ranks, dps, ctxs = (lax.axis_size(name) for name in ("tensor", "dp", "ctx"))
-    seqs, rank = picked[0].shape[:2]
+    seqs, rank = picks.shape[0], picked[0].shape[1]
     local_heads = heads // HEAD_DIM
     units = seqs * local_heads // ctxs
     rows = math.gcd(tok, CHUNK_ROWS)
@@ -845,6 +893,7 @@
     chips = dps * ctxs // 2
     vm = pl.BlockSpec(memory_space=pltpu.VMEM)
     hb = pl.BlockSpec(memory_space=pl.ANY)
+    sm = pl.BlockSpec(memory_space=pltpu.SMEM)
     half = rows // 2
     dma = pltpu.SemaphoreType.DMA
 
@@ -861,16 +910,17 @@
             shape(total, hidden_units),
             shape(total, width),
             shape(width, mix_width),
-            shape(total, heads),
+            shape(units, tok * ctxs, HEAD_DIM),
             shape(7, rank, total),
             shape(3, rank, total),
             shape(total, heads),
             shape(units, 3, tok * ctxs, HEAD_DIM),
             shape(units, tok * ctxs, HEAD_DIM),
         ),
-        in_specs=[hb] * 6 + [vm] * 10,
+        in_specs=[hb] * 6 + [vm] * 10 + [sm],
         out_specs=(hb,) * 7 + (vm,) * 6,
         scratch_shapes=[
+            pltpu.VMEM((total, heads), BF),
             pltpu.VMEM((seqs, local_heads, 3, tok, HEAD_DIM), BF),
             pltpu.VMEM((heads, width), BF),
             pltpu.VMEM((width, hidden_units), BF),
@@ -905,7 +955,9 @@
             dma((units, ctxs)),
             dma((units, ctxs)),
             dma((units, ctxs)),
-            dma((2, units)),
+            dma((units, ctxs)),
+            dma((units, ctxs)),
+            dma((3, units)),
         ],
         compiler_params=pltpu.CompilerParams(
             collective_id=0, has_side_effects=True, vmem_limit_bytes=VMEM_BYTES
@@ -915,31 +967,33 @@
             bytes_accessed=16 * total * width,
             transcendentals=total * hidden_units,
         ),
-    )(hidden, cotangent, *shards, *picked, gains, jnp.eye(rank, dtype=BF))
+    )(hidden, cotangent, *shards, *picked, gains, jnp.eye(rank, dtype=BF), picks)
 
 
 def mixing_kernel(
     sizes,
-    context_grad,
+    unit_go,
     unit_qkv,
     unit_out,
-    mixing,
+    mixing_far,
     mu,
     md,
     attn_low,
     unit_rank,
-    hidden,
+    hidden_far,
     mix_rank,
     row_hot,
+    picks,
     input_grad,
+    table_sum,
     grads,
-    table_sum,
+    mixing,
+    hidden,
     rank_part,
     rank_in,
     wide,
     table_part,
     table_in,
-    unit_go,
     unit_grad,
     sum_k,
     sum_v,
@@ -955,8 +1009,7 @@
     red_recv,
     cast_send,
     cast_recv,
-    go_send,
-    go_recv,
+    far_sem,
     grad_send,
     grad_recv,
     unit_sem,
@@ -999,35 +1052,11 @@
     def unit_place(device, u):
         return (device // local_heads) * units + u, device % local_heads
 
-    def go_copy(u, step):
-        peer = (ctx + step) % ctxs
-        s, h = unit_place(peer, u)
-        return pltpu.make_async_remote_copy(
-            src_ref=context_grad.at[tile(s, tok), tile(h, HEAD_DIM)],
-            dst_ref=unit_go.at[u, tile(ctx, tok)],
-            send_sem=go_send.at[u, step],
-            recv_sem=go_recv.at[u, step],
-            device_id={"ctx": peer},
-            device_id_type=MESH_IDS,
-        )
-
-    def go_arrival(u, step):
-        return pltpu.make_async_remote_copy(
-            src_ref=context_grad.at[tile(0, tok), tile(0, HEAD_DIM)],
-            dst_ref=unit_go.at[u, tile((ctx + ctxs - step) % ctxs, tok)],
-            send_sem=go_send.at[u, step],
-            recv_sem=go_recv.at[u, step],
-            device_id={"ctx": (ctx + step) % ctxs},
-            device_id_type=MESH_IDS,
-        )
-
-    def go_own(u):
-        s, h = unit_place(ctx, u)
-        return pltpu.make_async_copy(
-            context_grad.at[tile(s, tok), tile(h, HEAD_DIM)],
-            unit_go.at[u, tile(ctx, tok)],
-            unit_sem.at[0, u],
-        )
+    def mixing_load():
+        return pltpu.make_async_copy(mixing_far, mixing, far_sem.at[0])
+
+    def hidden_load():
+        return pltpu.make_async_copy(hidden_far, hidden, far_sem.at[1])
 
     def grads_place(device, u):
         s, h = unit_place(device, u)
@@ -1056,13 +1085,10 @@
 
     def grad_own(u):
         return pltpu.make_async_copy(
-            unit_grad.at[u, :, tile(ctx, tok)], grads_place(ctx, u), unit_sem.at[1, u]
+            unit_grad.at[u, :, tile(ctx, tok)], grads_place(ctx, u), unit_sem.at[u]
         )
 
     def attend_back(u):
-        go_own(u).wait()
-        for step in range(1, ctxs):
-            go_arrival(u, step).wait_recv()
         part = math.gcd(seq_all, 256)
         sum_k[...] = jnp.zeros_like(sum_k)
         sum_v[...] = jnp.zeros_like(sum_v)
@@ -1094,10 +1120,8 @@
         for step in range(1, ctxs):
             grad_arrival(u, step).wait_recv()
 
-    for u in range(units):
-        go_own(u).start()
-        for step in range(1, ctxs):
-            go_copy(u, step).start()
+    mixing_load().start()
+    hidden_load().start()
 
     def job_of(number):
         return (number >= 0) & (number < chunks), jnp.clip(number, 0, chunks - 1)
@@ -1119,7 +1143,7 @@
         rs = pl.ds(pl.multiple_of(c * rows, group * rows), group * rows)
         low = jnp.zeros((group * rows, mu.shape[1]), F32)
         for j in range(3):
-            low = low + dot_nt(grads[j, rs, :], mu[s, :, pl.ds(j * heads, heads)])
+            low = low + dot_nt(grads[j, rs, :], mu[picks[s], :, pl.ds(j * heads, heads)])
         low = low.astype(BF)
         rank_part[:, pl.ds(pl.multiple_of(c * rows, group * rows), group * rows)] = dot_nt(
             unit_rank[...], low
@@ -1129,7 +1153,7 @@
         @pl.loop(0, width // tile_d)
         def _(i):
             cs = tile(i, tile_d)
-            total = dot_nn(rank_buf[...], md[s, :, cs])
+            total = dot_nn(rank_buf[...], md[picks[s], :, cs])
             for j in range(3):
                 total = total + dot_nt(grads[j, rs, :], mixing[cs, pl.ds(j * heads, heads)])
             total = total.astype(BF)
@@ -1253,9 +1277,14 @@
         )
         comm(tick, 1)
 
+        pl.when(tick == 0)(lambda: mixing_load().wait())
         pl.when(valid & (tick % group == 0))(lambda: back_part(c, s))
 
-        pl.when(tick == chunks + 1)(make_tables)
+        @pl.when(tick == chunks + 1)
+        def _():
+            hidden_load().wait()
+            make_tables()
+
         pl.when(tick == chunks + 4)(sum_tables)
 
         pl.when(before)(lambda: keep(c_before).wait())
@@ -1272,16 +1301,15 @@
         whole_copy(step).wait_send()
     for u in range(units):
         for step in range(1, ctxs):
-            go_copy(u, step).wait_send()
             grad_copy(u, step).wait_send()
 
 
 def mixing_back(
-    context_grad, unit_qkv, unit_out, mixing, picked, attn_low, hidden, mix_rank, row_hot
+    unit_go, unit_qkv, unit_out, mixing, picked, attn_low, hidden, mix_rank, row_hot, picks
 ):
     mu, md = picked
     total, width = attn_low.shape
-    heads = context_grad.shape[1]
+    heads = mixing.shape[1] // 3
     ranks, dps, ctxs = (lax.axis_size(name) for name in ("tensor", "dp", "ctx"))
     parts = dps * ctxs
     part_width = (width + 3 * heads) * NADAPT // parts
@@ -1296,23 +1324,25 @@
     sizes = (ranks, dps, ctxs, chunks, rows, per_seq, group)
     vm = pl.BlockSpec(memory_space=pltpu.VMEM)
     hb = pl.BlockSpec(memory_space=pl.ANY)
+    sm = pl.BlockSpec(memory_space=pltpu.SMEM)
     dma = pltpu.SemaphoreType.DMA
     return pl.pallas_call(
         functools.partial(mixing_kernel, sizes),
         out_shape=(
             jax.ShapeDtypeStruct((total, width), BF),
-            jax.ShapeDtypeStruct((3, total, heads), BF),
             jax.ShapeDtypeStruct((parts, rank, part_width), BF),
         ),
-        in_specs=[vm] * 6 + [hb] + [vm] * 4,
-        out_specs=(hb, vm, vm),
+        in_specs=[vm] * 3 + [hb] + [vm] * 2 + [hb, vm, hb] + [vm] * 2 + [sm],
+        out_specs=(hb, vm),
         scratch_shapes=[
+            pltpu.VMEM((3, total, heads), BF),
+            pltpu.VMEM((width, 3 * heads), BF),
+            pltpu.VMEM((total, width), BF),
             pltpu.VMEM((rank, total), BF),
             pltpu.VMEM((ranks, rank, total), BF),
             pltpu.VMEM((2, NADAPT * rank, total), BF),
             pltpu.VMEM((parts, rank, part_width), BF),
             pltpu.VMEM((parts, rank, part_width), BF),
-            pltpu.VMEM((units, seq_all, HEAD_DIM), BF),
             pltpu.VMEM((units, 3, seq_all, HEAD_DIM), BF),
             pltpu.VMEM((seq_all, HEAD_DIM), F32),
             pltpu.VMEM((seq_all, HEAD_DIM), F32),
@@ -1328,11 +1358,10 @@
             dma((2, chunks)),
             dma((2, chunks)),
             dma((2, chunks)),
+            dma((2,)),
             dma((units, ctxs)),
             dma((units, ctxs)),
-            dma((units, ctxs)),
-            dma((units, ctxs)),
-            dma((2, units)),
+            dma((units,)),
             dma((ranks,)),
             dma((ranks,)),
             dma((parts,)),
@@ -1349,7 +1378,7 @@
             transcendentals=units * seq_all * seq_all,
         ),
     )(
-        context_grad,
+        unit_go,
         unit_qkv,
         unit_out,
         mixing,
@@ -1360,13 +1389,8 @@
         hidden,
         mix_rank,
         row_hot,
+        picks,
     )
-
-
-def pick_rows(onehot_low, table):
-    return jnp.einsum(
-        "sn,n...->s...", onehot_low, table, preferred_element_type=jnp.float32
-    ).astype(jnp.bfloat16)
 
 
 def per_device(
@@ -1396,18 +1420,11 @@
     rows_all = seq_count * tok_count
     adapter_ids = jnp.arange(NADAPT, dtype=jnp.int32)
     onehot_low = (adapter_index == adapter_ids[None, :]).astype(jnp.bfloat16)
-    mixing_down_sel = pick_rows(onehot_low, mixing_down)
-    mixing_up_sel = pick_rows(onehot_low, mixing_up)
-    output_down_sel = pick_rows(onehot_low, output_down)
-    output_up_sel = pick_rows(onehot_low, output_up)
-    expand_down_sel = pick_rows(onehot_low, expand_down)
-    expand_up_sel = pick_rows(onehot_low, expand_up)
-    contract_down_sel = pick_rows(onehot_low, contract_down)
-    contract_up_sel = pick_rows(onehot_low, contract_up)
+    picks = adapter_index.reshape(-1)
     rank = mixing_down.shape[1]
     mixing_flat = mixing_weight.reshape(mixing_weight.shape[0], 3 * local_width)
     hidden_rows = hidden_in.reshape(rows_all, model_width)
-    mixing_up_flat = mixing_up_sel.reshape(seq_count, rank, 3 * local_width)
+    mixing_up_flat = mixing_up.reshape(NADAPT, rank, 3 * local_width)
     gains = jnp.stack([first_gain, first_shift, second_gain, second_shift])
     (
         out_rows,
@@ -1417,7 +1434,7 @@
         before_low,
         attn_low,
         mixing_full,
-        context_grad,
+        unit_go,
         part_ranks,
         full_ranks,
         context,
@@ -1428,17 +1445,18 @@
         output_cotangent.reshape(rows_all, model_width),
         (mixing_flat, output_weight, expand_weight, contract_weight),
         (
-            mixing_down_sel,
+            mixing_down,
             mixing_up_flat,
-            output_down_sel,
-            output_up_sel,
-            expand_down_sel,
-            expand_up_sel,
-            contract_down_sel,
-            contract_up_sel,
+            output_down,
+            output_up,
+            expand_down,
+            expand_up,
+            contract_down,
+            contract_up,
         ),
         gains,
         tok_count,
+        picks,
     )
     row_hot = jnp.repeat(onehot_low.T, tok_count, axis=1)
 
@@ -1455,17 +1473,18 @@
         table_grad(part_ranks[5], active_low),
         table_grad(full_ranks[1], second_low),
     )
-    early, context_grad = lax.optimization_barrier((early, context_grad))
-    input_rows, _, late = mixing_back(
-        context_grad,
+    early, unit_go = lax.optimization_barrier((early, unit_go))
+    input_rows, late = mixing_back(
+        unit_go,
         unit_qkv,
         unit_out,
         mixing_full,
-        (mixing_up_flat, mixing_down_sel),
+        (mixing_up_flat, mixing_down),
         attn_low,
         hidden_rows,
         part_ranks[3],
         row_hot.astype(jnp.float32),
+        picks,
     )
     early = lax.psum(early, ("dp", "ctx"))
     late = late.reshape(NADAPT, -1, rank, late.shape[2]).swapaxes(1, 2).reshape(NADAPT, rank, -1)

time: 649 us -> 627 us (0.966)
  Pallas kernels: 585 us -> 569 us
  matrix products: 17.8 us -> 10.9 us
    pallas_call x1, Pallas kernels: 167 us -> 148 us  [mixing_back(): pl.pallas_call(functools.partial(mixing_kernel, sizes), out_shape=(jax.Sh...]
    dot_general x8 -> x0, matrix products: 6.89 us -> none  [pick_rows(): jnp.einsum('sn,n...->s...', onehot_low, table, preferred_element_type=jnp...]
  transfers between devices with their start and end apart: 1 -> 1, of which waited for: 0 -> 0; matrix products, arithmetic and copies ran while one was open for 0% -> 1% of each run, Pallas kernels for 26% -> 24%
where the time goes in v5:
time: 627 us; the launch traced here: 624 us
  Pallas kernels  569 us (91%)
  other arithmetic  17.1 us (3%)
  between operations  14.1 us (2%)
  local copies, waits for them, and re-layouts  12.7 us (2%)
  matrix products  10.9 us (2%)
    pallas_call x1, Pallas kernels, middle(): pl.pallas_call(functools.partial(middle_kernel, sizes), out_shape=(shape(...  421 us
    pallas_call x1, Pallas kernels, mixing_back(): pl.pallas_call(functools.partial(mixing_kernel, sizes), out_shape=(jax.Sh...  148 us
    convert_element_type x8, other arithmetic, per_device(): summed = tuple((part.astype(jnp.float32) for part in late + early))  13.6 us
  transfers between devices with their start and end apart: 1, of which 0 were waited for; matrix products, arithmetic and copies ran while one was open for 1% of the time, Pallas kernels for 24%

profile of v5, /device:TPU:0, one launch (start us, length us, event | category | flops | bytes accessed | tf_op | source)
XLA Modules:
  0.0 624.0 jit_solution(6418173393836186972)
XLA Ops:
  7.2 0.0 all-reduce.3.cloned.1.call-start
  7.2 0.6 fusion.unit_rank
  7.8 1.8 copy.37
  9.6 1.4 copy.32
  11.0 1.2 copy.34.shard_mix
  12.1 0.7 fusion.1
  12.9 1.4 pad_maximum_fusion.gains
  14.3 420.7 %shard_map.258 = (bf16[1024,2048]{1,0:T(8,128)(2,1)}, bf16[1024,2048]{1,0:T(8,128)(2,1)}, bf16[1024,2048]{1,0:T(8,128)(2,1)}, bf16[1024,2048]{1,0:T(8,128)(2,1)}...) custom-call(bf16[1024,2048]{1,0:T(8,128)(2,1)} %bitcast.82, ...), custom_call_target="tpu_custom_call" | custom-call | flops 38654705664 | bytes 33554432 | tf_op jit(solution)/shard_map/pallas_call | solution.py:903
  434.9 0.0 copy-start.3
  435.0 1.6 slice_bitcast_fusion
  436.6 0.1 broadcast_in_dim.4
  436.7 0.1 broadcast_multiply_fusion
  436.8 0.0 copy-start.2
  436.8 3.9 convolution_convert_fusion
  440.7 0.0 copy-done.3
  440.7 0.0 copy-start.1
  440.7 1.5 convolution_convert_fusion.1
  442.2 0.0 copy-done.2
  442.2 0.0 copy-start
  442.2 1.5 convolution_convert_fusion.2
  443.7 0.0 copy-done.1
  443.7 0.0 copy-start.6
  443.7 1.5 convolution_convert_fusion.3
  445.3 0.0 copy-done
  445.3 1.5 convolution_convert_fusion.4
  446.8 0.0 copy-done.6
  446.8 1.0 convolution_convert_fusion.5
  447.8 0.0 all-reduce.3.cloned.1.call-update
  447.8 0.6 convert_element_type.66.row_hot
  448.4 148.4 %shard_map.259 = (bf16[1024,2048]{1,0:T(8,128)(2,1)}, bf16[8,16,3584]{2,1,0:T(8,128)(2,1)}) custom-call(bf16[4,1024,128]{2,1,0:T(8,128)(2,1)} %get-tuple-element.42.unit_go, bf16[4,3,1024,128]{3,2,1,0:T(8,128)(2,1)} %get-tuple-element.43.unit_qkv, bf16[4,1024,128]{2,1,0:T(8,128)(2,1)} %get-tuple-element.44.unit_out, ...), custom_call_target="tpu_custom_call" | custom-call | flops 11811160064 | bytes 16777216 | tf_op jit(solution)/shard_map/pallas_call | solution.py:1329
  596.8 1.1 slice_convert_fusion.1
  597.9 1.0 copy.39
  598.9 2.1 slice_convert_fusion
  601.0 0.0 all-reduce.3.cloned.1.call-done
  601.0 0.0 copy-start.7
  601.0 0.0 copy-start.8
  601.0 0.0 copy-start.4
  601.0 2.3 convert_element_type.71
  603.3 2.1 convert_element_type.72
  605.4 2.1 convert_element_type.73
  607.5 2.1 convert_element_type.74
  609.6 0.0 copy-done.7
  609.6 1.1 convert_element_type.75
  610.7 0.0 copy-done.8
  610.7 0.7 convert_element_type.70
  611.4 0.0 copy-done.4
  611.4 0.0 copy-start.5
  611.4 2.1 copy.48
  613.6 1.6 copy-done.5
  615.1 2.0 copy.49
Async XLA Ops:
  7.2 593.8 %all-reduce.3.cloned.1.call-start = ((), (), s32[]{:S(2)}) async-start(), calls=%async_computation | async-start | bytes 5505024 | tf_op jit(solution)/shard_map/psum | solution.py:1489
  434.9 5.7 copy-start.3
  436.8 5.4 copy-start.2
  440.7 3.1 copy-start.1
  442.2 3.1 copy-start
  443.7 3.1 copy-start.6
  601.0 8.6 %copy-start.7 = (bf16[8,16,2048]{2,1,0:T(8,128)(2,1)S(1)}, bf16[8,16,2048]{2,1,0:T(8,128)(2,1)}, u32[]{:S(2)}) copy-start(bf16[8,16,2048]{2,1,0:T(8,128)(2,1)} %get-tuple-element.79) | copy-start | bytes 1572868
  601.0 9.7 %copy-start.8 = (bf16[8,16,512]{2,1,0:T(8,128)(2,1)S(1)}, bf16[8,16,512]{2,1,0:T(8,128)(2,1)}, u32[]{:S(2)}) copy-start(bf16[8,16,512]{2,1,0:T(8,128)(2,1)} %get-tuple-element.74) | copy-start | bytes 393220
  601.0 10.4 %copy-start.4 = (bf16[1024,2048]{1,0:T(8,128)(2,1)S(1)}, bf16[1024,2048]{1,0:T(8,128)(2,1)}, u32[]{:S(2)}) copy-start(bf16[1024,2048]{1,0:T(8,128)(2,1)} %get-tuple-element.32) | copy-start | bytes 12582916
  611.4 3.7 copy-start.5
Sparse Core Ops, SparseCore 0:
  447.9 82.0 all-reduce.2

commit v6 on v5

--- a/solution.py
+++ b/solution.py
@@ -773,28 +773,29 @@
             keep(2, stash.at[spot(2, last_c)], second_low, last_c).wait()
 
         pl.when(now == 1)(lambda: weight_forward(1))
+        pl.when((now % per_seq == 0) & (now < units * per_seq))(lambda: attend(now // per_seq))
         if flowing:
 
-            @pl.when((now % per_seq == 0) & (now < (units - 2) * per_seq))
+            @pl.when((now % per_seq == 1) & (now < (units - 2) * per_seq))
             def _():
                 project(now // per_seq + 2)
                 send_unit(now // per_seq + 2)
 
-        @pl.when((now % per_seq == 0) & (now > 0) & (now <= PIECES * per_seq))
+        @pl.when((now % per_seq == 1) & (now > per_seq) & (now <= PIECES * per_seq + 1))
         def _():
             p = now // per_seq - 1
             weight_relay(2, p)
             weight_relay(3, p)
 
-        @pl.when((now % per_seq == 0) & (now < PIECES * per_seq))
+        @pl.when((now % per_seq == 1) & (now < PIECES * per_seq))
         def _():
             for w in (2, 3):
                 along_start(w, now // per_seq)
                 across_start(w, now // per_seq)
 
-        @pl.when((now % per_seq == 1 % per_seq) & (now > per_seq) & (now <= PIECES * per_seq + 1))
-        def _():
-            p = (now - 1) // per_seq - 1
+        @pl.when((now % per_seq == 0) & (now > per_seq) & (now <= (PIECES + 1) * per_seq))
+        def _():
+            p = now // per_seq - 2
             weight_forward(2, p)
             weight_forward(3, p)
 
@@ -804,7 +805,6 @@
                 weight_finish(2, p)
                 weight_finish(3, p)
 
-        pl.when((now % per_seq == 0) & (now < units * per_seq))(lambda: attend(now // per_seq))
         pl.when(now == lead)(lambda: weight_finish(1))
 
         @pl.when(now == lead + period - 2)

time: 627 us -> 619 us (0.987)
  Pallas kernels: 569 us -> 560 us
  transfers between devices with their start and end apart: 1 -> 1, of which waited for: 0 -> 0; matrix products, arithmetic and copies ran while one was open for 1% -> 1% of each run, Pallas kernels for 24% -> 23%
where the time goes in v6:
time: 619 us; the launch traced here: 615 us
  Pallas kernels  560 us (90%)
  other arithmetic  17.1 us (3%)
  between operations  14.1 us (2%)
  local copies, waits for them, and re-layouts  12.7 us (2%)
  matrix products  10.9 us (2%)
    pallas_call x1, Pallas kernels, middle(): pl.pallas_call(functools.partial(middle_kernel, sizes), out_shape=(shape(...  416 us
    pallas_call x1, Pallas kernels, mixing_back(): pl.pallas_call(functools.partial(mixing_kernel, sizes), out_shape=(jax.Sh...  144 us
    convert_element_type x8, other arithmetic, per_device(): summed = tuple((part.astype(jnp.float32) for part in late + early))  13.6 us
  transfers between devices with their start and end apart: 1, of which 0 were waited for; matrix products, arithmetic and copies ran while one was open for 1% of the time, Pallas kernels for 23%

profile of v6, /device:TPU:0, one launch (start us, length us, event | category | flops | bytes accessed | tf_op | source)
XLA Modules:
  0.0 615.1 jit_solution(14751343757780280180)
XLA Ops:
  7.2 0.0 all-reduce.3.cloned.1.call-start
  7.2 0.6 fusion.unit_rank
  7.8 1.8 copy.37
  9.6 1.4 copy.32
  11.0 1.2 copy.34.shard_mix
  12.1 0.7 fusion.1
  12.9 1.4 pad_maximum_fusion.gains
  14.3 415.9 %shard_map.258 = (bf16[1024,2048]{1,0:T(8,128)(2,1)}, bf16[1024,2048]{1,0:T(8,128)(2,1)}, bf16[1024,2048]{1,0:T(8,128)(2,1)}, bf16[1024,2048]{1,0:T(8,128)(2,1)}...) custom-call(bf16[1024,2048]{1,0:T(8,128)(2,1)} %bitcast.82, ...), custom_call_target="tpu_custom_call" | custom-call | flops 38654705664 | bytes 33554432 | tf_op jit(solution)/shard_map/pallas_call | solution.py:903
  430.2 0.0 copy-start.3
  430.2 1.6 slice_bitcast_fusion
  431.9 0.1 broadcast_in_dim.4
  431.9 0.1 broadcast_multiply_fusion
  432.1 0.0 copy-start.2
  432.1 3.9 convolution_convert_fusion
  435.9 0.0 copy-done.3
  436.0 0.0 copy-start.1
  436.0 1.5 convolution_convert_fusion.1
  437.5 0.0 copy-done.2
  437.5 0.0 copy-start
  437.5 1.5 convolution_convert_fusion.2
  439.0 0.0 copy-done.1
  439.0 0.0 copy-start.6
  439.0 1.5 convolution_convert_fusion.3
  440.5 0.0 copy-done
  440.5 1.5 convolution_convert_fusion.4
  442.1 0.0 copy-done.6
  442.1 1.0 convolution_convert_fusion.5
  443.0 0.0 all-reduce.3.cloned.1.call-update
  443.1 0.6 convert_element_type.66.row_hot
  443.7 144.3 %shard_map.259 = (bf16[1024,2048]{1,0:T(8,128)(2,1)}, bf16[8,16,3584]{2,1,0:T(8,128)(2,1)}) custom-call(bf16[4,1024,128]{2,1,0:T(8,128)(2,1)} %get-tuple-element.42.unit_go, bf16[4,3,1024,128]{3,2,1,0:T(8,128)(2,1)} %get-tuple-element.43.unit_qkv, bf16[4,1024,128]{2,1,0:T(8,128)(2,1)} %get-tuple-element.44.unit_out, ...), custom_call_target="tpu_custom_call" | custom-call | flops 11811160064 | bytes 16777216 | tf_op jit(solution)/shard_map/pallas_call | solution.py:1329
  588.0 1.1 slice_convert_fusion.1
  589.1 1.0 copy.39
  590.0 2.1 slice_convert_fusion
  592.1 0.0 all-reduce.3.cloned.1.call-done
  592.1 0.0 copy-start.7
  592.1 0.0 copy-start.8
  592.1 0.0 copy-start.4
  592.2 2.3 convert_element_type.71
  594.4 2.1 convert_element_type.72
  596.5 2.1 convert_element_type.73
  598.7 2.1 convert_element_type.74
  600.8 0.0 copy-done.7
  600.8 1.1 convert_element_type.75
  601.8 0.0 copy-done.8
  601.9 0.7 convert_element_type.70
  602.6 0.0 copy-done.4
  602.6 0.0 copy-start.5
  602.6 2.1 copy.48
  604.7 1.6 copy-done.5
  606.3 2.0 copy.49
Async XLA Ops:
  7.2 585.0 %all-reduce.3.cloned.1.call-start = ((), (), s32[]{:S(2)}) async-start(), calls=%async_computation | async-start | bytes 5505024 | tf_op jit(solution)/shard_map/psum | solution.py:1489
  430.2 5.7 copy-start.3
  432.1 5.4 copy-start.2
  436.0 3.1 copy-start.1
  437.5 3.1 copy-start
  439.0 3.1 copy-start.6
  592.1 8.6 %copy-start.7 = (bf16[8,16,2048]{2,1,0:T(8,128)(2,1)S(1)}, bf16[8,16,2048]{2,1,0:T(8,128)(2,1)}, u32[]{:S(2)}) copy-start(bf16[8,16,2048]{2,1,0:T(8,128)(2,1)} %get-tuple-element.79) | copy-start | bytes 1572868
  592.1 9.7 %copy-start.8 = (bf16[8,16,512]{2,1,0:T(8,128)(2,1)S(1)}, bf16[8,16,512]{2,1,0:T(8,128)(2,1)}, u32[]{:S(2)}) copy-start(bf16[8,16,512]{2,1,0:T(8,128)(2,1)} %get-tuple-element.74) | copy-start | bytes 393220
  592.1 10.4 %copy-start.4 = (bf16[1024,2048]{1,0:T(8,128)(2,1)S(1)}, bf16[1024,2048]{1,0:T(8,128)(2,1)}, u32[]{:S(2)}) copy-start(bf16[1024,2048]{1,0:T(8,128)(2,1)} %get-tuple-element.32) | copy-start | bytes 12582916
  602.6 3.7 copy-start.5
Sparse Core Ops, SparseCore 0:
  443.2 78.0 all-reduce.2

commit v7 on v6

--- a/solution.py
+++ b/solution.py
@@ -15,6 +15,7 @@
 VMEM_BYTES = 62 * 2**20
 VMEM_LAST = 56 * 2**20
 PIECES = 4
+EARLY_AT = 3
 
 
 BF = jnp.bfloat16
@@ -128,6 +129,38 @@
         def _():
             cast_copy(cc).start()
     return comm
+
+
+def attention_back(unit_qkv, unit_go, unit_out, unit_grad, sum_k, sum_v, u, v):
+    seq_all = unit_qkv.shape[2]
+    scale = HEAD_DIM ** (-0.5)
+    part = math.gcd(seq_all, 256)
+    sum_k[...] = jnp.zeros_like(sum_k)
+    sum_v[...] = jnp.zeros_like(sum_v)
+
+    @pl.loop(0, seq_all // part)
+    def _(i):
+        rs = tile(i, part)
+        queries = unit_qkv[u, 0, rs, :]
+        go = unit_go[u, rs, :]
+        scores = dot_nt(queries, unit_qkv[u, 1]) * scale
+        raised = jnp.exp(scores - jnp.max(scores, axis=-1, keepdims=True))
+        probs = raised * (1.0 / jnp.sum(raised, axis=-1, keepdims=True))
+        delta = jnp.sum(
+            go.astype(F32) * unit_out[u, rs, :].astype(F32), axis=-1, keepdims=True
+        )
+        dscores = (probs * (dot_nt(go, unit_qkv[u, 2]) - delta)).astype(BF)
+        unit_grad[v, 0, rs, :] = (scale * dot_nn(dscores, unit_qkv[u, 1])).astype(BF)
+        sum_k[...] += dot_tn(dscores, queries)
+        sum_v[...] += dot_tn(probs.astype(BF), go)
+
+    unit_grad[v, 1] = (scale * sum_k[...]).astype(BF)
+    unit_grad[v, 2] = sum_v[...].astype(BF)
+
+
+def early_units(total, tok, units):
+    rows = math.gcd(tok, CHUNK_ROWS)
+    return int(units == total // tok and tok // rows >= 2 and units >= 2)
 
 
 def middle_kernel(
@@ -157,12 +190,16 @@
     attn_low,
     mixing,
     unit_go,
+    early_grads,
     part_ranks,
     full_ranks,
     context,
     unit_qkv,
     unit_out,
     context_grad,
+    unit_grad,
+    sum_k,
+    sum_v,
     local_qkv,
     w_out,
     w_exp,
@@ -199,6 +236,8 @@
     ctx_recv,
     go_send,
     go_recv,
+    early_send,
+    early_recv,
     unit_sem,
 ):
     ranks, dps, ctxs, chunks, rows, per_seq, period = sizes
@@ -495,6 +534,49 @@
             go_copy(u, step).start()
         go_own(u).start()
 
+    early = early_units(total, tok, units)
+
+    def go_ready(u):
+        go_own(u).wait()
+        for step in range(1, ctxs):
+            go_arrival(u, step).wait_recv()
+
+    def early_place(device):
+        return early_grads.at[:, :, tile(unit_place(device, 0)[1], HEAD_DIM)]
+
+    def early_copy(step):
+        peer = (ctx + step) % ctxs
+        return pltpu.make_async_remote_copy(
+            src_ref=unit_grad.at[0, :, tile(peer, tok)],
+            dst_ref=early_place(ctx),
+            send_sem=early_send.at[step],
+            recv_sem=early_recv.at[step],
+            device_id={"ctx": peer},
+            device_id_type=MESH_IDS,
+        )
+
+    def early_arrival(step):
+        return pltpu.make_async_remote_copy(
+            src_ref=unit_grad.at[0, :, tile(ctx, tok)],
+            dst_ref=early_place((ctx + ctxs - step) % ctxs),
+            send_sem=early_send.at[step],
+            recv_sem=early_recv.at[step],
+            device_id={"ctx": (ctx + step) % ctxs},
+            device_id_type=MESH_IDS,
+        )
+
+    def early_own():
+        return pltpu.make_async_copy(
+            unit_grad.at[0, :, tile(ctx, tok)], early_place(ctx), unit_sem.at[3, 0]
+        )
+
+    def early_back():
+        go_ready(0)
+        attention_back(unit_qkv, unit_go, unit_out, unit_grad, sum_k, sum_v, 0, 0)
+        for step in range(1, ctxs):
+            early_copy(step).start()
+        early_own().start()
+
     def attend(u):
         qkv_own(u).wait()
         for step in range(1, ctxs):
@@ -836,6 +918,8 @@
         pl.when(valid & (stage == 3))(lambda: last_second(c, s))
         if flowing:
             pl.when(valid & (stage == 3) & (c % per_seq == per_seq - 1))(lambda: go_start(s))
+        if early:
+            pl.when(tick == 3 * period + EARLY_AT)(early_back)
 
         next_valid, next_c = job_of(tick + 1, 4)
         next_stage = jnp.maximum(tick + 1, 0) // period
@@ -865,10 +949,15 @@
             qkv_copy(u, step).wait_send()
             context_copy(u, step).wait_send()
     for u in range(units):
-        go_own(u).wait()
+        if u >= early:
+            go_ready(u)
         for step in range(1, ctxs):
-            go_arrival(u, step).wait_recv()
             go_copy(u, step).wait_send()
+    if early:
+        early_own().wait()
+        for step in range(1, ctxs):
+            early_arrival(step).wait_recv()
+            early_copy(step).wait_send()
 
 
 def enter(others):
@@ -911,6 +1000,7 @@
             shape(total, width),
             shape(width, mix_width),
             shape(units, tok * ctxs, HEAD_DIM),
+            shape(3, tok, heads),
             shape(7, rank, total),
             shape(3, rank, total),
             shape(total, heads),
@@ -918,9 +1008,12 @@
             shape(units, tok * ctxs, HEAD_DIM),
         ),
         in_specs=[hb] * 6 + [vm] * 10 + [sm],
-        out_specs=(hb,) * 7 + (vm,) * 6,
+        out_specs=(hb,) * 7 + (vm,) * 7,
         scratch_shapes=[
             pltpu.VMEM((total, heads), BF),
+            pltpu.VMEM((1, 3, tok * ctxs, HEAD_DIM), BF),
+            pltpu.VMEM((tok * ctxs, HEAD_DIM), F32),
+            pltpu.VMEM((tok * ctxs, HEAD_DIM), F32),
             pltpu.VMEM((seqs, local_heads, 3, tok, HEAD_DIM), BF),
             pltpu.VMEM((heads, width), BF),
             pltpu.VMEM((width, hidden_units), BF),
@@ -957,7 +1050,9 @@
             dma((units, ctxs)),
             dma((units, ctxs)),
             dma((units, ctxs)),
-            dma((3, units)),
+            dma((ctxs,)),
+            dma((ctxs,)),
+            dma((4, units)),
         ],
         compiler_params=pltpu.CompilerParams(
             collective_id=0, has_side_effects=True, vmem_limit_bytes=VMEM_BYTES
@@ -980,6 +1075,7 @@
     md,
     attn_low,
     unit_rank,
+    early_grads,
     hidden_far,
     mix_rank,
     row_hot,
@@ -1055,6 +1151,9 @@
     def mixing_load():
         return pltpu.make_async_copy(mixing_far, mixing, far_sem.at[0])
 
+    def early_load():
+        return pltpu.make_async_copy(early_grads, grads.at[:, pl.ds(0, tok)], far_sem.at[2])
+
     def hidden_load():
         return pltpu.make_async_copy(hidden_far, hidden, far_sem.at[1])
 
@@ -1089,28 +1188,7 @@
         )
 
     def attend_back(u):
-        part = math.gcd(seq_all, 256)
-        sum_k[...] = jnp.zeros_like(sum_k)
-        sum_v[...] = jnp.zeros_like(sum_v)
-
-        @pl.loop(0, seq_all // part)
-        def _(i):
-            rs = tile(i, part)
-            queries = unit_qkv[u, 0, rs, :]
-            go = unit_go[u, rs, :]
-            scores = dot_nt(queries, unit_qkv[u, 1]) * scale
-            raised = jnp.exp(scores - jnp.max(scores, axis=-1, keepdims=True))
-            probs = raised * (1.0 / jnp.sum(raised, axis=-1, keepdims=True))
-            delta = jnp.sum(
-                go.astype(F32) * unit_out[u, rs, :].astype(F32), axis=-1, keepdims=True
-            )
-            dscores = (probs * (dot_nt(go, unit_qkv[u, 2]) - delta)).astype(BF)
-            unit_grad[u, 0, rs, :] = (scale * dot_nn(dscores, unit_qkv[u, 1])).astype(BF)
-            sum_k[...] += dot_tn(dscores, queries)
-            sum_v[...] += dot_tn(probs.astype(BF), go)
-
-        unit_grad[u, 1] = (scale * sum_k[...]).astype(BF)
-        unit_grad[u, 2] = sum_v[...].astype(BF)
+        attention_back(unit_qkv, unit_go, unit_out, unit_grad, sum_k, sum_v, u, u)
         for step in range(1, ctxs):
             grad_copy(u, step).start()
         grad_own(u).start()
@@ -1120,6 +1198,10 @@
         for step in range(1, ctxs):
             grad_arrival(u, step).wait_recv()
 
+    early = early_units(chunks * rows, tok, units)
+    lead = per_seq * (1 - early)
+    if early:
+        early_load().start()
     mixing_load().start()
     hidden_load().start()
 
@@ -1254,9 +1336,9 @@
 
     delay = 2 * ranks
 
-    @pl.loop(0, per_seq + chunks + delay)
+    @pl.loop(0, lead + chunks + delay)
     def _(now):
-        tick = now - per_seq
+        tick = now - lead
 
         @pl.when(tick == chunks)
         def _():
@@ -1271,11 +1353,19 @@
 
         comm(tick, 0)
 
-        pl.when((now % per_seq == 0) & (now < units * per_seq))(lambda: attend_back(now // per_seq))
-        pl.when((tick >= 0) & (tick % per_seq == 0) & (tick < units * per_seq))(
-            lambda: grads_ready(s)
-        )
+        pl.when(
+            (tick >= early * per_seq) & (tick % per_seq == 0) & (tick < units * per_seq)
+        )(lambda: grads_ready(s))
+        if not early:
+            pl.when((now % per_seq == 0) & (now < units * per_seq))(
+                lambda: attend_back(now // per_seq)
+            )
         comm(tick, 1)
+        if early:
+            pl.when((now % per_seq == 0) & (now < (units - 1) * per_seq))(
+                lambda: attend_back(now // per_seq + 1)
+            )
+            pl.when(tick == 0)(lambda: early_load().wait())
 
         pl.when(tick == 0)(lambda: mixing_load().wait())
         pl.when(valid & (tick % group == 0))(lambda: back_part(c, s))
@@ -1299,13 +1389,13 @@
     for step in range(1, parts):
         part_copy(step).wait_send()
         whole_copy(step).wait_send()
-    for u in range(units):
+    for u in range(early, units):
         for step in range(1, ctxs):
             grad_copy(u, step).wait_send()
 
 
 def mixing_back(
-    unit_go, unit_qkv, unit_out, mixing, picked, attn_low, hidden, mix_rank, row_hot, picks
+    unit_go, early_grads, unit_qkv, unit_out, mixing, picked, attn_low, hidden, mix_rank, row_hot, picks
 ):
     mu, md = picked
     total, width = attn_low.shape
@@ -1332,7 +1422,7 @@
             jax.ShapeDtypeStruct((total, width), BF),
             jax.ShapeDtypeStruct((parts, rank, part_width), BF),
         ),
-        in_specs=[vm] * 3 + [hb] + [vm] * 2 + [hb, vm, hb] + [vm] * 2 + [sm],
+        in_specs=[vm] * 3 + [hb] + [vm] * 2 + [hb, vm, hb, hb] + [vm] * 2 + [sm],
         out_specs=(hb, vm),
         scratch_shapes=[
             pltpu.VMEM((3, total, heads), BF),
@@ -1358,7 +1448,7 @@
             dma((2, chunks)),
             dma((2, chunks)),
             dma((2, chunks)),
-            dma((2,)),
+            dma((3,)),
             dma((units, ctxs)),
             dma((units, ctxs)),
             dma((units,)),
@@ -1386,6 +1476,7 @@
         md,
         attn_low,
         jnp.eye(rank, dtype=BF),
+        early_grads,
         hidden,
         mix_rank,
         row_hot,
@@ -1435,6 +1526,7 @@
         attn_low,
         mixing_full,
         unit_go,
+        early_grads,
         part_ranks,
         full_ranks,
         context,
@@ -1476,6 +1568,7 @@
     early, unit_go = lax.optimization_barrier((early, unit_go))
     input_rows, late = mixing_back(
         unit_go,
+        early_grads,
         unit_qkv,
         unit_out,
         mixing_full,

time: 619 us -> 612 us (0.989)
    pallas_call x1, Pallas kernels: 144 us -> 138 us  [mixing_back(): pl.pallas_call(functools.partial(mixing_kernel, sizes), out_shape=(jax.Sh...]
where the time goes in v7:
time: 612 us; the launch traced here: 611 us
  Pallas kernels  556 us (91%)
  other arithmetic  17.1 us (3%)
  between operations  14.1 us (2%)
  local copies, waits for them, and re-layouts  12.7 us (2%)
  matrix products  10.9 us (2%)
    pallas_call x1, Pallas kernels, middle(): pl.pallas_call(functools.partial(middle_kernel, sizes), out_shape=(shape(...  418 us
    pallas_call x1, Pallas kernels, mixing_back(): pl.pallas_call(functools.partial(mixing_kernel, sizes), out_shape=(jax.Sh...  138 us
    convert_element_type x8, other arithmetic, per_device(): summed = tuple((part.astype(jnp.float32) for part in late + early))  13.6 us
  transfers between devices with their start and end apart: 1, of which 0 were waited for; matrix products, arithmetic and copies ran while one was open for 1% of the time, Pallas kernels for 23%

profile of v7, /device:TPU:0, one launch (start us, length us, event | category | flops | bytes accessed | tf_op | source)
XLA Modules:
  0.0 610.6 jit_solution(3370507953167533254)
XLA Ops:
  7.2 0.0 all-reduce.3.cloned.1.call-start
  7.2 0.6 fusion.unit_rank
  7.8 1.8 copy.37
  9.6 1.4 copy.32
  11.0 1.2 copy.34.shard_mix
  12.1 0.7 fusion.1
  12.9 1.4 pad_maximum_fusion.gains
  14.3 418.2 %shard_map.258 = (bf16[1024,2048]{1,0:T(8,128)(2,1)}, bf16[1024,2048]{1,0:T(8,128)(2,1)}, bf16[1024,2048]{1,0:T(8,128)(2,1)}, bf16[1024,2048]{1,0:T(8,128)(2,1)}...) custom-call(bf16[1024,2048]{1,0:T(8,128)(2,1)} %bitcast.82, ...), custom_call_target="tpu_custom_call" | custom-call | flops 38654705664 | bytes 33554432 | tf_op jit(solution)/shard_map/pallas_call | solution.py:992
  432.4 0.0 copy-start.3
  432.4 1.6 slice_bitcast_fusion
  434.1 0.1 broadcast_in_dim.4
  434.2 0.1 broadcast_multiply_fusion
  434.3 0.0 copy-start.2
  434.3 3.9 convolution_convert_fusion
  438.2 0.0 copy-done.3
  438.2 0.0 copy-start.1
  438.2 1.5 convolution_convert_fusion.1
  439.7 0.0 copy-done.2
  439.7 0.0 copy-start
  439.7 1.5 convolution_convert_fusion.2
  441.2 0.0 copy-done.1
  441.2 0.0 copy-start.6
  441.2 1.5 convolution_convert_fusion.3
  442.8 0.0 copy-done
  442.8 1.5 convolution_convert_fusion.4
  444.3 0.0 copy-done.6
  444.3 1.0 convolution_convert_fusion.5
  445.3 0.0 all-reduce.3.cloned.1.call-update
  445.3 0.6 convert_element_type.66.row_hot
  445.9 137.6 %shard_map.259 = (bf16[1024,2048]{1,0:T(8,128)(2,1)}, bf16[8,16,3584]{2,1,0:T(8,128)(2,1)}) custom-call(bf16[4,1024,128]{2,1,0:T(8,128)(2,1)} %get-tuple-element.43.unit_go, bf16[4,3,1024,128]{3,2,1,0:T(8,128)(2,1)} %get-tuple-element.44.unit_qkv, bf16[4,1024,128]{2,1,0:T(8,128)(2,1)} %get-tuple-element.45.unit_out, ...), custom_call_target="tpu_custom_call" | custom-call | flops 11811160064 | bytes 16777216 | tf_op jit(solution)/shard_map/pallas_call | solution.py:1419
  583.5 1.1 slice_convert_fusion.1
  584.5 1.0 copy.39
  585.5 2.1 slice_convert_fusion
  587.6 0.0 all-reduce.3.cloned.1.call-done
  587.6 0.0 copy-start.7
  587.6 0.0 copy-start.8
  587.6 0.0 copy-start.4
  587.6 2.3 convert_element_type.71
  589.9 2.1 convert_element_type.72
  592.0 2.1 convert_element_type.73
  594.1 2.1 convert_element_type.74
  596.3 0.0 copy-done.7
  596.3 1.1 convert_element_type.75
  597.3 0.0 copy-done.8
  597.3 0.7 convert_element_type.70
  598.1 0.0 copy-done.4
  598.1 0.0 copy-start.5
  598.1 2.1 copy.48
  600.2 1.6 copy-done.5
  601.8 2.0 copy.49
Async XLA Ops:
  7.2 580.4 %all-reduce.3.cloned.1.call-start = ((), (), s32[]{:S(2)}) async-start(), calls=%async_computation | async-start | bytes 5505024 | tf_op jit(solution)/shard_map/psum | solution.py:1582
  432.4 5.7 copy-start.3
  434.3 5.4 copy-start.2
  438.2 3.1 copy-start.1
  439.7 3.1 copy-start
  441.2 3.1 copy-start.6
  587.6 8.6 %copy-start.7 = (bf16[8,16,2048]{2,1,0:T(8,128)(2,1)S(1)}, bf16[8,16,2048]{2,1,0:T(8,128)(2,1)}, u32[]{:S(2)}) copy-start(bf16[8,16,2048]{2,1,0:T(8,128)(2,1)} %get-tuple-element.81) | copy-start | bytes 1572868
  587.6 9.7 %copy-start.8 = (bf16[8,16,512]{2,1,0:T(8,128)(2,1)S(1)}, bf16[8,16,512]{2,1,0:T(8,128)(2,1)}, u32[]{:S(2)}) copy-start(bf16[8,16,512]{2,1,0:T(8,128)(2,1)} %get-tuple-element.76) | copy-start | bytes 393220
  587.6 10.4 %copy-start.4 = (bf16[1024,2048]{1,0:T(8,128)(2,1)S(1)}, bf16[1024,2048]{1,0:T(8,128)(2,1)}, u32[]{:S(2)}) copy-start(bf16[1024,2048]{1,0:T(8,128)(2,1)} %get-tuple-element.33) | copy-start | bytes 12582916
  598.1 3.7 copy-start.5
Sparse Core Ops, SparseCore 0:
  445.4 77.5 all-reduce.2

commit v8 on v7

--- a/solution.py
+++ b/solution.py
@@ -1334,7 +1334,7 @@
         for step in range(1, parts):
             whole_copy(step).start()
 
-    delay = 2 * ranks
+    delay = max(2 * ranks - 1, 4)
 
     @pl.loop(0, lead + chunks + delay)
     def _(now):
@@ -1375,7 +1375,7 @@
             hidden_load().wait()
             make_tables()
 
-        pl.when(tick == chunks + 4)(sum_tables)
+        pl.when(tick == chunks + 3)(sum_tables)
 
         pl.when(before)(lambda: keep(c_before).wait())
         pl.when(final)(lambda: final_part(c_final))

time: 612 us -> 610 us (level)
  transfers between devices with their start and end apart: 1 -> 1, of which waited for: 0 -> 0; matrix products, arithmetic and copies ran while one was open for 1% -> 1% of each run, Pallas kernels for 23% -> 22%
where the time goes in v8:
time: 610 us; the launch traced here: 609 us
  Pallas kernels  554 us (91%)
  other arithmetic  17.1 us (3%)
  between operations  14.1 us (2%)
  local copies, waits for them, and re-layouts  12.7 us (2%)
  matrix products  10.9 us (2%)
    pallas_call x1, Pallas kernels, middle(): pl.pallas_call(functools.partial(middle_kernel, sizes), out_shape=(shape(...  418 us
    pallas_call x1, Pallas kernels, mixing_back(): pl.pallas_call(functools.partial(mixing_kernel, sizes), out_shape=(jax.Sh...  136 us
    convert_element_type x8, other arithmetic, per_device(): summed = tuple((part.astype(jnp.float32) for part in late + early))  13.6 us
  transfers between devices with their start and end apart: 1, of which 0 were waited for; matrix products, arithmetic and copies ran while one was open for 1% of the time, Pallas kernels for 22%

profile of v8, /device:TPU:0, one launch (start us, length us, event | category | flops | bytes accessed | tf_op | source)
XLA Modules:
  0.0 609.2 jit_solution(16355316311230157559)
XLA Ops:
  7.2 0.0 all-reduce.3.cloned.1.call-start
  7.2 0.6 fusion.unit_rank
  7.8 1.8 copy.37
  9.6 1.4 copy.32
  11.0 1.2 copy.34.shard_mix
  12.1 0.7 fusion.1
  12.9 1.4 pad_maximum_fusion.gains
  14.3 418.2 %shard_map.258 = (bf16[1024,2048]{1,0:T(8,128)(2,1)}, bf16[1024,2048]{1,0:T(8,128)(2,1)}, bf16[1024,2048]{1,0:T(8,128)(2,1)}, bf16[1024,2048]{1,0:T(8,128)(2,1)}...) custom-call(bf16[1024,2048]{1,0:T(8,128)(2,1)} %bitcast.82, ...), custom_call_target="tpu_custom_call" | custom-call | flops 38654705664 | bytes 33554432 | tf_op jit(solution)/shard_map/pallas_call | solution.py:992
  432.4 0.0 copy-start.3
  432.4 1.6 slice_bitcast_fusion
  434.1 0.1 broadcast_in_dim.4
  434.2 0.1 broadcast_multiply_fusion
  434.3 0.0 copy-start.2
  434.3 3.9 convolution_convert_fusion
  438.2 0.0 copy-done.3
  438.2 0.0 copy-start.1
  438.2 1.5 convolution_convert_fusion.1
  439.7 0.0 copy-done.2
  439.7 0.0 copy-start
  439.7 1.5 convolution_convert_fusion.2
  441.2 0.0 copy-done.1
  441.2 0.0 copy-start.6
  441.2 1.5 convolution_convert_fusion.3
  442.8 0.0 copy-done
  442.8 1.5 convolution_convert_fusion.4
  444.3 0.0 copy-done.6
  444.3 1.0 convolution_convert_fusion.5
  445.3 0.0 all-reduce.3.cloned.1.call-update
  445.3 0.6 convert_element_type.66.row_hot
  445.9 136.2 %shard_map.259 = (bf16[1024,2048]{1,0:T(8,128)(2,1)}, bf16[8,16,3584]{2,1,0:T(8,128)(2,1)}) custom-call(bf16[4,1024,128]{2,1,0:T(8,128)(2,1)} %get-tuple-element.43.unit_go, bf16[4,3,1024,128]{3,2,1,0:T(8,128)(2,1)} %get-tuple-element.44.unit_qkv, bf16[4,1024,128]{2,1,0:T(8,128)(2,1)} %get-tuple-element.45.unit_out, ...), custom_call_target="tpu_custom_call" | custom-call | flops 11811160064 | bytes 16777216 | tf_op jit(solution)/shard_map/pallas_call | solution.py:1419
  582.1 1.1 slice_convert_fusion.1
  583.2 1.0 copy.39
  584.1 2.1 slice_convert_fusion
  586.2 0.0 all-reduce.3.cloned.1.call-done
  586.2 0.0 copy-start.7
  586.2 0.0 copy-start.8
  586.2 0.0 copy-start.4
  586.2 2.3 convert_element_type.71
  588.5 2.1 convert_element_type.72
  590.6 2.1 convert_element_type.73
  592.7 2.1 convert_element_type.74
  594.9 0.0 copy-done.7
  594.9 1.1 convert_element_type.75
  595.9 0.0 copy-done.8
  595.9 0.7 convert_element_type.70
  596.7 0.0 copy-done.4
  596.7 0.0 copy-start.5
  596.7 2.1 copy.48
  598.8 1.6 copy-done.5
  600.4 2.0 copy.49
Async XLA Ops:
  7.2 579.1 %all-reduce.3.cloned.1.call-start = ((), (), s32[]{:S(2)}) async-start(), calls=%async_computation | async-start | bytes 5505024 | tf_op jit(solution)/shard_map/psum | solution.py:1582
  432.4 5.7 copy-start.3
  434.3 5.4 copy-start.2
  438.2 3.1 copy-start.1
  439.7 3.1 copy-start
  441.2 3.1 copy-start.6
  586.2 8.6 %copy-start.7 = (bf16[8,16,2048]{2,1,0:T(8,128)(2,1)S(1)}, bf16[8,16,2048]{2,1,0:T(8,128)(2,1)}, u32[]{:S(2)}) copy-start(bf16[8,16,2048]{2,1,0:T(8,128)(2,1)} %get-tuple-element.81) | copy-start | bytes 1572868
  586.2 9.7 %copy-start.8 = (bf16[8,16,512]{2,1,0:T(8,128)(2,1)S(1)}, bf16[8,16,512]{2,1,0:T(8,128)(2,1)}, u32[]{:S(2)}) copy-start(bf16[8,16,512]{2,1,0:T(8,128)(2,1)} %get-tuple-element.76) | copy-start | bytes 393220
  586.2 10.4 %copy-start.4 = (bf16[1024,2048]{1,0:T(8,128)(2,1)S(1)}, bf16[1024,2048]{1,0:T(8,128)(2,1)}, u32[]{:S(2)}) copy-start(bf16[1024,2048]{1,0:T(8,128)(2,1)} %get-tuple-element.33) | copy-start | bytes 12582916
  596.7 3.7 copy-start.5
Sparse Core Ops, SparseCore 0:
  445.4 77.5 all-reduce.2

commit v9 on v8

--- a/solution.py
+++ b/solution.py
@@ -246,8 +246,8 @@
     hidden_units = w_exp.shape[1]
     heads = w_out.shape[0]
     block = min(16, half)
-    tile_f = math.gcd(hidden_units, 256)
-    tile_d = math.gcd(width, 256)
+    tile_f = math.gcd(hidden_units, 512)
+    tile_d = math.gcd(width, 512)
     tile_h = math.gcd(heads, 256)
     me = lax.axis_index("tensor")
     dp = lax.axis_index("dp")
@@ -1124,7 +1124,7 @@
     units, seq_all = unit_go.shape[0], unit_go.shape[1]
     tok = seq_all // ctxs
     block = min(16, half)
-    tile_d = math.gcd(width, 256)
+    tile_d = math.gcd(width, 512)
     scale = HEAD_DIM ** (-0.5)
     me = lax.axis_index("tensor")
     ctx = lax.axis_index("ctx")

time: 610 us -> 606 us (level)
  no operation moved by 1% of the time
where the time goes in v9:
time: 606 us; the launch traced here: 605 us
  Pallas kernels  550 us (91%)
  other arithmetic  17.1 us (3%)
  between operations  14.1 us (2%)
  local copies, waits for them, and re-layouts  12.7 us (2%)
  matrix products  10.9 us (2%)
    pallas_call x1, Pallas kernels, middle(): pl.pallas_call(functools.partial(middle_kernel, sizes), out_shape=(shape(...  414 us
    pallas_call x1, Pallas kernels, mixing_back(): pl.pallas_call(functools.partial(mixing_kernel, sizes), out_shape=(jax.Sh...  136 us
    convert_element_type x8, other arithmetic, per_device(): summed = tuple((part.astype(jnp.float32) for part in late + early))  13.6 us
  transfers between devices with their start and end apart: 1, of which 0 were waited for; matrix products, arithmetic and copies ran while one was open for 1% of the time, Pallas kernels for 22%

profile of v9, /device:TPU:0, one launch (start us, length us, event | category | flops | bytes accessed | tf_op | source)
XLA Modules:
  0.0 605.3 jit_solution(3176873729975978008)
XLA Ops:
  7.2 0.0 all-reduce.3.cloned.1.call-start
  7.2 0.6 fusion.unit_rank
  7.8 1.8 copy.37
  9.6 1.4 copy.32
  11.0 1.2 copy.34.shard_mix
  12.1 0.7 fusion.1
  12.9 1.4 pad_maximum_fusion.gains
  14.3 414.4 %shard_map.258 = (bf16[1024,2048]{1,0:T(8,128)(2,1)}, bf16[1024,2048]{1,0:T(8,128)(2,1)}, bf16[1024,2048]{1,0:T(8,128)(2,1)}, bf16[1024,2048]{1,0:T(8,128)(2,1)}...) custom-call(bf16[1024,2048]{1,0:T(8,128)(2,1)} %bitcast.82, ...), custom_call_target="tpu_custom_call" | custom-call | flops 38654705664 | bytes 33554432 | tf_op jit(solution)/shard_map/pallas_call | solution.py:992
  428.7 0.0 copy-start.3
  428.7 1.6 slice_bitcast_fusion
  430.3 0.1 broadcast_in_dim.4
  430.4 0.1 broadcast_multiply_fusion
  430.5 0.0 copy-start.2
  430.5 3.9 convolution_convert_fusion
  434.4 0.0 copy-done.3
  434.4 0.0 copy-start.1
  434.4 1.5 convolution_convert_fusion.1
  435.9 0.0 copy-done.2
  436.0 0.0 copy-start
  436.0 1.5 convolution_convert_fusion.2
  437.5 0.0 copy-done.1
  437.5 0.0 copy-start.6
  437.5 1.5 convolution_convert_fusion.3
  439.0 0.0 copy-done
  439.0 1.5 convolution_convert_fusion.4
  440.5 0.0 copy-done.6
  440.5 1.0 convolution_convert_fusion.5
  441.5 0.0 all-reduce.3.cloned.1.call-update
  441.5 0.6 convert_element_type.66.row_hot
  442.2 136.0 %shard_map.259 = (bf16[1024,2048]{1,0:T(8,128)(2,1)}, bf16[8,16,3584]{2,1,0:T(8,128)(2,1)}) custom-call(bf16[4,1024,128]{2,1,0:T(8,128)(2,1)} %get-tuple-element.43.unit_go, bf16[4,3,1024,128]{3,2,1,0:T(8,128)(2,1)} %get-tuple-element.44.unit_qkv, bf16[4,1024,128]{2,1,0:T(8,128)(2,1)} %get-tuple-element.45.unit_out, ...), custom_call_target="tpu_custom_call" | custom-call | flops 11811160064 | bytes 16777216 | tf_op jit(solution)/shard_map/pallas_call | solution.py:1419
  578.1 1.1 slice_convert_fusion.1
  579.2 1.0 copy.39
  580.2 2.1 slice_convert_fusion
  582.3 0.0 all-reduce.3.cloned.1.call-done
  582.3 0.0 copy-start.7
  582.3 0.0 copy-start.8
  582.3 0.0 copy-start.4
  582.3 2.3 convert_element_type.71
  584.6 2.1 convert_element_type.72
  586.7 2.1 convert_element_type.73
  588.8 2.1 convert_element_type.74
  590.9 0.0 copy-done.7
  590.9 1.1 convert_element_type.75
  592.0 0.0 copy-done.8
  592.0 0.7 convert_element_type.70
  592.7 0.0 copy-done.4
  592.7 0.0 copy-start.5
  592.7 2.1 copy.48
  594.9 1.6 copy-done.5
  596.4 2.0 copy.49
Async XLA Ops:
  7.2 575.1 %all-reduce.3.cloned.1.call-start = ((), (), s32[]{:S(2)}) async-start(), calls=%async_computation | async-start | bytes 5505024 | tf_op jit(solution)/shard_map/psum | solution.py:1582
  428.7 5.7 copy-start.3
  430.5 5.4 copy-start.2
  434.4 3.1 copy-start.1
  436.0 3.1 copy-start
  437.5 3.1 copy-start.6
  582.3 8.6 %copy-start.7 = (bf16[8,16,2048]{2,1,0:T(8,128)(2,1)S(1)}, bf16[8,16,2048]{2,1,0:T(8,128)(2,1)}, u32[]{:S(2)}) copy-start(bf16[8,16,2048]{2,1,0:T(8,128)(2,1)} %get-tuple-element.81) | copy-start | bytes 1572868
  582.3 9.7 %copy-start.8 = (bf16[8,16,512]{2,1,0:T(8,128)(2,1)S(1)}, bf16[8,16,512]{2,1,0:T(8,128)(2,1)}, u32[]{:S(2)}) copy-start(bf16[8,16,512]{2,1,0:T(8,128)(2,1)} %get-tuple-element.76) | copy-start | bytes 393220
  582.3 10.4 %copy-start.4 = (bf16[1024,2048]{1,0:T(8,128)(2,1)S(1)}, bf16[1024,2048]{1,0:T(8,128)(2,1)}, u32[]{:S(2)}) copy-start(bf16[1024,2048]{1,0:T(8,128)(2,1)} %get-tuple-element.33) | copy-start | bytes 12582916
  592.7 3.7 copy-start.5
Sparse Core Ops, SparseCore 0:
  441.7 77.2 all-reduce.2
